TPU v7x, 256 devices: a whole 4x4x8 slice. The times are simulated.
256 devices in a mesh: row: 32 (over y, x, core), col: 8 (over z).
Axes of the slice: x: 4, y: 4, z: 8, core: 2. Of those that a mesh axis runs over, the one named last changes fastest.
Arguments:
- tokens: bfloat16 [256, 8192], P('row', 'col'), may hold values from -6 to 6
- gate_weight: bfloat16 [8192, 28672], P('row', 'col'), may hold values from -0.0625 to 0.0625
- up_weight: bfloat16 [8192, 28672], P('row', 'col'), may hold values from -0.0625 to 0.0625
- down_weight: bfloat16 [28672, 8192], P('row', 'col'), may hold values from -0.03125 to 0.03125
- out_grad: bfloat16 [256, 8192], P('row', 'col'), may hold values from -1.5 to 1.5
Outputs:
- output: bfloat16 [256, 8192], P('row', 'col')
- grad_tokens: bfloat16 [256, 8192], P('row', 'col')
- grad_gate_weight: bfloat16 [8192, 28672], P('row', 'col')
- grad_up_weight: bfloat16 [8192, 28672], P('row', 'col')
- grad_down_weight: bfloat16 [28672, 8192], P('row', 'col')
All inputs are finite; a program needn't handle non-finite values.
Results may differ from a plain program's by a relative error of at most 0.04.
Values may be sent and summed in bfloat16 or wider, within the bound.
No kernel may reach another device: no remote copies, remote signals or barrier semaphores. Data moves between devices by JAX's collectives and lax.ppermute only.
A program may use at most 64 MiB of HBM per device.

v0:
```python
import jax
import jax.numpy as jnp
from jax import lax
from jax.sharding import PartitionSpec as P


def rows_times(left, right):
    return lax.dot_general(
        left, right, (((1,), (1,)), ((), ())), preferred_element_type=jnp.float32
    )


def columns_times(left, right):
    return lax.dot_general(
        left, right, (((0,), (0,)), ((), ())), preferred_element_type=jnp.float32
    )


def token_panel(tokens):
    every_feature = lax.all_gather(tokens, "col", axis=1, tiled=True)
    return lax.all_to_all(every_feature, "row", split_axis=1, concat_axis=0, tiled=True)


def local(tokens, gate_weight, up_weight, down_weight, out_grad):
    panel = token_panel(tokens)
    rows = panel
    gate = lax.psum_scatter(
        jnp.dot(rows, gate_weight, preferred_element_type=jnp.float32).astype(jnp.bfloat16),
        "row",
        scatter_dimension=0,
        tiled=True,
    ).astype(jnp.float32)
    rows = panel
    up = lax.psum_scatter(
        jnp.dot(rows, up_weight, preferred_element_type=jnp.float32).astype(jnp.bfloat16),
        "row",
        scatter_dimension=0,
        tiled=True,
    ).astype(jnp.float32)
    sigmoid_gate = jax.nn.sigmoid(gate)
    silu_gate = gate * sigmoid_gate
    hidden = (silu_gate * up).astype(jnp.bfloat16)
    hidden_all = lax.all_gather(hidden, "col", axis=1, tiled=True)
    hidden_panel = lax.all_to_all(hidden_all, "row", split_axis=1, concat_axis=0, tiled=True)
    rows = hidden_panel
    output = lax.psum_scatter(
        jnp.dot(rows, down_weight, preferred_element_type=jnp.float32).astype(jnp.bfloat16),
        "row",
        scatter_dimension=0,
        tiled=True,
    )
    piece = lax.all_gather(out_grad, "row", axis=0, tiled=True)
    rows = hidden_panel
    weight_sum = columns_times(rows, piece)
    hidden_part = rows_times(piece, down_weight)
    down_sum, hidden_part = (weight_sum, hidden_part)
    grad_down_weight = down_sum.astype(jnp.bfloat16)
    hidden_terms = lax.all_to_all(
        hidden_part.astype(jnp.bfloat16), "row", split_axis=0, concat_axis=1, tiled=True
    )
    grad_hidden = lax.psum_scatter(
        hidden_terms.astype(jnp.float32).astype(jnp.bfloat16),
        "col",
        scatter_dimension=1,
        tiled=True,
    ).astype(jnp.float32)
    grad_gate = (grad_hidden * up * sigmoid_gate * (1.0 + gate * (1.0 - sigmoid_gate))).astype(
        jnp.bfloat16
    )
    grad_up = (grad_hidden * silu_gate).astype(jnp.bfloat16)
    piece_gate = lax.all_gather(grad_gate, "row", axis=0, tiled=True)
    piece_up = lax.all_gather(grad_up, "row", axis=0, tiled=True)
    rows = panel
    gate_sum = columns_times(rows, piece_gate)
    up_sum = columns_times(rows, piece_up)
    token_rows = rows_times(piece_gate, gate_weight) + rows_times(piece_up, up_weight)
    token_part = token_rows
    gate_sum, up_sum, token_part = (gate_sum, up_sum, token_part)
    token_terms = lax.all_to_all(
        token_part.astype(jnp.bfloat16), "row", split_axis=0, concat_axis=1, tiled=True
    )
    grad_tokens = lax.psum_scatter(
        token_terms.astype(jnp.float32).astype(jnp.bfloat16), "col", scatter_dimension=1, tiled=True
    )
    return (
        output,
        grad_tokens,
        gate_sum.astype(jnp.bfloat16),
        up_sum.astype(jnp.bfloat16),
        grad_down_weight,
    )


def solution(mesh):
    return jax.shard_map(
        local,
        mesh=mesh,
        in_specs=(
            P("row", "col"),
            P("row", "col"),
            P("row", "col"),
            P("row", "col"),
            P("row", "col"),
        ),
        out_specs=(
            P("row", "col"),
            P("row", "col"),
            P("row", "col"),
            P("row", "col"),
            P("row", "col"),
        ),
        check_vma=False,
    )
```

profile of v0, /device:TPU:1, one launch (start us, length us, event | category | flops | bytes accessed | tf_op | source)
XLA Modules:
  0.0 501.4 jit_solution(4171400332394637777)
XLA Ops:
  7.2 26.6 %all_gather.17 = bf16[256,1024]{1,0:T(8,128)(2,1)S(1)} all-gather(bf16[8,1024]{1,0:T(8,128)(2,1)} %param.9), channel_id=1, replica_groups=mesh['row'=32,'col'=8] {'row'}, dimensions={0}, use_global_device_ids=true | all-gather | bytes 540672 | tf_op jit(solution)/shard_map/all_gather | solution.py:52
  33.8 2.3 fusion.2
  36.1 15.9 %all_to_all.76 = bf16[32,8,896]{2,1,0:T(8,128)(2,1)} all-to-all(bf16[32,8,896]{2,1,0:T(8,128)(2,1)S(1)} %fusion.2), channel_id=1, replica_groups=mesh['row'=32,'col'=8] {'row'}, dimensions={0} | all-to-all | bytes 917504 | tf_op jit(solution)/shard_map/all_to_all | solution.py:58
  52.0 0.0 reduce-scatter.6.cloned.1.call-start
  52.0 22.6 %all_gather.15 = bf16[8,8192]{1,0:T(8,128)(2,1)S(1)} all-gather(bf16[8,1024]{1,0:T(8,128)(2,1)S(1)} %copy-done.2), channel_id=1, replica_groups=mesh['row'=32,'col'=8] {'col'}, dimensions={1}, use_global_device_ids=true | all-gather | bytes 147456 | tf_op jit(solution)/shard_map/all_gather | solution.py:20
  74.6 17.1 %all_to_all.77 = bf16[8,32,256]{2,0,1:T(8,128)(2,1)S(1)} all-to-all(bf16[8,32,256]{2,0,1:T(8,128)(2,1)S(1)} %bitcast.49), channel_id=1, replica_groups=mesh['row'=32,'col'=8] {'row'}, dimensions={1} | all-to-all | bytes 262144 | tf_op jit(solution)/shard_map/all_to_all | solution.py:21
  91.7 1.9 convolution_convert_fusion.3
  93.6 0.0 reduce-scatter.8.cloned.1.call-start
  93.7 3.4 convolution_convert_fusion.2
  97.1 0.0 all-gather.3.cloned.1.call-start
  97.1 79.5 %reduce-scatter.6.cloned.1.call-done = bf16[8,3584]{1,0:T(8,128)(2,1)} async-done(((bf16[256,3584]{1,0:T(8,128)(2,1)}), bf16[8,3584]{1,0:T(8,128)(2,1)}) %reduce-scatter.6.cloned.1.call-update) | async-done | bytes 57360 | tf_op jit(solution)/shard_map/reduce_scatter | solution.py:27
  176.6 90.5 %reduce-scatter.8.cloned.1.call-done = bf16[8,3584]{1,0:T(8,128)(2,1)} async-done(((bf16[256,3584]{1,0:T(8,128)(2,1)}), bf16[8,3584]{1,0:T(8,128)(2,1)}) %reduce-scatter.8.cloned.1.call-update) | async-done | bytes 57360 | tf_op jit(solution)/shard_map/reduce_scatter | solution.py:34
  267.1 1.6 fusion.15
  268.8 0.5 all-gather.5.cloned.1.call-update
  269.4 21.0 %all_gather.16 = bf16[8,28672]{1,0:T(8,128)(2,1)S(1)} all-gather(bf16[8,3584]{1,0:T(8,128)(2,1)S(1)} %get-tuple-element.12), channel_id=1, replica_groups=mesh['row'=32,'col'=8] {'col'}, dimensions={1}, use_global_device_ids=true | all-gather | bytes 516096 | tf_op jit(solution)/shard_map/all_gather | solution.py:43
  290.4 24.8 %all_to_all.78 = bf16[8,32,896]{2,0,1:T(8,128)(2,1)S(1)} all-to-all(bf16[8,32,896]{2,0,1:T(8,128)(2,1)S(1)} %bitcast.47), channel_id=1, replica_groups=mesh['row'=32,'col'=8] {'row'}, dimensions={1} | all-to-all | bytes 917504 | tf_op jit(solution)/shard_map/all_to_all | solution.py:44
  315.2 3.0 convolution_convert_fusion.5
  318.2 1.9 convolution_convert_fusion.4
  320.1 2.2 all-gather.3.cloned.1.call-done
  322.4 2.2 fusion.20
  324.5 48.1 %all-gather.5.cloned.1.call-done = bf16[256,3584]{1,0:T(8,128)(2,1)} async-done(((bf16[8,3584]{1,0:T(8,128)(2,1)}), bf16[256,3584]{1,0:T(8,128)(2,1)}) %all-gather.5.cloned.1.call-update) | async-done | bytes 1835024 | tf_op jit(solution)/shard_map/all_gather | solution.py:72
  372.7 3.4 fusion.4
  376.0 5.2 %all-to-all-start.3 = ((bf16[32,8,256]{2,1,0:T(8,128)(2,1)}), bf16[32,8,256]{2,1,0:T(8,128)(2,1)S(1)}, u32[]{:S(2)}, u32[]{:S(2)}) async-start(bf16[32,8,256]{2,1,0:T(8,128)(2,1)} %fusion.4), calls=%async_computation.7 | async-start | bytes 262144 | tf_op jit(solution)/shard_map/all_to_all | solution.py:79
  381.2 0.0 reduce-scatter.14.cloned.1.call-start
  381.3 3.4 fusion
  384.7 3.8 copy.10
  388.5 0.3 all-to-all-done.3
  388.8 0.6 copy-done.1
  389.5 3.4 fusion.1
  393.0 3.8 copy.11
  396.8 62.2 %reduce-scatter.10.cloned.1.call-done = bf16[8,1024]{1,0:T(8,128)(2,1)} async-done(((bf16[256,1024]{1,0:T(8,128)(2,1)}), bf16[8,1024]{1,0:T(8,128)(2,1)}) %reduce-scatter.10.cloned.1.call-update) | async-done | bytes 16400 | tf_op jit(solution)/shard_map/reduce_scatter | solution.py:46
  459.0 35.6 %reduce-scatter.14.cloned.1.call-done = bf16[8,1024]{1,0:T(8,128)(2,1)} async-done(((bf16[8,8192]{1,0:T(8,128)(2,1)}), bf16[8,1024]{1,0:T(8,128)(2,1)}) %reduce-scatter.14.cloned.1.call-update) | async-done | bytes 16400 | tf_op jit(solution)/shard_map/reduce_scatter | solution.py:82
  (15 shorter events, 0.2 us)
Async XLA Ops:
  7.2 84.5 %copy-start = (bf16[256,3584]{1,0:T(8,128)(2,1)S(1)}, bf16[256,3584]{1,0:T(8,128)(2,1)}, u32[]{:S(2)}) copy-start(bf16[256,3584]{1,0:T(8,128)(2,1)} %param.6) | copy-start | bytes 5505028
  7.2 89.9 %reduce-scatter.12.cloned.1.call-start = ((), (), s32[]{:S(2)}) async-start(), calls=%async_computation.12 | async-start | bytes 516096 | tf_op jit(solution)/shard_map/reduce_scatter | solution.py:61
  33.8 18.2 %copy-start.2 = (bf16[8,1024]{1,0:T(8,128)(2,1)S(1)}, bf16[8,1024]{1,0:T(8,128)(2,1)}, u32[]{:S(2)}) copy-start(bf16[8,1024]{1,0:T(8,128)(2,1)} %param.5) | copy-start | bytes 49156
  52.0 124.6 %reduce-scatter.6.cloned.1.call-start = ((), (), s32[]{:S(2)}) async-start(), calls=%async_computation.9 | async-start | bytes 1892352 | tf_op jit(solution)/shard_map/reduce_scatter | solution.py:27
  93.6 173.5 %reduce-scatter.8.cloned.1.call-start = ((), (), s32[]{:S(2)}) async-start(), calls=%async_computation.10 | async-start | bytes 1892352 | tf_op jit(solution)/shard_map/reduce_scatter | solution.py:34
  97.1 225.3 %all-gather.3.cloned.1.call-start = ((), (), s32[]{:S(2)}) async-start(), calls=%async_computation.13 | async-start | bytes 1892352 | tf_op jit(solution)/shard_map/all_gather | solution.py:71
  268.7 103.9 %all-gather.5.cloned.1.call-start = ((), (), s32[]{:S(2)}) async-start(), calls=%async_computation.14 | async-start | bytes 1892352 | tf_op jit(solution)/shard_map/all_gather | solution.py:72
  269.3 189.6 %reduce-scatter.10.cloned.1.call-start = ((), (), s32[]{:S(2)}) async-start(), calls=%async_computation.11 | async-start | bytes 540672 | tf_op jit(solution)/shard_map/reduce_scatter | solution.py:46
  376.0 12.8 %all-to-all-start.3 = ((bf16[32,8,256]{2,1,0:T(8,128)(2,1)}), bf16[32,8,256]{2,1,0:T(8,128)(2,1)S(1)}, u32[]{:S(2)}, u32[]{:S(2)}) async-start(bf16[32,8,256]{2,1,0:T(8,128)(2,1)} %fusion.4), calls=%async_computation.7 | async-start | bytes 262144 | tf_op jit(solution)/shard_map/all_to_all | solution.py:79
  381.2 113.4 %reduce-scatter.14.cloned.1.call-start = ((), (), s32[]{:S(2)}) async-start(), calls=%async_computation.15 | async-start | bytes 147456 | tf_op jit(solution)/shard_map/reduce_scatter | solution.py:82
  388.8 0.7 copy-start.1
Sparse Core Ops, SparseCore 0:
  52.1 32.1 reduce-scatter.11
  93.7 82.8 reduce-scatter.5
  181.6 85.5 reduce-scatter.7
  270.4 51.9 all-gather.2
  325.7 46.9 all-gather.4
  377.3 81.6 reduce-scatter.9
  462.2 32.3 reduce-scatter.13
where the time goes:
time: 507 us; the launch traced here: 501 us
  waiting for transfers between devices  319 us (63%)
  blocking collectives  128 us (25%)
  matrix products  24.9 us (5%)
  between operations  14.2 us (3%)
  local copies, waits for them, and re-layouts  8.28 us (2%)
  starting transfers between devices  5.44 us (1%)
    reduce_scatter x1, waiting for transfers between devices, local(): lax.psum_scatter(jnp.dot(rows, up_weight, preferred_element_type=jnp.floa...  90.5 us
    reduce_scatter x1, waiting for transfers between devices, local(): lax.psum_scatter(jnp.dot(rows, gate_weight, preferred_element_type=jnp.fl...  79.5 us
    reduce_scatter x1, waiting for transfers between devices, local(): lax.psum_scatter(jnp.dot(rows, down_weight, preferred_element_type=jnp.fl...  62.2 us
    all_gather x1, waiting for transfers between devices, local(): piece_up = lax.all_gather(grad_up, 'row', axis=0, tiled=True)  48.1 us
    reduce_scatter x1, waiting for transfers between devices, local(): lax.psum_scatter(token_terms.astype(jnp.float32).astype(jnp.bfloat16), 'c...  35.6 us
    all_gather x1, blocking collectives, local(): piece = lax.all_gather(out_grad, 'row', axis=0, tiled=True)  26.6 us
    all_to_all x1, blocking collectives, local(): lax.all_to_all(hidden_all, 'row', split_axis=1, concat_axis=0, tiled=True)  24.8 us
    all_gather x1, blocking collectives, token_panel(): every_feature = lax.all_gather(tokens, 'col', axis=1, tiled=True)  22.6 us
  transfers between devices with their start and end apart: 8, of which 7 were waited for; matrix products, arithmetic and copies ran while one was open for 6% of the time, Pallas kernels for 0%

commit v1 on v0

v1 whole, which is shorter than its diff:
```python
import jax
import jax.numpy as jnp
from jax import lax
from jax.sharding import Mesh, PartitionSpec as P

Y, X, CORES, Z = 4, 4, 2, 8
CHIPS = Y * X
PLANE = ("y", "x")
ROW = ("y", "x", "core")
EVERY = ("y", "x", "core", "z")
SWAP = [(0, 1), (1, 0)]
BF16, F32 = jnp.bfloat16, jnp.float32


def rows_times(left, right):
    return lax.dot_general(left, right, (((1,), (1,)), ((), ())), preferred_element_type=F32)


def columns_times(left, right):
    return lax.dot_general(left, right, (((0,), (0,)), ((), ())), preferred_element_type=F32)


def times(left, right):
    return jnp.dot(left, right, preferred_element_type=F32)


def exchange(blocks, axis):
    return lax.all_to_all(blocks, axis, split_axis=0, concat_axis=0, tiled=True)


def spread(block, axis, count):
    return exchange(jnp.broadcast_to(block[None], (count,) + block.shape), axis)


def total(blocks):
    return jnp.sum(blocks.astype(F32), axis=0)


def unit_routes():
    routes = []
    for flip in range(2):
        route = []
        for chip in range(CHIPS):
            for core in range(CORES):
                for z in range(Z):
                    source = (chip * CORES + core) * Z + z
                    target = ((2 * z + (core ^ flip)) * CORES + chip % 2) * Z + chip // 2
                    route.append((source, target))
        routes.append(route)
    return routes


TO_OWNER = unit_routes()
FROM_OWNER = [[(b, a) for a, b in route] for route in TO_OWNER]


def local(tokens, gate_weight, up_weight, down_weight, out_grad):
    core = lax.axis_index("core")
    odd = lax.axis_index("x") % 2
    mine_tokens, width = tokens.shape
    depth, units = gate_weight.shape
    half = units // 2

    def halves(weight):
        mine = lax.dynamic_slice_in_dim(weight, core * half, half, 1)
        theirs = lax.dynamic_slice_in_dim(weight, (1 - core) * half, half, 1)
        return mine, lax.ppermute(theirs, "core", SWAP)

    gate_mine, gate_got = halves(gate_weight)
    up_mine, up_got = halves(up_weight)

    every_feature = spread(tokens, "z", Z)
    cotangent = spread(out_grad, ROW, CHIPS * CORES).reshape(-1, width)

    hidden_part = rows_times(cotangent, down_weight).astype(BF16)
    hidden_sum = total(exchange(hidden_part.reshape(Z, -1, hidden_part.shape[1]), "z")).astype(BF16)
    sixteen = hidden_sum.shape[0] // 2
    got = [
        lax.ppermute(
            lax.dynamic_slice_in_dim(hidden_sum, (core ^ flip) * sixteen, sixteen, 0),
            EVERY,
            TO_OWNER[flip],
        )
        for flip in range(2)
    ]
    grad_hidden = jnp.where(
        odd == 0, jnp.concatenate(got, 1), jnp.concatenate(got[::-1], 1)
    ).astype(F32)

    features = width * Z // CHIPS
    parts = every_feature.reshape(Z, mine_tokens, 2, features).transpose(0, 2, 1, 3)
    parts = parts.reshape(CHIPS, 1, mine_tokens, features)
    parts = jnp.broadcast_to(parts, (CHIPS, CORES, mine_tokens, features))
    panel = exchange(parts.reshape(CHIPS * CORES, mine_tokens, features), ROW).reshape(-1, features)
    panel_mine = lax.dynamic_slice_in_dim(panel, core * depth, depth, 1)
    panel_other = lax.dynamic_slice_in_dim(panel, (1 - core) * depth, depth, 1)

    gate_part = (times(panel_mine, gate_mine) + times(panel_other, gate_got)).astype(BF16)
    up_part = (times(panel_mine, up_mine) + times(panel_other, up_got)).astype(BF16)
    both = jnp.concatenate([gate_part, up_part], 1).reshape(CHIPS, -1, 2 * half)
    both = total(exchange(both, PLANE))
    gate, up = both[:, :half], both[:, half:]
    sigmoid_gate = jax.nn.sigmoid(gate)
    silu_gate = gate * sigmoid_gate
    hidden = (silu_gate * up).astype(BF16)
    grad_gate = grad_hidden * up * sigmoid_gate * (1.0 + gate * (1.0 - sigmoid_gate))
    grad_up = grad_hidden * silu_gate
    grads = jnp.concatenate([grad_gate.astype(BF16), grad_up.astype(BF16)], 1)

    quarter = half // 2
    got = [
        lax.ppermute(
            lax.dynamic_slice_in_dim(hidden, (odd ^ flip) * quarter, quarter, 1),
            EVERY,
            FROM_OWNER[flip],
        )
        for flip in range(2)
    ]
    hidden_rows = jnp.where(core == 0, jnp.concatenate(got, 0), jnp.concatenate(got[::-1], 0))

    pieces = spread(grads, PLANE, CHIPS).reshape(-1, 2 * half)
    hidden_panel = spread(hidden_rows, "z", Z).reshape(-1, quarter)
    piece_gate, piece_up = pieces[:, :half], pieces[:, half:]

    token_mine = rows_times(piece_gate, gate_mine) + rows_times(piece_up, up_mine)
    token_other = rows_times(piece_gate, gate_got) + rows_times(piece_up, up_got)
    token_mine, token_other = token_mine.astype(BF16), token_other.astype(BF16)
    token_part = jnp.where(
        core == 0,
        jnp.concatenate([token_mine, token_other], 1),
        jnp.concatenate([token_other, token_mine], 1),
    )
    output_part = times(hidden_panel, down_weight).astype(BF16)
    parts = jnp.concatenate([output_part, token_part], 1)
    parts = exchange(parts.reshape(CHIPS * CORES, mine_tokens, -1), ROW)
    output = total(parts[:, :, :width]).astype(BF16)
    terms = parts[:, :, width:].reshape(CHIPS, CORES, mine_tokens, features).astype(F32)
    terms = jnp.sum(terms, axis=1).astype(BF16).reshape(Z, 2, mine_tokens, features)
    terms = terms.transpose(0, 2, 1, 3).reshape(Z, mine_tokens, width)
    grad_tokens = total(exchange(terms, "z")).astype(BF16)

    grad_down_weight = columns_times(hidden_panel, cotangent).astype(BF16)

    def weight_grad(piece):
        mine = columns_times(panel_mine, piece).astype(BF16)
        other = columns_times(panel_other, piece).astype(BF16)
        got = lax.ppermute(other, "core", SWAP)
        return jnp.where(
            core == 0, jnp.concatenate([mine, got], 1), jnp.concatenate([got, mine], 1)
        )

    return output, grad_tokens, weight_grad(piece_gate), weight_grad(piece_up), grad_down_weight


def solution(mesh):
    fine = Mesh(mesh.devices.reshape(Y, X, CORES, Z), EVERY)
    spec = P(ROW, "z")
    return jax.shard_map(
        local, mesh=fine, in_specs=(spec,) * 5, out_specs=(spec,) * 5, check_vma=False
    )
```

time: 507 us -> 229 us (0.45)
  waiting for transfers between devices: 319 us -> 101 us
  blocking collectives: 128 us -> 0 us
  starting transfers between devices: 5.44 us -> 68.8 us
  other arithmetic: 1.59 us -> 15.3 us
  between operations: 14.2 us -> 0.98 us
  matrix products: 24.9 us -> 32.9 us
    reduce_scatter x5 -> x0, waiting for transfers between devices: 268 us -> none  [the longest x1 90.5 us: local(): lax.psum_scatter(jnp.dot(rows, up_weight, preferred_element_type=jnp.floa...]
    all_to_all x1 -> x9, waiting for transfers between devices: 0.35 us -> 99 us  [exchange(): return lax.all_to_all(blocks, axis, split_axis=0, concat_axis=0, tiled=True)]
    all_gather x3 -> x0, blocking collectives: 70.2 us -> none  [the longest x1 26.6 us: local(): piece = lax.all_gather(out_grad, 'row', axis=0, tiled=True)]
    all_to_all x3 -> x0, blocking collectives: 57.7 us -> none  [the longest x1 24.8 us: local(): lax.all_to_all(hidden_all, 'row', split_axis=1, concat_axis=0, tiled=True)]
    all_to_all x1 -> x9, starting transfers between devices: 5.15 us -> 58.7 us  [exchange(): return lax.all_to_all(blocks, axis, split_axis=0, concat_axis=0, tiled=True)]
    all_gather x2 -> x0, waiting for transfers between devices: 50.4 us -> none  [the longest x1 48.1 us: local(): piece_up = lax.all_gather(grad_up, 'row', axis=0, tiled=True)]
    ppermute x0 -> x8, starting transfers between devices: none -> 10.1 us  [the longest x2 4.93 us: local(): lax.ppermute(lax.dynamic_slice_in_dim(hidden, (odd ^ flip) * quarter, qua...]
    unnamed x8 -> x10, local copies, waits for them, and re-layouts: 8.28 us -> 0.03 us
  transfers between devices with their start and end apart: 8 -> 17, of which waited for: 7 -> 9; matrix products, arithmetic and copies ran while one was open for 6% -> 18% of each run, Pallas kernels for 0% -> 0%
where the time goes in v1:
time: 229 us; the launch traced here: 227 us
  waiting for transfers between devices  101 us (44%)
  starting transfers between devices  68.8 us (30%)
  matrix products  32.9 us (14%)
  other arithmetic  15.3 us (7%)
  local copies, waits for them, and re-layouts  8.57 us (4%)
    all_to_all x9, waiting for transfers between devices, exchange(): return lax.all_to_all(blocks, axis, split_axis=0, concat_axis=0, tiled=True)  99 us
    all_to_all x9, starting transfers between devices, exchange(): return lax.all_to_all(blocks, axis, split_axis=0, concat_axis=0, tiled=True)  58.7 us
    dot_general x5, matrix products, times(): return jnp.dot(left, right, preferred_element_type=F32)  11.4 us
    dot_general x5, matrix products, columns_times(): lax.dot_general(left, right, (((0,), (0,)), ((), ())), preferred_element_...  11.2 us
    dot_general x5, matrix products, rows_times(): lax.dot_general(left, right, (((1,), (1,)), ((), ())), preferred_element_...  10.3 us
    select_n x2, other arithmetic, weight_grad(): jnp.where(core == 0, jnp.concatenate([mine, got], 1), jnp.concatenate([go...  6.88 us
    ppermute x2, starting transfers between devices, local(): lax.ppermute(lax.dynamic_slice_in_dim(hidden, (odd ^ flip) * quarter, qua...  4.93 us
    broadcast_in_dim x4, local copies, waits for them, and re-layouts, spread(): return exchange(jnp.broadcast_to(block[None], (count,) + block.shape), axis)  4.6 us
  transfers between devices with their start and end apart: 17, of which 9 were waited for; matrix products, arithmetic and copies ran while one was open for 18% of the time, Pallas kernels for 0%

profile of v1, /device:TPU:1, one launch (start us, length us, event | category | flops | bytes accessed | tf_op | source)
XLA Modules:
  0.0 227.3 jit_solution(4624242706228154359)
XLA Ops:
  2.2 9.0 %all-to-all-start = ((bf16[8,8,1024]{2,1,0:T(8,128)(2,1)}), bf16[8,8,1024]{2,1,0:T(8,128)(2,1)S(1)}, u32[]{:S(2)}, u32[]{:S(2)}) async-start(bf16[8,8,1024]{2,1,0:T(8,128)(2,1)} %broadcast_in_dim.12), calls=%async_computation | async-start | bytes 262144 | tf_op jit(solution)/shard_map/all_to_all | solution.py:28
  11.2 7.8 %all-to-all-done = bf16[8,8,1024]{2,1,0:T(8,128)(2,1)S(1)} async-done(((bf16[8,8,1024]{2,1,0:T(8,128)(2,1)}), bf16[8,8,1024]{2,1,0:T(8,128)(2,1)S(1)}, u32[]{:S(2)}, u32[]{:S(2)}) %all-to-all-start) | async-done | bytes 131104 | tf_op jit(solution)/shard_map/all_to_all | solution.py:28
  19.7 9.4 %all-to-all-start.1 = ((bf16[32,8,512]{2,1,0:T(8,128)(2,1)}), bf16[32,8,512]{2,1,0:T(8,128)(2,1)S(1)}, u32[]{:S(2)}, u32[]{:S(2)}) async-start(bf16[32,8,512]{2,1,0:T(8,128)(2,1)} %bitcast.1), calls=%async_computation.1 | async-start | bytes 524288 | tf_op jit(solution)/shard_map/all_to_all | solution.py:28
  29.1 2.2 constant_dynamic-slice_fusion.4
  31.5 6.5 %all-to-all-done.1 = bf16[32,8,512]{2,1,0:T(8,128)(2,1)S(1)} async-done(((bf16[32,8,512]{2,1,0:T(8,128)(2,1)}), bf16[32,8,512]{2,1,0:T(8,128)(2,1)S(1)}, u32[]{:S(2)}, u32[]{:S(2)}) %all-to-all-start.1) | async-done | bytes 262176 | tf_op jit(solution)/shard_map/all_to_all | solution.py:28
  38.9 3.8 %all-to-all-start.4 = ((bf16[32,8,1024]{2,1,0:T(8,128)(2,1)}), bf16[32,8,1024]{2,1,0:T(8,128)(2,1)S(1)}, u32[]{:S(2)}, u32[]{:S(2)}) async-start(bf16[32,8,1024]{2,1,0:T(8,128)(2,1)} %broadcast_in_dim.16), calls=%async_computation.4 | async-start | bytes 1048576 | tf_op jit(solution)/shard_map/all_to_all | solution.py:28
  44.0 2.8 %fusion.5 = f32[256,1792]{1,0:T(8,128)} fusion(bf16[256,3584]{1,0:T(8,128)(2,1)} %param.7, s32[]{:T(128)S(6)} %select_n.75, bf16[256,512]{1,0:T(8,128)(2,1)S(1)} %bitcast.30, s32[]{:T(128)S(6)} %select_n.74), kind=kOutput, calls=%fused_computation.20 | convolution fusion | flops 234881024 | bytes 2883592 | tf_op jit(solution)/shard_map/dot_general | solution.py:24
  48.5 5.8 %all-to-all-done.4 = bf16[32,8,1024]{2,1,0:T(8,128)(2,1)S(1)} async-done(((bf16[32,8,1024]{2,1,0:T(8,128)(2,1)}), bf16[32,8,1024]{2,1,0:T(8,128)(2,1)S(1)}, u32[]{:S(2)}, u32[]{:S(2)}) %all-to-all-start.4) | async-done | bytes 524320 | tf_op jit(solution)/shard_map/all_to_all | solution.py:28
  54.3 3.0 %convolution_convert_fusion.6 = bf16[256,896]{1,0:T(8,128)(2,1)} fusion(bf16[896,1024]{1,0:T(8,128)(2,1)} %param.8, bf16[32,8,1024]{2,1,0:T(8,128)(2,1)S(1)} %all-to-all-done.4), kind=kOutput, calls=%fused_computation.14 | convolution fusion | flops 469991424 | bytes 2818048 | tf_op jit(solution)/shard_map/dot_general | solution.py:16
  57.3 3.5 %all-to-all-start.5 = ((bf16[8,32,896]{2,1,0:T(8,128)(2,1)}), bf16[8,32,896]{2,1,0:T(8,128)(2,1)S(1)}, u32[]{:S(2)}, u32[]{:S(2)}) async-start(bf16[8,32,896]{2,1,0:T(8,128)(2,1)} %bitcast.6), calls=%async_computation.5 | async-start | bytes 917504 | tf_op jit(solution)/shard_map/all_to_all | solution.py:28
  60.8 2.3 %fusion.1 = bf16[256,1792]{1,0:T(8,128)(2,1)S(1)} fusion(f32[256,1792]{1,0:T(8,128)} %fusion.5, bf16[256,1792]{1,0:T(8,128)(2,1)} %collective-permute-done.1, bf16[256,512]{1,0:T(8,128)(2,1)S(1)} %bitcast.32, s32[]{:T(128)S(6)} %select_n.76), kind=kOutput, calls=%fused_computation.4 | convolution fusion | flops 235798528 | bytes 3801092 | tf_op jit(solution)/shard_map/dot_general | solution.py:24
  66.2 11.1 %all-to-all-done.5 = bf16[8,32,896]{2,1,0:T(8,128)(2,1)S(1)} async-done(((bf16[8,32,896]{2,1,0:T(8,128)(2,1)}), bf16[8,32,896]{2,1,0:T(8,128)(2,1)S(1)}, u32[]{:S(2)}, u32[]{:S(2)}) %all-to-all-start.5) | async-done | bytes 458784 | tf_op jit(solution)/shard_map/all_to_all | solution.py:28
  77.3 4.4 %all-to-all-start.2 = ((bf16[16,16,3584]{2,1,0:T(8,128)(2,1)}), bf16[16,16,3584]{2,1,0:T(8,128)(2,1)}, u32[]{:S(2)}, u32[]{:S(2)}) async-start(bf16[16,16,3584]{2,1,0:T(8,128)(2,1)} %bitcast.29), calls=%async_computation.2 | async-start | bytes 3670016 | tf_op jit(solution)/shard_map/all_to_all | solution.py:28
  81.9 3.7 %collective-permute-start.4 = (bf16[16,896]{1,0:T(8,128)(2,1)S(1)}, bf16[16,896]{1,0:T(8,128)(2,1)S(1)}, u32[]{:S(2)}, u32[]{:S(2)}) collective-permute-start(bf16[16,896]{1,0:T(8,128)(2,1)S(1)} %get-tuple-element.13), channel_id=1, source_target_pairs={{0,0},{1,32},{2,64},{3,96},{4,128},{5,160},{6,192},{7,224},{8,16},... | collective-permute-start | bytes 86024 | tf_op jit(solution)/shard_map/ppermute | solution.py:79
  85.7 24.7 %all-to-all-done.2 = bf16[16,16,3584]{2,1,0:T(8,128)(2,1)} async-done(((bf16[16,16,3584]{2,1,0:T(8,128)(2,1)}), bf16[16,16,3584]{2,1,0:T(8,128)(2,1)}, u32[]{:S(2)}, u32[]{:S(2)}) %all-to-all-start.2) | async-done | bytes 1835040 | tf_op jit(solution)/shard_map/all_to_all | solution.py:28
  112.4 4.8 %collective-permute-start.2 = (bf16[16,896]{1,0:T(8,128)(2,1)S(1)}, bf16[16,896]{1,0:T(8,128)(2,1)S(1)}, u32[]{:S(2)}, u32[]{:S(2)}) collective-permute-start(bf16[16,896]{1,0:T(8,128)(2,1)S(1)} %get-tuple-element.10), channel_id=1, source_target_pairs={{0,0},{32,1},{64,2},{96,3},{128,4},{160,5},{192,6},{224,7},{16,8},... | collective-permute-start | bytes 86024 | tf_op jit(solution)/shard_map/ppermute | solution.py:112
  119.9 13.5 %all-to-all-start.3 = ((bf16[8,32,896]{2,1,0:T(8,128)(2,1)}), bf16[8,32,896]{2,1,0:T(8,128)(2,1)S(1)}, u32[]{:S(2)}, u32[]{:S(2)}) async-start(bf16[8,32,896]{2,1,0:T(8,128)(2,1)} %broadcast_in_dim.15), calls=%async_computation.3 | async-start | bytes 917504 | tf_op jit(solution)/shard_map/all_to_all | solution.py:28
  133.4 15.7 %all-to-all-done.3 = bf16[8,32,896]{2,1,0:T(8,128)(2,1)S(1)} async-done(((bf16[8,32,896]{2,1,0:T(8,128)(2,1)}), bf16[8,32,896]{2,1,0:T(8,128)(2,1)S(1)}, u32[]{:S(2)}, u32[]{:S(2)}) %all-to-all-start.3) | async-done | bytes 458784 | tf_op jit(solution)/shard_map/all_to_all | solution.py:28
  150.5 4.4 %all-to-all-start.6 = ((bf16[16,16,3584]{2,1,0:T(8,128)(2,1)}), bf16[16,16,3584]{2,1,0:T(8,128)(2,1)}, u32[]{:S(2)}, u32[]{:S(2)}) async-start(bf16[16,16,3584]{2,1,0:T(8,128)(2,1)} %broadcast_in_dim.17), calls=%async_computation.6 | async-start | bytes 3670016 | tf_op jit(solution)/shard_map/all_to_all | solution.py:28
  154.9 3.0 %convolution_convert_fusion.5 = bf16[256,1024]{1,0:T(8,128)(2,1)} fusion(bf16[256,896]{1,0:T(8,128)(2,1)S(1)} %bitcast.38, bf16[896,1024]{1,0:T(8,128)(2,1)} %param.8), kind=kOutput, calls=%fused_computation.13 | convolution fusion | flops 470024192 | bytes 2818048 | tf_op jit(solution)/shard_map/dot_general | solution.py:24
  157.9 1.9 convolution_convert_fusion.4
  159.8 20.5 %all-to-all-done.6 = bf16[16,16,3584]{2,1,0:T(8,128)(2,1)} async-done(((bf16[16,16,3584]{2,1,0:T(8,128)(2,1)}), bf16[16,16,3584]{2,1,0:T(8,128)(2,1)}, u32[]{:S(2)}, u32[]{:S(2)}) %all-to-all-start.6) | async-done | bytes 1835040 | tf_op jit(solution)/shard_map/all_to_all | solution.py:28
  182.1 2.6 %convolution_convert_fusion.2 = bf16[256,1792]{1,0:T(8,128)(2,1)} fusion(bf16[256,3584]{1,0:T(8,128)(2,1)} %bitcast.7, bf16[256,512]{1,0:T(8,128)(2,1)S(1)} %bitcast.34, s32[]{:T(128)S(6)} %select_n.76), kind=kOutput, calls=%fused_computation.7 | convolution fusion | flops 235339776 | bytes 1966084 | tf_op jit(solution)/shard_map/dot_general | solution.py:20
  186.3 1.9 fusion.13
  188.2 1.9 fusion.3
  191.2 7.3 %all-to-all-start.7 = ((bf16[32,8,1536]{2,1,0:T(8,128)(2,1)}), bf16[32,8,1536]{2,1,0:T(8,128)(2,1)}, u32[]{:S(2)}, u32[]{:S(2)}) async-start(bf16[32,8,1536]{2,1,0:T(8,128)(2,1)} %maximum_bitcast_fusion), calls=%async_computation.7 | async-start | bytes 1572864 | tf_op jit(solution)/shard_map/all_to_all | solution.py:28
  199.2 2.6 %convolution_convert_fusion = bf16[256,1792]{1,0:T(8,128)(2,1)} fusion(bf16[256,3584]{1,0:T(8,128)(2,1)} %bitcast.7, bf16[256,512]{1,0:T(8,128)(2,1)S(1)} %bitcast.35, s32[]{:T(128)S(6)} %select_n.76), kind=kOutput, calls=%fused_computation.5 | convolution fusion | flops 235339776 | bytes 1966084 | tf_op jit(solution)/shard_map/dot_general | solution.py:20
  201.9 2.6 %convolution_convert_fusion.3 = bf16[256,1792]{1,0:T(8,128)(2,1)} fusion(bf16[256,3584]{1,0:T(8,128)(2,1)} %bitcast.7, bf16[256,512]{1,0:T(8,128)(2,1)S(1)} %bitcast.36, s32[]{:T(128)S(6)} %select_n.74), kind=kOutput, calls=%fused_computation.8 | convolution fusion | flops 235339776 | bytes 1966084 | tf_op jit(solution)/shard_map/dot_general | solution.py:20
  206.1 6.8 %all-to-all-done.7 = bf16[32,8,1536]{2,1,0:T(8,128)(2,1)} async-done(((bf16[32,8,1536]{2,1,0:T(8,128)(2,1)}), bf16[32,8,1536]{2,1,0:T(8,128)(2,1)}, u32[]{:S(2)}, u32[]{:S(2)}) %all-to-all-start.7) | async-done | bytes 786464 | tf_op jit(solution)/shard_map/all_to_all | solution.py:28
  214.6 3.4 %all-to-all-start.8 = ((bf16[8,8,1024]{2,1,0:T(8,128)(2,1)}), bf16[8,8,1024]{2,1,0:T(8,128)(2,1)S(1)}, u32[]{:S(2)}, u32[]{:S(2)}) async-start(bf16[8,8,1024]{2,1,0:T(8,128)(2,1)} %bitcast.12), calls=%async_computation.8 | async-start | bytes 262144 | tf_op jit(solution)/shard_map/all_to_all | solution.py:28
  219.8 3.8 %maximum_select_fusion = bf16[256,3584]{1,0:T(8,128)(2,1)} fusion(bf16[256,1792]{1,0:T(8,128)(2,1)} %collective-permute-done.6, bf16[256,1792]{1,0:T(8,128)(2,1)} %convolution_convert_fusion.3, pred[]{:T(512)S(6)} %eq.6), kind=kLoop, calls=%fused_computation.10 | loop fusion | flops 8257536 | bytes 3670017 | tf_op jit(solution)/shard_map/jit(_where)/select_n | solution.py:148
  223.5 3.1 %maximum_select_fusion.1 = bf16[256,3584]{1,0:T(8,128)(2,1)} fusion(bf16[256,1792]{1,0:T(8,128)(2,1)} %collective-permute-done.7, bf16[256,1792]{1,0:T(8,128)(2,1)S(1)} %convolution_convert_fusion.1, pred[]{:T(512)S(6)} %eq.6), kind=kLoop, calls=%fused_computation.11 | loop fusion | flops 8257536 | bytes 3670017 | tf_op jit(solution)/shard_map/jit(_where)/select_n | solution.py:148
  (51 shorter events, 26.4 us)
Async XLA Ops:
  0.6 42.0 %copy-start = (bf16[256,3584]{1,0:T(8,128)(2,1)S(1)}, bf16[256,3584]{1,0:T(8,128)(2,1)}, u32[]{:S(2)}) copy-start(bf16[256,3584]{1,0:T(8,128)(2,1)} %param.6) | copy-start | bytes 5505028
  0.6 37.3 %copy-start.4 = (bf16[8,1024]{1,0:T(8,128)(2,1)S(1)}, bf16[8,1024]{1,0:T(8,128)(2,1)}, u32[]{:S(2)}) copy-start(bf16[8,1024]{1,0:T(8,128)(2,1)} %param.9) | copy-start | bytes 49156
  2.2 16.8 %all-to-all-start = ((bf16[8,8,1024]{2,1,0:T(8,128)(2,1)}), bf16[8,8,1024]{2,1,0:T(8,128)(2,1)S(1)}, u32[]{:S(2)}, u32[]{:S(2)}) async-start(bf16[8,8,1024]{2,1,0:T(8,128)(2,1)} %broadcast_in_dim.12), calls=%async_computation | async-start | bytes 262144 | tf_op jit(solution)/shard_map/all_to_all | solution.py:28
  19.7 18.3 %all-to-all-start.1 = ((bf16[32,8,512]{2,1,0:T(8,128)(2,1)}), bf16[32,8,512]{2,1,0:T(8,128)(2,1)S(1)}, u32[]{:S(2)}, u32[]{:S(2)}) async-start(bf16[32,8,512]{2,1,0:T(8,128)(2,1)} %bitcast.1), calls=%async_computation.1 | async-start | bytes 524288 | tf_op jit(solution)/shard_map/all_to_all | solution.py:28
  31.3 29.6 %collective-permute-start.1 = (bf16[256,1792]{1,0:T(8,128)(2,1)}, bf16[256,1792]{1,0:T(8,128)(2,1)}, u32[]{:S(2)}, u32[]{:S(2)}) collective-permute-start(bf16[256,1792]{1,0:T(8,128)(2,1)} %constant_dynamic-slice_fusion.4), channel_id=1, source_target_pairs={{0,8},{8,0},{1,9},{9,1},{2,10},{10,2},{3,11},{11,3},{4,12},{12,4},... | collective-permute-start | bytes 2752520 | tf_op jit(solution)/shard_map/ppermute | solution.py:67
  38.9 15.4 %all-to-all-start.4 = ((bf16[32,8,1024]{2,1,0:T(8,128)(2,1)}), bf16[32,8,1024]{2,1,0:T(8,128)(2,1)S(1)}, u32[]{:S(2)}, u32[]{:S(2)}) async-start(bf16[32,8,1024]{2,1,0:T(8,128)(2,1)} %broadcast_in_dim.16), calls=%async_computation.4 | async-start | bytes 1048576 | tf_op jit(solution)/shard_map/all_to_all | solution.py:28
  43.7 19.5 %collective-permute-start = (bf16[256,1792]{1,0:T(8,128)(2,1)}, bf16[256,1792]{1,0:T(8,128)(2,1)}, u32[]{:S(2)}, u32[]{:S(2)}) collective-permute-start(bf16[256,1792]{1,0:T(8,128)(2,1)} %constant_dynamic-slice_fusion.5), channel_id=1, source_target_pairs={{0,8},{8,0},{1,9},{9,1},{2,10},{10,2},{3,11},{11,3},{4,12},{12,4},... | collective-permute-start | bytes 2752520 | tf_op jit(solution)/shard_map/ppermute | solution.py:67
  57.3 20.0 %all-to-all-start.5 = ((bf16[8,32,896]{2,1,0:T(8,128)(2,1)}), bf16[8,32,896]{2,1,0:T(8,128)(2,1)S(1)}, u32[]{:S(2)}, u32[]{:S(2)}) async-start(bf16[8,32,896]{2,1,0:T(8,128)(2,1)} %bitcast.6), calls=%async_computation.5 | async-start | bytes 917504 | tf_op jit(solution)/shard_map/all_to_all | solution.py:28
  60.8 2.4 %copy-start.1 = (f32[256,1792]{1,0:T(8,128)S(1)}, f32[256,1792]{1,0:T(8,128)}, u32[]{:S(2)}) copy-start(f32[256,1792]{1,0:T(8,128)} %fusion.9) | copy-start | bytes 5505028
  77.3 33.1 %all-to-all-start.2 = ((bf16[16,16,3584]{2,1,0:T(8,128)(2,1)}), bf16[16,16,3584]{2,1,0:T(8,128)(2,1)}, u32[]{:S(2)}, u32[]{:S(2)}) async-start(bf16[16,16,3584]{2,1,0:T(8,128)(2,1)} %bitcast.29), calls=%async_computation.2 | async-start | bytes 3670016 | tf_op jit(solution)/shard_map/all_to_all | solution.py:28
  81.9 30.3 %collective-permute-start.4 = (bf16[16,896]{1,0:T(8,128)(2,1)S(1)}, bf16[16,896]{1,0:T(8,128)(2,1)S(1)}, u32[]{:S(2)}, u32[]{:S(2)}) collective-permute-start(bf16[16,896]{1,0:T(8,128)(2,1)S(1)} %get-tuple-element.13), channel_id=1, source_target_pairs={{0,0},{1,32},{2,64},{3,96},{4,128},{5,160},{6,192},{7,224},{8,16},... | collective-permute-start | bytes 86024 | tf_op jit(solution)/shard_map/ppermute | solution.py:79
  85.6 26.6 %collective-permute-start.5 = (bf16[16,896]{1,0:T(8,128)(2,1)S(1)}, bf16[16,896]{1,0:T(8,128)(2,1)S(1)}, u32[]{:S(2)}, u32[]{:S(2)}) collective-permute-start(bf16[16,896]{1,0:T(8,128)(2,1)S(1)} %get-tuple-element.12), channel_id=1, source_target_pairs={{0,16},{1,48},{2,80},{3,112},{4,144},{5,176},{6,208},{7,240},{8,0}... | collective-permute-start | bytes 86024 | tf_op jit(solution)/shard_map/ppermute | solution.py:79
  112.3 5.0 %collective-permute-start.3 = (bf16[16,896]{1,0:T(8,128)(2,1)S(1)}, bf16[16,896]{1,0:T(8,128)(2,1)S(1)}, u32[]{:S(2)}, u32[]{:S(2)}) collective-permute-start(bf16[16,896]{1,0:T(8,128)(2,1)S(1)} %get-tuple-element.11), channel_id=1, source_target_pairs={{16,0},{48,1},{80,2},{112,3},{144,4},{176,5},{208,6},{240,7},{0,8}... | collective-permute-start | bytes 86024 | tf_op jit(solution)/shard_map/ppermute | solution.py:112
  112.4 6.6 %collective-permute-start.2 = (bf16[16,896]{1,0:T(8,128)(2,1)S(1)}, bf16[16,896]{1,0:T(8,128)(2,1)S(1)}, u32[]{:S(2)}, u32[]{:S(2)}) collective-permute-start(bf16[16,896]{1,0:T(8,128)(2,1)S(1)} %get-tuple-element.10), channel_id=1, source_target_pairs={{0,0},{32,1},{64,2},{96,3},{128,4},{160,5},{192,6},{224,7},{16,8},... | collective-permute-start | bytes 86024 | tf_op jit(solution)/shard_map/ppermute | solution.py:112
  119.9 29.2 %all-to-all-start.3 = ((bf16[8,32,896]{2,1,0:T(8,128)(2,1)}), bf16[8,32,896]{2,1,0:T(8,128)(2,1)S(1)}, u32[]{:S(2)}, u32[]{:S(2)}) async-start(bf16[8,32,896]{2,1,0:T(8,128)(2,1)} %broadcast_in_dim.15), calls=%async_computation.3 | async-start | bytes 917504 | tf_op jit(solution)/shard_map/all_to_all | solution.py:28
  150.5 29.8 %all-to-all-start.6 = ((bf16[16,16,3584]{2,1,0:T(8,128)(2,1)}), bf16[16,16,3584]{2,1,0:T(8,128)(2,1)}, u32[]{:S(2)}, u32[]{:S(2)}) async-start(bf16[16,16,3584]{2,1,0:T(8,128)(2,1)} %broadcast_in_dim.17), calls=%async_computation.6 | async-start | bytes 3670016 | tf_op jit(solution)/shard_map/all_to_all | solution.py:28
  180.3 4.3 %copy-start.2 = (bf16[256,3584]{1,0:T(8,128)(2,1)S(1)}, bf16[256,3584]{1,0:T(8,128)(2,1)}, u32[]{:S(2)}) copy-start(bf16[256,3584]{1,0:T(8,128)(2,1)} %param.7) | copy-start | bytes 5505028
  188.2 2.1 copy-start.3
  191.2 21.7 %all-to-all-start.7 = ((bf16[32,8,1536]{2,1,0:T(8,128)(2,1)}), bf16[32,8,1536]{2,1,0:T(8,128)(2,1)}, u32[]{:S(2)}, u32[]{:S(2)}) async-start(bf16[32,8,1536]{2,1,0:T(8,128)(2,1)} %maximum_bitcast_fusion), calls=%async_computation.7 | async-start | bytes 1572864 | tf_op jit(solution)/shard_map/all_to_all | solution.py:28
  198.6 21.2 %collective-permute-start.6 = (bf16[256,1792]{1,0:T(8,128)(2,1)}, bf16[256,1792]{1,0:T(8,128)(2,1)}, u32[]{:S(2)}, u32[]{:S(2)}) collective-permute-start(bf16[256,1792]{1,0:T(8,128)(2,1)} %convolution_convert_fusion.2), channel_id=1, source_target_pairs={{0,8},{8,0},{1,9},{9,1},{2,10},{10,2},{3,11},{11,3},{4,12},{12,4},... | collective-permute-start | bytes 2752520 | tf_op jit(solution)/shard_map/ppermute | solution.py:147
  201.8 21.7 %collective-permute-start.7 = (bf16[256,1792]{1,0:T(8,128)(2,1)}, bf16[256,1792]{1,0:T(8,128)(2,1)}, u32[]{:S(2)}, u32[]{:S(2)}) collective-permute-start(bf16[256,1792]{1,0:T(8,128)(2,1)} %convolution_convert_fusion), channel_id=1, source_target_pairs={{0,8},{8,0},{1,9},{9,1},{2,10},{10,2},{3,11},{11,3},{4,12},{12,4},... | collective-permute-start | bytes 2752520 | tf_op jit(solution)/shard_map/ppermute | solution.py:147
  214.6 12.0 %all-to-all-start.8 = ((bf16[8,8,1024]{2,1,0:T(8,128)(2,1)}), bf16[8,8,1024]{2,1,0:T(8,128)(2,1)S(1)}, u32[]{:S(2)}, u32[]{:S(2)}) async-start(bf16[8,8,1024]{2,1,0:T(8,128)(2,1)} %bitcast.12), calls=%async_computation.8 | async-start | bytes 262144 | tf_op jit(solution)/shard_map/all_to_all | solution.py:28

commit v2 on v1

v2 whole, which is shorter than its diff:
```python
import jax
import jax.numpy as jnp
from jax import lax
from jax.experimental import pallas as pl
from jax.experimental.pallas import tpu as pltpu
from jax.sharding import Mesh, PartitionSpec as P

Y, X, CORES, Z = 4, 4, 2, 8
CHIPS = Y * X
ROWS = CHIPS * CORES
PLANE = ("y", "x")
ROW = ("y", "x", "core")
EVERY = ("y", "x", "core", "z")
SWAP = [(0, 1), (1, 0)]
BF16, F32 = jnp.bfloat16, jnp.float32
VMEM_LIMIT = 48 * 1024 * 1024


def rows_times(left, right):
    return lax.dot_general(left, right, (((1,), (1,)), ((), ())), preferred_element_type=F32)


def columns_times(left, right):
    return lax.dot_general(left, right, (((0,), (0,)), ((), ())), preferred_element_type=F32)


def times(left, right):
    return jnp.dot(left, right, preferred_element_type=F32)


def exchange(blocks, axis):
    return lax.all_to_all(blocks, axis, split_axis=0, concat_axis=0, tiled=True)


def total(blocks):
    return jnp.sum(blocks.astype(F32), axis=0)


def pairs(distance):
    return [(z, z ^ distance) for z in range(Z)]


def paired(at_core, own, got):
    return jnp.where(at_core == 0, jnp.stack([own, got]), jnp.stack([got, own]))


def gather_columns(block, late=()):
    z = lax.axis_index("z")
    share = block[None, None, None]
    for axis, distance in enumerate((4, 2, 1)):
        got = lax.ppermute(share, "z", pairs(distance))
        if axis == 0 and late:
            got, *late = lax.optimization_barrier((got, *late))
        low = (z // distance) % 2 == 0
        share = jnp.where(
            low, jnp.concatenate([share, got], axis), jnp.concatenate([got, share], axis)
        )
    share = share.reshape((Z,) + block.shape)
    return (share, *late) if late else share


def scatter_columns(blocks, after=None):
    z = lax.axis_index("z")
    share = blocks.reshape((2, 2, 2) + blocks.shape[1:])
    for axis, distance in ((2, 1), (1, 2), (0, 4)):
        bit = (z // distance) % 2
        keep = lax.dynamic_index_in_dim(share, bit, axis, keepdims=False)
        send = lax.dynamic_index_in_dim(share, 1 - bit, axis, keepdims=False)
        got = lax.ppermute(send, "z", pairs(distance))
        if axis == 2 and after is not None:
            got, after = lax.optimization_barrier((got, after))
        share = (keep.astype(F32) + got.astype(F32)).astype(BF16)
    return share if after is None else (share, after)


def owner_route():
    route = []
    for chip in range(CHIPS):
        for core in range(CORES):
            for z in range(Z):
                source = (chip * CORES + core) * Z + z
                target = ((2 * z + core) * CORES + chip % 2) * Z + chip // 2
                route.append((source, target))
    return route


TO_OWNER = owner_route()


def call(body, core, arrays, in_specs, out_shapes, out_specs, steps, scratch=(), aliases=None, cost=0):
    moved = sum(a.size * a.dtype.itemsize for a in arrays)
    return pl.pallas_call(
        body,
        grid_spec=pltpu.PrefetchScalarGridSpec(
            num_scalar_prefetch=1,
            grid=(steps,),
            in_specs=in_specs,
            out_specs=out_specs,
            scratch_shapes=list(scratch),
        ),
        out_shape=out_shapes,
        input_output_aliases=aliases or {},
        cost_estimate=pl.CostEstimate(flops=cost, bytes_accessed=moved, transcendentals=0),
        compiler_params=pltpu.CompilerParams(vmem_limit_bytes=VMEM_LIMIT),
    )(core, *arrays)


def my_columns(step, core, *_):
    return (0, 2 * core[0] + step)


def your_columns(step, core, *_):
    return (0, 2 * (1 - core[0]) + step)


def in_turn(step, *_):
    return (0, step)


def panels(core, panel_ref, depth):
    first, second = panel_ref[:, :depth], panel_ref[:, depth:]
    own = core[0] == 0
    return jnp.where(own, first, second), jnp.where(own, second, first)


def forward_products(core, arrivals, gate_weight, gate_got, up_weight, up_got):
    rows, depth = arrivals.shape[0], gate_weight.shape[0]
    quarter = gate_weight.shape[1] // 4

    def body(core, panel, gate_mine, gate_other, up_mine, up_other, out):
        mine, other = panels(core, panel, depth)
        gate = times(mine, gate_mine[...]) + times(other, gate_other[...])
        out[:, :quarter] = gate.astype(BF16)
        up = times(mine, up_mine[...]) + times(other, up_other[...])
        out[:, quarter:] = up.astype(BF16)

    weight = pl.BlockSpec((depth, quarter), my_columns)
    got = pl.BlockSpec((depth, quarter), in_turn)
    return call(
        body,
        core,
        (arrivals, gate_weight, gate_got, up_weight, up_got),
        [pl.BlockSpec((rows, 2 * depth), lambda step, core: (0, 0)), weight, got, weight, got],
        jax.ShapeDtypeStruct((rows, 4 * quarter), BF16),
        pl.BlockSpec((rows, 2 * quarter), in_turn),
        2,
        cost=16 * rows * depth * quarter,
    )


def activations(core, terms, grad_hidden):
    chips, tall, wide = terms.shape
    quarter = wide // 4

    def body(core, terms, grad_hidden, copies, keep, send):
        both = terms[0].astype(F32)
        for chip in range(1, chips):
            both = both + terms[chip].astype(F32)
        gate, up = both[:, :quarter], both[:, quarter:]
        sigmoid_gate = 1.0 / (1.0 + jnp.exp(-gate))
        silu_gate = gate * sigmoid_gate
        hidden = (silu_gate * up).astype(BF16)

        @pl.when(pl.program_id(0) == core[0])
        def _():
            keep[...] = hidden

        @pl.when(pl.program_id(0) != core[0])
        def _():
            send[...] = hidden

        cotangent = grad_hidden[0].astype(F32)
        grad_gate = cotangent * up * sigmoid_gate * (1.0 + gate * (1.0 - sigmoid_gate))
        grad_gate = grad_gate.astype(BF16)
        grad_up = (cotangent * silu_gate).astype(BF16)
        for chip in range(chips):
            copies[chip, :, :quarter] = grad_gate
            copies[chip, :, quarter:] = grad_up

    half = pl.BlockSpec((chips, tall, 2 * quarter), lambda step, core: (0, 0, step))
    flat = pl.BlockSpec((tall, quarter), lambda step, core: (0, 0))
    return call(
        body,
        core,
        (terms, grad_hidden),
        [half, pl.BlockSpec((1, tall, quarter), lambda step, core: (step, 0, 0))],
        [jax.ShapeDtypeStruct(terms.shape, BF16)]
        + [jax.ShapeDtypeStruct((tall, quarter), BF16)] * 2,
        [half, flat, flat],
        2,
        cost=30 * tall * wide,
    )


def token_products(core, pieces, gate_weight, gate_got, up_weight, up_got):
    depth = gate_weight.shape[0]
    rows, half = pieces.shape[0], pieces.shape[1] // 2
    quarter = half // 2

    def body(core, piece, gate_mine, gate_other, up_mine, up_other, out, mine, other):
        piece_gate, piece_up = piece[:, :quarter], piece[:, quarter:]
        term_mine = rows_times(piece_gate, gate_mine[...]) + rows_times(piece_up, up_mine[...])
        term_other = rows_times(piece_gate, gate_other[...]) + rows_times(piece_up, up_other[...])

        @pl.when(pl.program_id(0) == 0)
        def _():
            mine[...] = term_mine
            other[...] = term_other

        @pl.when(pl.program_id(0) == 1)
        def _():
            sum_mine = (mine[...] + term_mine).astype(BF16)
            sum_other = (other[...] + term_other).astype(BF16)
            own = core[0] == 0
            out[:, :depth] = jnp.where(own, sum_mine, sum_other)
            out[:, depth:] = jnp.where(own, sum_other, sum_mine)

    weight = pl.BlockSpec((depth, quarter), my_columns)
    got = pl.BlockSpec((depth, quarter), in_turn)
    return call(
        body,
        core,
        (pieces, gate_weight, gate_got, up_weight, up_got),
        [
            pl.BlockSpec((rows, half), in_turn),
            weight,
            got,
            weight,
            got,
        ],
        jax.ShapeDtypeStruct((rows, 2 * depth), BF16),
        pl.BlockSpec((rows, 2 * depth), lambda step, core: (0, 0)),
        2,
        scratch=[pltpu.VMEM((rows, depth), F32)] * 2,
        cost=16 * rows * depth * quarter,
    )


def output_product(core, hidden_panel, down_weight, token_part):
    rows, quarter = hidden_panel.shape
    width, features = down_weight.shape[1], token_part.shape[1]

    def body(core, hidden, down, tokens, out):
        out[:, :width] = times(hidden[...], down[...]).astype(BF16)
        out[:, width:] = tokens[...]

    def whole(*shape):
        return pl.BlockSpec(shape, lambda step, core: (0, 0))

    return call(
        body,
        core,
        (hidden_panel, down_weight, token_part),
        [whole(rows, quarter), whole(quarter, width), whole(rows, features)],
        jax.ShapeDtypeStruct((rows, width + features), BF16),
        whole(rows, width + features),
        1,
        cost=2 * rows * quarter * width,
    )


def weight_grads(core, arrivals, pieces, depth):
    rows = arrivals.shape[0]
    wide = pieces.shape[1] // 2
    quarter = wide // 2

    def body(core, panel, piece, gate_grad, up_grad, gate_send, up_send):
        mine, other = panels(core, panel, depth)
        piece_gate, piece_up = piece[:, :quarter], piece[:, quarter:]
        gate_send[...] = columns_times(other, piece_gate).astype(BF16)
        up_send[...] = columns_times(other, piece_up).astype(BF16)
        gate_grad[...] = columns_times(mine, piece_gate).astype(BF16)
        up_grad[...] = columns_times(mine, piece_up).astype(BF16)

    mine = pl.BlockSpec((depth, quarter), my_columns)
    send = pl.BlockSpec((depth, quarter), in_turn)
    return call(
        body,
        core,
        (arrivals, pieces),
        [
            pl.BlockSpec((rows, 2 * depth), lambda step, core: (0, 0)),
            pl.BlockSpec((rows, wide), in_turn),
        ],
        [jax.ShapeDtypeStruct((depth, 4 * quarter), BF16)] * 2
        + [jax.ShapeDtypeStruct((depth, 2 * quarter), BF16)] * 2,
        [mine, mine, send, send],
        2,
        cost=16 * rows * depth * quarter,
    )


def fill(core, gate_grad, up_grad, gate_got, up_got):
    depth, units = gate_grad.shape
    quarter = units // 4

    def body(core, _, __, gate_got, up_got, gate_out, up_out):
        gate_out[...] = gate_got[...]
        up_out[...] = up_got[...]

    anywhere = pl.BlockSpec(memory_space=pl.ANY)
    got = pl.BlockSpec((depth, quarter), in_turn)
    out = pl.BlockSpec((depth, quarter), your_columns)
    return call(
        body,
        core,
        (gate_grad, up_grad, gate_got, up_got),
        [anywhere, anywhere, got, got],
        [jax.ShapeDtypeStruct(gate_grad.shape, BF16)] * 2,
        [out, out],
        2,
        aliases={1: 0, 2: 1},
    )


def local(tokens, gate_weight, up_weight, down_weight, out_grad):
    at_core = lax.axis_index("core")
    core = at_core.astype(jnp.int32).reshape(1)
    few, width = tokens.shape
    depth, units = gate_weight.shape
    half, quarter = units // 2, units // 4

    def swapped_half(weight):
        theirs = lax.dynamic_slice_in_dim(weight, (1 - at_core) * half, half, 1)
        return lax.ppermute(theirs, "core", SWAP)

    features = 2 * depth
    copies = jnp.broadcast_to(out_grad[None], (ROWS, few, width))
    cotangent = exchange(copies, ROW).reshape(ROWS * few, width)

    parts, gate_late, up_late = gather_columns(tokens, (gate_weight, up_weight))
    parts = parts.reshape(Z, few, 2, features).transpose(0, 2, 1, 3)
    parts = parts.reshape(CHIPS, 1, few, features)
    parts = jnp.broadcast_to(parts, (CHIPS, CORES, few, features))
    parts = parts.reshape(ROWS, few, features)
    parts, cotangent = lax.optimization_barrier((parts, cotangent))
    arrivals = exchange(parts, ROW).reshape(ROWS * few, features)

    hidden_part = rows_times(cotangent, down_weight).astype(BF16)
    hidden_sum, arrivals = scatter_columns(hidden_part.reshape(Z, -1, quarter), arrivals)
    hidden_sum = hidden_sum.reshape(2, -1, quarter)
    hidden_keep = lax.dynamic_index_in_dim(hidden_sum, at_core, 0, keepdims=False)
    hidden_send = lax.dynamic_index_in_dim(hidden_sum, 1 - at_core, 0, keepdims=False)
    hidden_sum = paired(at_core, hidden_keep, lax.ppermute(hidden_send, "core", SWAP))
    grad_hidden = lax.ppermute(hidden_sum, EVERY, TO_OWNER)

    gate_got, up_got = swapped_half(gate_late), swapped_half(up_late)
    sent = forward_products(core, arrivals, gate_weight, gate_got, up_weight, up_got)

    terms = exchange(sent.reshape(CHIPS, -1, units), PLANE)
    copies, hidden_keep, hidden_send = activations(core, terms, grad_hidden)
    hidden = paired(at_core, hidden_keep, lax.ppermute(hidden_send, "core", SWAP))
    hidden = gather_columns(hidden).reshape(CHIPS, -1, quarter)
    pieces = exchange(copies, PLANE).reshape(-1, units)
    pieces, hidden = lax.optimization_barrier((pieces, hidden))
    hidden_panel = exchange(hidden, PLANE).reshape(-1, quarter)

    token_part = token_products(core, pieces, gate_weight, gate_got, up_weight, up_got)
    parts = output_product(core, hidden_panel, down_weight, token_part)
    parts = exchange(parts.reshape(ROWS, few, width + features), ROW)

    gate_grad, up_grad, gate_send, up_send = weight_grads(core, arrivals, pieces, depth)
    grad_down_weight = columns_times(hidden_panel, cotangent).astype(BF16)
    parts, gate_send, grad_down_weight = lax.optimization_barrier(
        (parts, gate_send, grad_down_weight)
    )
    output = total(parts[:, :, :width]).astype(BF16)
    terms = parts[:, :, width:].reshape(CHIPS, CORES, few, features).astype(F32)
    terms = jnp.sum(terms, axis=1).astype(BF16).reshape(Z, 2, few, features)
    terms = terms.transpose(0, 2, 1, 3).reshape(Z, few, width)
    terms = exchange(terms, "z")

    gate_back = lax.ppermute(gate_send, "core", SWAP)
    up_back = lax.ppermute(up_send, "core", SWAP)
    gate_grad, up_grad = fill(core, gate_grad, up_grad, gate_back, up_back)
    terms, gate_grad, up_grad = lax.optimization_barrier((terms, gate_grad, up_grad))
    grad_tokens = total(terms).astype(BF16)
    return output, grad_tokens, gate_grad, up_grad, grad_down_weight


def solution(mesh):
    fine = Mesh(mesh.devices.reshape(Y, X, CORES, Z), EVERY)
    spec = P(ROW, "z")
    return jax.shard_map(
        local, mesh=fine, in_specs=(spec,) * 5, out_specs=(spec,) * 5, check_vma=False
    )
```

time: 229 us -> 181 us (0.79)
  waiting for transfers between devices: 101 us -> 71 us
  matrix products: 32.9 us -> 4.27 us
  Pallas kernels: 0 us -> 14.6 us
  other arithmetic: 15.3 us -> 6.87 us
  local copies, waits for them, and re-layouts: 8.57 us -> 12.1 us
    all_to_all x9 -> x7, waiting for transfers between devices: 99 us -> 23.9 us  [exchange(): return lax.all_to_all(blocks, axis, split_axis=0, concat_axis=0, tiled=True)]
    ppermute x8 -> x16, waiting for transfers between devices: 1.79 us -> 47.1 us  [the longest x6 23.3 us: gather_columns(): got = lax.ppermute(share, 'z', pairs(distance))]
    pallas_call x0 -> x6, Pallas kernels: none -> 14.6 us  [call(): pl.pallas_call(body, grid_spec=pltpu.PrefetchScalarGridSpec(num_scalar_pr...]
    dot_general x5 -> x0, matrix products: 11.4 us -> none  [times(): return jnp.dot(left, right, preferred_element_type=F32)]
    ppermute x8 -> x16, starting transfers between devices: 10.1 us -> 20.7 us  [the longest x6 10.2 us: gather_columns(): got = lax.ppermute(share, 'z', pairs(distance))]
    dot_general x5 -> x1, matrix products: 11.2 us -> 1.9 us  [columns_times(): lax.dot_general(left, right, (((0,), (0,)), ((), ())), preferred_element_...]
    all_to_all x9 -> x7, starting transfers between devices: 58.7 us -> 49.6 us  [exchange(): return lax.all_to_all(blocks, axis, split_axis=0, concat_axis=0, tiled=True)]
    dot_general x5 -> x1, matrix products: 10.3 us -> 2.37 us  [rows_times(): lax.dot_general(left, right, (((1,), (1,)), ((), ())), preferred_element_...]
  transfers between devices with their start and end apart: 17 -> 23, of which waited for: 9 -> 16; matrix products, arithmetic and copies ran while one was open for 18% -> 9% of each run, Pallas kernels for 0% -> 5%
where the time goes in v2:
time: 181 us; the launch traced here: 180 us
  waiting for transfers between devices  71 us (39%)
  starting transfers between devices  70.4 us (39%)
  Pallas kernels  14.6 us (8%)
  local copies, waits for them, and re-layouts  12.1 us (7%)
  other arithmetic  6.87 us (4%)
  matrix products  4.27 us (2%)
    all_to_all x7, starting transfers between devices, exchange(): return lax.all_to_all(blocks, axis, split_axis=0, concat_axis=0, tiled=True)  49.6 us
    all_to_all x7, waiting for transfers between devices, exchange(): return lax.all_to_all(blocks, axis, split_axis=0, concat_axis=0, tiled=True)  23.9 us
    ppermute x6, waiting for transfers between devices, gather_columns(): got = lax.ppermute(share, 'z', pairs(distance))  23.3 us
    ppermute x3, waiting for transfers between devices, scatter_columns(): got = lax.ppermute(send, 'z', pairs(distance))  20 us
    pallas_call x6, Pallas kernels, call(): pl.pallas_call(body, grid_spec=pltpu.PrefetchScalarGridSpec(num_scalar_pr...  14.6 us
    ppermute x6, starting transfers between devices, gather_columns(): got = lax.ppermute(share, 'z', pairs(distance))  10.2 us
    unnamed x22, local copies, waits for them, and re-layouts  6.5 us
  transfers between devices with their start and end apart: 23, of which 16 were waited for; matrix products, arithmetic and copies ran while one was open for 9% of the time, Pallas kernels for 5%

profile of v2, /device:TPU:1, one launch (start us, length us, event | category | flops | bytes accessed | tf_op | source)
XLA Modules:
  0.0 180.2 jit_solution(1841492232953379827)
XLA Ops:
  0.6 7.8 %collective-permute-start = (bf16[1,1,1,8,1024]{4,3,2,1,0:T(8,128)(2,1)}, bf16[1,1,1,8,1024]{4,3,2,1,0:T(8,128)(2,1)S(1)}, u32[]{:S(2)}, u32[]{:S(2)}) collective-permute-start(bf16[1,1,1,8,1024]{4,3,2,1,0:T(8,128)(2,1)} %bitcast.81), channel_id=1, source_target_pairs={{0,4},{1,5},{2,6},{3,7},{4,0},{5,1},{6,2},{7,3},{8,12},{9,13},{10,... | collective-permute-start | bytes 49160 | tf_op jit(solution)/shard_map/ppermute | solution.py:51
  10.0 8.0 %all-to-all-start = ((bf16[32,8,1024]{2,1,0:T(8,128)(2,1)}), bf16[32,8,1024]{2,1,0:T(8,128)(2,1)S(1)}, u32[]{:S(2)}, u32[]{:S(2)}) async-start(bf16[32,8,1024]{2,1,0:T(8,128)(2,1)} %broadcast_in_dim.20), calls=%async_computation | async-start | bytes 1048576 | tf_op jit(solution)/shard_map/all_to_all | solution.py:32
  20.2 2.2 %constant_dynamic-slice_fusion.3 = bf16[256,1792]{1,0:T(8,128)(2,1)} fusion(bf16[256,3584]{1,0:T(8,128)(2,1)} %gate_mine.3, s32[]{:T(128)S(6)} %select_n.269), kind=kLoop, calls=%fused_computation.33 | loop fusion | bytes 1835012 | tf_op jit(solution)/shard_map/dynamic_slice | solution.py:324
  24.8 2.7 %collective-permute-done.2 = bf16[2,2,1,8,1024]{4,3,2,1,0:T(8,128)(2,1)S(1)} collective-permute-done((bf16[2,2,1,8,1024]{4,3,2,1,0:T(8,128)(2,1)S(1)}, bf16[2,2,1,8,1024]{4,3,2,1,0:T(8,128)(2,1)S(1)}, u32[]{:S(2)}, u32[]{:S(2)}) %collective-permute-start.2) | collective-permute-done | bytes 65568 | tf_op jit(solution)/shard_map/ppermute | solution.py:51
  27.5 2.2 %all-to-all-done = bf16[32,8,1024]{2,1,0:T(8,128)(2,1)S(1)} async-done(((bf16[32,8,1024]{2,1,0:T(8,128)(2,1)}), bf16[32,8,1024]{2,1,0:T(8,128)(2,1)S(1)}, u32[]{:S(2)}, u32[]{:S(2)}) %all-to-all-start) | async-done | bytes 524320 | tf_op jit(solution)/shard_map/all_to_all | solution.py:32
  30.4 6.4 %all-to-all-start.1 = ((bf16[32,8,512]{2,1,0:T(8,128)(2,1)}), bf16[32,8,512]{2,1,0:T(8,128)(2,1)S(1)}, u32[]{:S(2)}, u32[]{:S(2)}) async-start(bf16[32,8,512]{2,1,0:T(8,128)(2,1)} %bitcast.8), calls=%async_computation.1 | async-start | bytes 524288 | tf_op jit(solution)/shard_map/all_to_all | solution.py:32
  36.8 2.4 %convolution_convert_fusion.1 = bf16[256,896]{1,0:T(8,128)(2,1)S(1)} fusion(bf16[256,1024]{1,0:T(8,128)(2,1)S(1)} %bitcast.71, bf16[896,1024]{1,0:T(8,128)(2,1)} %down.1), kind=kOutput, calls=%fused_computation.1 | convolution fusion | flops 469991424 | bytes 2818048 | tf_op jit(solution)/shard_map/dot_general | solution.py:20
  40.1 6.3 %collective-permute-done.3 = bf16[2,2,32,896]{3,2,0,1:T(8,128)(2,1)} collective-permute-done((bf16[2,2,32,896]{3,2,0,1:T(8,128)(2,1)S(1)}, bf16[2,2,32,896]{3,2,0,1:T(8,128)(2,1)}, u32[]{:S(2)}, u32[]{:S(2)}) %collective-permute-start.3) | collective-permute-done | bytes 229408 | tf_op jit(solution)/shard_map/ppermute | solution.py:69
  46.4 2.8 %shard_map.92 = bf16[256,3584]{1,0:T(8,128)(2,1)S(1)} custom-call(s32[1]{0:T(128)} %bitcast.core, bf16[256,512]{1,0:T(8,128)(2,1)S(1)} %bitcast.67, bf16[256,3584]{1,0:T(8,128)(2,1)S(1)} %copy-done, bf16[256,1792]{1,0:T(8,128)(2,1)} %collective-permute-done.4.gate_other, bf16[256,3584]{1,0:T(8,128)(2,1)} %up_mine.3, ...), custom_call_target="tpu_custom_call" | custom-call | flops 939524096 | bytes 5767168 | tf_op jit(solution)/shard_map/pallas_call | solution.py:92
  50.5 6.6 %all-to-all-start.2 = ((bf16[16,16,3584]{2,1,0:T(8,128)(2,1)}), bf16[16,16,3584]{2,1,0:T(8,128)(2,1)}, u32[]{:S(2)}, u32[]{:S(2)}) async-start(bf16[16,16,3584]{2,1,0:T(8,128)(2,1)} %bitcast.64), calls=%async_computation.2 | async-start | bytes 3670016 | tf_op jit(solution)/shard_map/all_to_all | solution.py:32
  59.4 6.7 %collective-permute-done.6 = bf16[2,32,896]{2,1,0:T(8,128)(2,1)S(1)} collective-permute-done((bf16[2,32,896]{2,1,0:T(8,128)(2,1)S(1)}, bf16[2,32,896]{2,1,0:T(8,128)(2,1)S(1)}, u32[]{:S(2)}, u32[]{:S(2)}) %collective-permute-start.6) | collective-permute-done | bytes 114720 | tf_op jit(solution)/shard_map/ppermute | solution.py:69
  66.2 7.0 %collective-permute-done.7 = bf16[32,896]{1,0:T(8,128)(2,1)S(1)} collective-permute-done((bf16[32,896]{1,0:T(8,128)(2,1)S(1)}, bf16[32,896]{1,0:T(8,128)(2,1)S(1)}, u32[]{:S(2)}, u32[]{:S(2)}) %collective-permute-start.7) | collective-permute-done | bytes 57376 | tf_op jit(solution)/shard_map/ppermute | solution.py:69
  73.3 2.2 %collective-permute-start.8 = (bf16[16,896]{1,0:T(8,128)(2,1)S(1)}, bf16[16,896]{1,0:T(8,128)(2,1)S(1)}, u32[]{:S(2)}, u32[]{:S(2)}) collective-permute-start(bf16[16,896]{1,0:T(8,128)(2,1)S(1)} %get-tuple-element.58), channel_id=1, source_target_pairs={{0,8},{8,0},{1,9},{9,1},{2,10},{10,2},{3,11},{11,3},{4,12},{12,4},... | collective-permute-start | bytes 86024 | tf_op jit(solution)/shard_map/ppermute | solution.py:344
  76.4 3.5 %collective-permute-start.9 = (bf16[2,16,896]{2,1,0:T(8,128)(2,1)S(1)}, bf16[2,16,896]{2,1,0:T(8,128)(2,1)S(1)}, u32[]{:S(2)}, u32[]{:S(2)}) collective-permute-start(bf16[2,16,896]{2,1,0:T(8,128)(2,1)S(1)} %maximum_select_fusion.6), channel_id=1, source_target_pairs={{0,0},{1,32},{2,64},{3,96},{4,128},{5,160},{6,192},{7,224},{8,16},... | collective-permute-start | bytes 172040 | tf_op jit(solution)/shard_map/ppermute | solution.py:345
  79.8 2.0 %collective-permute-done.9.grad_hidden = bf16[2,16,896]{2,1,0:T(8,128)(2,1)S(1)} collective-permute-done((bf16[2,16,896]{2,1,0:T(8,128)(2,1)S(1)}, bf16[2,16,896]{2,1,0:T(8,128)(2,1)S(1)}, u32[]{:S(2)}, u32[]{:S(2)}) %collective-permute-start.9) | collective-permute-done | bytes 57376 | tf_op jit(solution)/shard_map/ppermute | solution.py:345
  82.2 1.8 shard_map.93
  85.2 14.6 %all-to-all-start.3 = ((bf16[16,16,3584]{2,1,0:T(8,128)(2,1)}), bf16[16,16,3584]{2,1,0:T(8,128)(2,1)}, u32[]{:S(2)}, u32[]{:S(2)}) async-start(bf16[16,16,3584]{2,1,0:T(8,128)(2,1)} %copy-done.2), calls=%async_computation.3 | async-start | bytes 3670016 | tf_op jit(solution)/shard_map/all_to_all | solution.py:32
  102.1 7.3 %collective-permute-done.11 = bf16[1,1,1,2,16,896]{5,4,3,2,1,0:T(8,128)(2,1)S(1)} collective-permute-done((bf16[1,1,1,2,16,896]{5,4,3,2,1,0:T(8,128)(2,1)S(1)}, bf16[1,1,1,2,16,896]{5,4,3,2,1,0:T(8,128)(2,1)S(1)}, u32[]{:S(2)}, u32[]{:S(2)}) %collective-permute-start.11) | collective-permute-done | bytes 57376 | tf_op jit(solution)/shard_map/ppermute | solution.py:51
  109.5 6.9 %collective-permute-done.12 = bf16[2,1,1,2,16,896]{5,4,3,2,1,0:T(8,128)(2,1)S(1)} collective-permute-done((bf16[2,1,1,2,16,896]{5,4,3,2,1,0:T(8,128)(2,1)S(1)}, bf16[2,1,1,2,16,896]{5,4,3,2,1,0:T(8,128)(2,1)S(1)}, u32[]{:S(2)}, u32[]{:S(2)}) %collective-permute-start.12) | collective-permute-done | bytes 114720 | tf_op jit(solution)/shard_map/ppermute | solution.py:51
  116.5 6.4 %collective-permute-done.13 = bf16[2,2,1,2,16,896]{5,4,3,2,1,0:T(8,128)(2,1)S(1)} collective-permute-done((bf16[2,2,1,2,16,896]{5,4,3,2,1,0:T(8,128)(2,1)S(1)}, bf16[2,2,1,2,16,896]{5,4,3,2,1,0:T(8,128)(2,1)S(1)}, u32[]{:S(2)}, u32[]{:S(2)}) %collective-permute-start.13) | collective-permute-done | bytes 229408 | tf_op jit(solution)/shard_map/ppermute | solution.py:51
  123.8 2.1 %all-to-all-done.3 = bf16[16,16,3584]{2,1,0:T(8,128)(2,1)} async-done(((bf16[16,16,3584]{2,1,0:T(8,128)(2,1)}), bf16[16,16,3584]{2,1,0:T(8,128)(2,1)}, u32[]{:S(2)}, u32[]{:S(2)}) %all-to-all-start.3) | async-done | bytes 1835040 | tf_op jit(solution)/shard_map/all_to_all | solution.py:32
  125.9 4.9 %all-to-all-start.4 = ((bf16[16,16,896]{2,1,0:T(8,128)(2,1)}), bf16[16,16,896]{2,1,0:T(8,128)(2,1)S(1)}, u32[]{:S(2)}, u32[]{:S(2)}) async-start(bf16[16,16,896]{2,1,0:T(8,128)(2,1)} %bitcast.73), calls=%async_computation.4 | async-start | bytes 917504 | tf_op jit(solution)/shard_map/all_to_all | solution.py:32
  130.8 3.1 %shard_map.94.tokens = bf16[256,512]{1,0:T(8,128)(2,1)S(1)} custom-call(s32[1]{0:T(128)} %bitcast.core, bf16[256,3584]{1,0:T(8,128)(2,1)} %bitcast.22.piece, bf16[256,3584]{1,0:T(8,128)(2,1)S(1)} %copy-done, bf16[256,1792]{1,0:T(8,128)(2,1)} %collective-permute-done.4.gate_other, bf16[256,3584]{1,0:T(8,128)(2,1)} %up_mine.3, ...), custom_call_target="tpu_custom_call" | custom-call | flops 939524096 | bytes 7340032 | tf_op jit(solution)/shard_map/pallas_call | solution.py:92
  134.6 5.7 %all-to-all-done.4 = bf16[16,16,896]{2,1,0:T(8,128)(2,1)S(1)} async-done(((bf16[16,16,896]{2,1,0:T(8,128)(2,1)}), bf16[16,16,896]{2,1,0:T(8,128)(2,1)S(1)}, u32[]{:S(2)}, u32[]{:S(2)}) %all-to-all-start.4) | async-done | bytes 458784 | tf_op jit(solution)/shard_map/all_to_all | solution.py:32
  144.4 5.8 %all-to-all-start.5 = ((bf16[32,8,1536]{2,1,0:T(8,128)(2,1)}), bf16[32,8,1536]{2,1,0:T(8,128)(2,1)S(1)}, u32[]{:S(2)}, u32[]{:S(2)}) async-start(bf16[32,8,1536]{2,1,0:T(8,128)(2,1)} %bitcast.33), calls=%async_computation.5 | async-start | bytes 1572864 | tf_op jit(solution)/shard_map/all_to_all | solution.py:32
  150.1 3.8 %shard_map.96 = (bf16[256,3584]{1,0:T(8,128)(2,1)}, bf16[256,3584]{1,0:T(8,128)(2,1)}, bf16[256,1792]{1,0:T(8,128)(2,1)S(1)}, bf16[256,1792]{1,0:T(8,128)(2,1)}) custom-call(s32[1]{0:T(128)} %bitcast.core, bf16[256,512]{1,0:T(8,128)(2,1)S(1)} %bitcast.68, bf16[256,3584]{1,0:T(8,128)(2,1)} %bitcast.22.piece), custom_call_target="tpu_custom_call" | custom-call | flops 939524096 | bytes 2097152 | tf_op jit(solution)/shard_map/pallas_call | solution.py:92
  154.3 1.9 %convolution_convert_fusion = bf16[896,1024]{1,0:T(8,128)(2,1)} fusion(bf16[256,896]{1,0:T(8,128)(2,1)S(1)} %bitcast.66, bf16[256,1024]{1,0:T(8,128)(2,1)S(1)} %bitcast.72), kind=kOutput, calls=%fused_computation | convolution fusion | flops 470679552 | bytes 2818048 | tf_op jit(solution)/shard_map/dot_general | solution.py:24
  156.2 8.3 %all-to-all-done.5 = bf16[32,8,1536]{2,1,0:T(8,128)(2,1)S(1)} async-done(((bf16[32,8,1536]{2,1,0:T(8,128)(2,1)}), bf16[32,8,1536]{2,1,0:T(8,128)(2,1)S(1)}, u32[]{:S(2)}, u32[]{:S(2)}) %all-to-all-start.5) | async-done | bytes 786464 | tf_op jit(solution)/shard_map/all_to_all | solution.py:32
  165.9 1.7 bitcast_reduce_fusion
  167.6 3.4 %all-to-all-start.6 = ((bf16[8,8,1024]{2,1,0:T(8,128)(2,1)}), bf16[8,8,1024]{2,1,0:T(8,128)(2,1)S(1)}, u32[]{:S(2)}, u32[]{:S(2)}) async-start(bf16[8,8,1024]{2,1,0:T(8,128)(2,1)} %bitcast.37), calls=%async_computation.6 | async-start | bytes 262144 | tf_op jit(solution)/shard_map/all_to_all | solution.py:32
  171.0 1.7 slice_reduce_fusion
  174.3 5.3 %all-to-all-done.6 = bf16[8,8,1024]{2,1,0:T(8,128)(2,1)S(1)} async-done(((bf16[8,8,1024]{2,1,0:T(8,128)(2,1)}), bf16[8,8,1024]{2,1,0:T(8,128)(2,1)S(1)}, u32[]{:S(2)}, u32[]{:S(2)}) %all-to-all-start.6) | async-done | bytes 131104 | tf_op jit(solution)/shard_map/all_to_all | solution.py:32
  (70 shorter events, 25.8 us)
Async XLA Ops:
  0.6 21.8 %copy-start.6 = (bf16[256,3584]{1,0:T(8,128)(2,1)S(1)}, bf16[256,3584]{1,0:T(8,128)(2,1)}, u32[]{:S(2)}) copy-start(bf16[256,3584]{1,0:T(8,128)(2,1)} %up_mine.3) | copy-start | bytes 5505028
  0.6 17.5 %collective-permute-start = (bf16[1,1,1,8,1024]{4,3,2,1,0:T(8,128)(2,1)}, bf16[1,1,1,8,1024]{4,3,2,1,0:T(8,128)(2,1)S(1)}, u32[]{:S(2)}, u32[]{:S(2)}) collective-permute-start(bf16[1,1,1,8,1024]{4,3,2,1,0:T(8,128)(2,1)} %bitcast.81), channel_id=1, source_target_pairs={{0,4},{1,5},{2,6},{3,7},{4,0},{5,1},{6,2},{7,3},{8,12},{9,13},{10,... | collective-permute-start | bytes 49160 | tf_op jit(solution)/shard_map/ppermute | solution.py:51
  10.0 19.6 %all-to-all-start = ((bf16[32,8,1024]{2,1,0:T(8,128)(2,1)}), bf16[32,8,1024]{2,1,0:T(8,128)(2,1)S(1)}, u32[]{:S(2)}, u32[]{:S(2)}) async-start(bf16[32,8,1024]{2,1,0:T(8,128)(2,1)} %broadcast_in_dim.20), calls=%async_computation | async-start | bytes 1048576 | tf_op jit(solution)/shard_map/all_to_all | solution.py:32
  19.0 4.9 %copy-start.10 = (bf16[8,1024]{1,0:T(8,128)(2,1)S(1)}, bf16[8,1024]{1,0:T(8,128)(2,1)}, u32[]{:S(2)}) copy-start(bf16[8,1024]{1,0:T(8,128)(2,1)} %param.5) | copy-start | bytes 49156
  19.0 5.0 %collective-permute-start.1 = (bf16[2,1,1,8,1024]{4,3,2,1,0:T(8,128)(2,1)S(1)}, bf16[2,1,1,8,1024]{4,3,2,1,0:T(8,128)(2,1)S(1)}, u32[]{:S(2)}, u32[]{:S(2)}) collective-permute-start(bf16[2,1,1,8,1024]{4,3,2,1,0:T(8,128)(2,1)S(1)} %maximum_select_fusion.10), channel_id=1, source_target_pairs={{0,2},{1,3},{2,0},{3,1},{4,6},{5,7},{6,4},{7,5},{8,10},{9,11},{10,... | collective-permute-start | bytes 98312 | tf_op jit(solution)/shard_map/ppermute | solution.py:51
  23.4 23.0 %collective-permute-start.5 = (bf16[256,1792]{1,0:T(8,128)(2,1)}, bf16[256,1792]{1,0:T(8,128)(2,1)S(1)}, u32[]{:S(2)}, u32[]{:S(2)}) collective-permute-start(bf16[256,1792]{1,0:T(8,128)(2,1)} %constant_dynamic-slice_fusion.2), channel_id=1, source_target_pairs={{0,8},{8,0},{1,9},{9,1},{2,10},{10,2},{3,11},{11,3},{4,12},{12,4},... | collective-permute-start | bytes 2752520 | tf_op jit(solution)/shard_map/ppermute | solution.py:325
  23.9 22.5 %collective-permute-start.4 = (bf16[256,1792]{1,0:T(8,128)(2,1)}, bf16[256,1792]{1,0:T(8,128)(2,1)}, u32[]{:S(2)}, u32[]{:S(2)}) collective-permute-start(bf16[256,1792]{1,0:T(8,128)(2,1)} %constant_dynamic-slice_fusion.3), channel_id=1, source_target_pairs={{0,8},{8,0},{1,9},{9,1},{2,10},{10,2},{3,11},{11,3},{4,12},{12,4},... | collective-permute-start | bytes 2752520 | tf_op jit(solution)/shard_map/ppermute | solution.py:325
  23.9 3.5 %collective-permute-start.2 = (bf16[2,2,1,8,1024]{4,3,2,1,0:T(8,128)(2,1)S(1)}, bf16[2,2,1,8,1024]{4,3,2,1,0:T(8,128)(2,1)S(1)}, u32[]{:S(2)}, u32[]{:S(2)}) collective-permute-start(bf16[2,2,1,8,1024]{4,3,2,1,0:T(8,128)(2,1)S(1)} %maximum_select_fusion.5), channel_id=1, source_target_pairs={{0,1},{1,0},{2,3},{3,2},{4,5},{5,4},{6,7},{7,6},{8,9},{9,8},{10,11... | collective-permute-start | bytes 196616 | tf_op jit(solution)/shard_map/ppermute | solution.py:51
  29.6 9.5 %copy-start.8 = (bf16[32,8,1024]{2,1,0:T(8,128)(2,1)}, bf16[32,8,1024]{2,1,0:T(8,128)(2,1)S(1)}, u32[]{:S(2)}) copy-start(bf16[32,8,1024]{2,1,0:T(8,128)(2,1)S(1)} %all-to-all-done) | copy-start | bytes 1572868
  30.4 16.0 %all-to-all-start.1 = ((bf16[32,8,512]{2,1,0:T(8,128)(2,1)}), bf16[32,8,512]{2,1,0:T(8,128)(2,1)S(1)}, u32[]{:S(2)}, u32[]{:S(2)}) async-start(bf16[32,8,512]{2,1,0:T(8,128)(2,1)} %bitcast.8), calls=%async_computation.1 | async-start | bytes 524288 | tf_op jit(solution)/shard_map/all_to_all | solution.py:32
  36.8 9.7 %copy-start = (bf16[256,3584]{1,0:T(8,128)(2,1)S(1)}, bf16[256,3584]{1,0:T(8,128)(2,1)}, u32[]{:S(2)}) copy-start(bf16[256,3584]{1,0:T(8,128)(2,1)} %gate_mine.3) | copy-start | bytes 5505028
  39.3 7.2 %collective-permute-start.3 = (bf16[2,2,32,896]{3,2,0,1:T(8,128)(2,1)S(1)}, bf16[2,2,32,896]{3,2,0,1:T(8,128)(2,1)}, u32[]{:S(2)}, u32[]{:S(2)}) collective-permute-start(bf16[2,2,32,896]{3,2,0,1:T(8,128)(2,1)S(1)} %bitcast.77), channel_id=1, source_target_pairs={{0,1},{1,0},{2,3},{3,2},{4,5},{5,4},{6,7},{7,6},{8,9},{9,8},{10,11... | collective-permute-start | bytes 688136 | tf_op jit(solution)/shard_map/ppermute | solution.py:69
  49.3 1.2 copy-start.1
  50.5 31.7 %all-to-all-start.2 = ((bf16[16,16,3584]{2,1,0:T(8,128)(2,1)}), bf16[16,16,3584]{2,1,0:T(8,128)(2,1)}, u32[]{:S(2)}, u32[]{:S(2)}) async-start(bf16[16,16,3584]{2,1,0:T(8,128)(2,1)} %bitcast.64), calls=%async_computation.2 | async-start | bytes 3670016 | tf_op jit(solution)/shard_map/all_to_all | solution.py:32
  58.1 7.9 %collective-permute-start.6 = (bf16[2,32,896]{2,1,0:T(8,128)(2,1)S(1)}, bf16[2,32,896]{2,1,0:T(8,128)(2,1)S(1)}, u32[]{:S(2)}, u32[]{:S(2)}) collective-permute-start(bf16[2,32,896]{2,1,0:T(8,128)(2,1)S(1)} %dynamic-slice_bitcast_fusion), channel_id=1, source_target_pairs={{0,2},{1,3},{2,0},{3,1},{4,6},{5,7},{6,4},{7,5},{8,10},{9,11},{10,... | collective-permute-start | bytes 344072 | tf_op jit(solution)/shard_map/ppermute | solution.py:69
  66.1 7.1 %collective-permute-start.7 = (bf16[32,896]{1,0:T(8,128)(2,1)S(1)}, bf16[32,896]{1,0:T(8,128)(2,1)S(1)}, u32[]{:S(2)}, u32[]{:S(2)}) collective-permute-start(bf16[32,896]{1,0:T(8,128)(2,1)S(1)} %dynamic-slice_bitcast_fusion.1), channel_id=1, source_target_pairs={{0,4},{1,5},{2,6},{3,7},{4,0},{5,1},{6,2},{7,3},{8,12},{9,13},{10,... | collective-permute-start | bytes 172040 | tf_op jit(solution)/shard_map/ppermute | solution.py:69
  73.3 3.0 %collective-permute-start.8 = (bf16[16,896]{1,0:T(8,128)(2,1)S(1)}, bf16[16,896]{1,0:T(8,128)(2,1)S(1)}, u32[]{:S(2)}, u32[]{:S(2)}) collective-permute-start(bf16[16,896]{1,0:T(8,128)(2,1)S(1)} %get-tuple-element.58), channel_id=1, source_target_pairs={{0,8},{8,0},{1,9},{9,1},{2,10},{10,2},{3,11},{11,3},{4,12},{12,4},... | collective-permute-start | bytes 86024 | tf_op jit(solution)/shard_map/ppermute | solution.py:344
  76.4 5.5 %collective-permute-start.9 = (bf16[2,16,896]{2,1,0:T(8,128)(2,1)S(1)}, bf16[2,16,896]{2,1,0:T(8,128)(2,1)S(1)}, u32[]{:S(2)}, u32[]{:S(2)}) collective-permute-start(bf16[2,16,896]{2,1,0:T(8,128)(2,1)S(1)} %maximum_select_fusion.6), channel_id=1, source_target_pairs={{0,0},{1,32},{2,64},{3,96},{4,128},{5,160},{6,192},{7,224},{8,16},... | collective-permute-start | bytes 172040 | tf_op jit(solution)/shard_map/ppermute | solution.py:345
  84.0 1.2 copy-start.2
  85.2 40.7 %all-to-all-start.3 = ((bf16[16,16,3584]{2,1,0:T(8,128)(2,1)}), bf16[16,16,3584]{2,1,0:T(8,128)(2,1)}, u32[]{:S(2)}, u32[]{:S(2)}) async-start(bf16[16,16,3584]{2,1,0:T(8,128)(2,1)} %copy-done.2), calls=%async_computation.3 | async-start | bytes 3670016 | tf_op jit(solution)/shard_map/all_to_all | solution.py:32
  99.8 2.1 %collective-permute-start.10 = (bf16[16,896]{1,0:T(8,128)(2,1)S(1)}, bf16[16,896]{1,0:T(8,128)(2,1)S(1)}, u32[]{:S(2)}, u32[]{:S(2)}) collective-permute-start(bf16[16,896]{1,0:T(8,128)(2,1)S(1)} %get-tuple-element.38), channel_id=1, source_target_pairs={{0,8},{8,0},{1,9},{9,1},{2,10},{10,2},{3,11},{11,3},{4,12},{12,4},... | collective-permute-start | bytes 86024 | tf_op jit(solution)/shard_map/ppermute | solution.py:352
  101.9 7.4 %collective-permute-start.11 = (bf16[1,1,1,2,16,896]{5,4,3,2,1,0:T(8,128)(2,1)S(1)}, bf16[1,1,1,2,16,896]{5,4,3,2,1,0:T(8,128)(2,1)S(1)}, u32[]{:S(2)}, u32[]{:S(2)}) collective-permute-start(bf16[1,1,1,2,16,896]{5,4,3,2,1,0:T(8,128)(2,1)S(1)} %maximum_select_fusion.8), channel_id=1, source_target_pairs={{0,4},{1,5},{2,6},{3,7},{4,0},{5,1},{6,2},{7,3},{8,12},{9,13},{10,... | collective-permute-start | bytes 172040 | tf_op jit(solution)/shard_map/ppermute | solution.py:51
  109.4 7.0 %collective-permute-start.12 = (bf16[2,1,1,2,16,896]{5,4,3,2,1,0:T(8,128)(2,1)S(1)}, bf16[2,1,1,2,16,896]{5,4,3,2,1,0:T(8,128)(2,1)S(1)}, u32[]{:S(2)}, u32[]{:S(2)}) collective-permute-start(bf16[2,1,1,2,16,896]{5,4,3,2,1,0:T(8,128)(2,1)S(1)} %maximum_select_fusion.4), channel_id=1, source_target_pairs={{0,2},{1,3},{2,0},{3,1},{4,6},{5,7},{6,4},{7,5},{8,10},{9,11},{10,... | collective-permute-start | bytes 344072 | tf_op jit(solution)/shard_map/ppermute | solution.py:51
  116.4 6.5 %collective-permute-start.13 = (bf16[2,2,1,2,16,896]{5,4,3,2,1,0:T(8,128)(2,1)S(1)}, bf16[2,2,1,2,16,896]{5,4,3,2,1,0:T(8,128)(2,1)S(1)}, u32[]{:S(2)}, u32[]{:S(2)}) collective-permute-start(bf16[2,2,1,2,16,896]{5,4,3,2,1,0:T(8,128)(2,1)S(1)} %maximum_select_fusion.1), channel_id=1, source_target_pairs={{0,1},{1,0},{2,3},{3,2},{4,5},{5,4},{6,7},{7,6},{8,9},{9,8},{10,11... | collective-permute-start | bytes 688136 | tf_op jit(solution)/shard_map/ppermute | solution.py:51
  125.9 14.4 %all-to-all-start.4 = ((bf16[16,16,896]{2,1,0:T(8,128)(2,1)}), bf16[16,16,896]{2,1,0:T(8,128)(2,1)S(1)}, u32[]{:S(2)}, u32[]{:S(2)}) async-start(bf16[16,16,896]{2,1,0:T(8,128)(2,1)} %bitcast.73), calls=%async_computation.4 | async-start | bytes 917504 | tf_op jit(solution)/shard_map/all_to_all | solution.py:32
  140.3 1.5 copy-start.3
  141.8 0.9 copy-start.5
  144.4 20.1 %all-to-all-start.5 = ((bf16[32,8,1536]{2,1,0:T(8,128)(2,1)}), bf16[32,8,1536]{2,1,0:T(8,128)(2,1)S(1)}, u32[]{:S(2)}, u32[]{:S(2)}) async-start(bf16[32,8,1536]{2,1,0:T(8,128)(2,1)} %bitcast.33), calls=%async_computation.5 | async-start | bytes 1572864 | tf_op jit(solution)/shard_map/all_to_all | solution.py:32
  150.1 4.2 %copy-start.9 = (bf16[32,8,1024]{2,1,0:T(8,128)(2,1)S(1)}, bf16[32,8,1024]{2,1,0:T(8,128)(2,1)}, u32[]{:S(2)}) copy-start(bf16[32,8,1024]{2,1,0:T(8,128)(2,1)} %copy-done.8) | copy-start | bytes 1572868
  153.9 18.8 %collective-permute-start.15 = (bf16[256,1792]{1,0:T(8,128)(2,1)}, bf16[256,1792]{1,0:T(8,128)(2,1)S(1)}, u32[]{:S(2)}, u32[]{:S(2)}) collective-permute-start(bf16[256,1792]{1,0:T(8,128)(2,1)} %get-tuple-element.46), channel_id=1, source_target_pairs={{0,8},{8,0},{1,9},{9,1},{2,10},{10,2},{3,11},{11,3},{4,12},{12,4},... | collective-permute-start | bytes 2752520 | tf_op jit(solution)/shard_map/ppermute | solution.py:374
  165.4 7.4 %collective-permute-start.14 = (bf16[256,1792]{1,0:T(8,128)(2,1)S(1)}, bf16[256,1792]{1,0:T(8,128)(2,1)S(1)}, u32[]{:S(2)}, u32[]{:S(2)}) collective-permute-start(bf16[256,1792]{1,0:T(8,128)(2,1)S(1)} %get-tuple-element.45), channel_id=1, source_target_pairs={{0,8},{8,0},{1,9},{9,1},{2,10},{10,2},{3,11},{11,3},{4,12},{12,4},... | collective-permute-start | bytes 2752520 | tf_op jit(solution)/shard_map/ppermute | solution.py:373
  167.6 11.9 %all-to-all-start.6 = ((bf16[8,8,1024]{2,1,0:T(8,128)(2,1)}), bf16[8,8,1024]{2,1,0:T(8,128)(2,1)S(1)}, u32[]{:S(2)}, u32[]{:S(2)}) async-start(bf16[8,8,1024]{2,1,0:T(8,128)(2,1)} %bitcast.37), calls=%async_computation.6 | async-start | bytes 262144 | tf_op jit(solution)/shard_map/all_to_all | solution.py:32
  (2 other events, 1.6 us)

commit v3 on v2

--- a/solution.py
+++ b/solution.py
@@ -59,18 +59,40 @@
     return (share, *late) if late else share
 
 
-def scatter_columns(blocks, after=None):
+def near_order(z, near):
+    near = [jnp.where(z % 2 == 0, near[at], near[at ^ 1]) for at in range(4)]
+    return [jnp.where(z // 2 % 2 == 0, near[at], near[at ^ 2]) for at in range(4)]
+
+
+def gather_hidden(block):
     z = lax.axis_index("z")
-    share = blocks.reshape((2, 2, 2) + blocks.shape[1:])
-    for axis, distance in ((2, 1), (1, 2), (0, 4)):
-        bit = (z // distance) % 2
-        keep = lax.dynamic_index_in_dim(share, bit, axis, keepdims=False)
-        send = lax.dynamic_index_in_dim(share, 1 - bit, axis, keepdims=False)
-        got = lax.ppermute(send, "z", pairs(distance))
-        if axis == 2 and after is not None:
-            got, after = lax.optimization_barrier((got, after))
-        share = (keep.astype(F32) + got.astype(F32)).astype(BF16)
-    return share if after is None else (share, after)
+    got = lax.ppermute(block, "z", pairs(4))
+    low = z < 4
+    share = jnp.where(low, jnp.stack([block, got]), jnp.stack([got, block]))
+    near = [share] + [lax.ppermute(share, "z", pairs(distance)) for distance in (1, 2, 3)]
+    return jnp.stack(near_order(z, near), 1).reshape((Z,) + block.shape)
+
+
+def near_exchange(blocks):
+    z = lax.axis_index("z")
+    share = blocks.reshape((2, 4) + blocks.shape[1:])
+    near = [
+        lax.dynamic_index_in_dim(share, (z % 4) ^ distance, 1, keepdims=False)
+        for distance in range(4)
+    ]
+    return near[0], [lax.ppermute(near[d], "z", pairs(d)) for d in (1, 2, 3)]
+
+
+def far_exchange(own, got):
+    z = lax.axis_index("z")
+    share = own.astype(F32)
+    for term in got:
+        share = share + term.astype(F32)
+    share = share.astype(BF16)
+    keep = lax.dynamic_index_in_dim(share, z // 4, 0, keepdims=False)
+    send = lax.dynamic_index_in_dim(share, 1 - z // 4, 0, keepdims=False)
+    far = lax.ppermute(send, "z", pairs(4))
+    return (keep.astype(F32) + far.astype(F32)).astype(BF16)
 
 
 def owner_route():
@@ -85,6 +107,10 @@
 
 
 TO_OWNER = owner_route()
+
+
+def in_hbm(array):
+    return pltpu.with_memory_space_constraint(array, pltpu.HBM)
 
 
 def call(body, core, arrays, in_specs, out_shapes, out_specs, steps, scratch=(), aliases=None, cost=0):
@@ -139,9 +165,9 @@
     return call(
         body,
         core,
-        (arrivals, gate_weight, gate_got, up_weight, up_got),
+        (arrivals, in_hbm(gate_weight), gate_got, in_hbm(up_weight), up_got),
         [pl.BlockSpec((rows, 2 * depth), lambda step, core: (0, 0)), weight, got, weight, got],
-        jax.ShapeDtypeStruct((rows, 4 * quarter), BF16),
+        pltpu.HBM((rows, 4 * quarter), BF16),
         pl.BlockSpec((rows, 2 * quarter), in_turn),
         2,
         cost=16 * rows * depth * quarter,
@@ -184,7 +210,7 @@
         core,
         (terms, grad_hidden),
         [half, pl.BlockSpec((1, tall, quarter), lambda step, core: (step, 0, 0))],
-        [jax.ShapeDtypeStruct(terms.shape, BF16)]
+        [pltpu.HBM(terms.shape, BF16)]
         + [jax.ShapeDtypeStruct((tall, quarter), BF16)] * 2,
         [half, flat, flat],
         2,
@@ -220,7 +246,7 @@
     return call(
         body,
         core,
-        (pieces, gate_weight, gate_got, up_weight, up_got),
+        (pieces, in_hbm(gate_weight), gate_got, in_hbm(up_weight), up_got),
         [
             pl.BlockSpec((rows, half), in_turn),
             weight,
@@ -236,29 +262,6 @@
     )
 
 
-def output_product(core, hidden_panel, down_weight, token_part):
-    rows, quarter = hidden_panel.shape
-    width, features = down_weight.shape[1], token_part.shape[1]
-
-    def body(core, hidden, down, tokens, out):
-        out[:, :width] = times(hidden[...], down[...]).astype(BF16)
-        out[:, width:] = tokens[...]
-
-    def whole(*shape):
-        return pl.BlockSpec(shape, lambda step, core: (0, 0))
-
-    return call(
-        body,
-        core,
-        (hidden_panel, down_weight, token_part),
-        [whole(rows, quarter), whole(quarter, width), whole(rows, features)],
-        jax.ShapeDtypeStruct((rows, width + features), BF16),
-        whole(rows, width + features),
-        1,
-        cost=2 * rows * quarter * width,
-    )
-
-
 def weight_grads(core, arrivals, pieces, depth):
     rows = arrivals.shape[0]
     wide = pieces.shape[1] // 2
@@ -337,44 +340,46 @@
     arrivals = exchange(parts, ROW).reshape(ROWS * few, features)
 
     hidden_part = rows_times(cotangent, down_weight).astype(BF16)
-    hidden_sum, arrivals = scatter_columns(hidden_part.reshape(Z, -1, quarter), arrivals)
+    gate_got, up_got = swapped_half(gate_late), swapped_half(up_late)
+    own, got = near_exchange(hidden_part.reshape(Z, -1, quarter))
+    got[0], arrivals = lax.optimization_barrier((got[0], arrivals))
+    sent = forward_products(core, arrivals, gate_weight, gate_got, up_weight, up_got)
+    got[1], sent = lax.optimization_barrier((got[1], sent))
+    hidden_sum = far_exchange(own, got)
     hidden_sum = hidden_sum.reshape(2, -1, quarter)
     hidden_keep = lax.dynamic_index_in_dim(hidden_sum, at_core, 0, keepdims=False)
     hidden_send = lax.dynamic_index_in_dim(hidden_sum, 1 - at_core, 0, keepdims=False)
     hidden_sum = paired(at_core, hidden_keep, lax.ppermute(hidden_send, "core", SWAP))
     grad_hidden = lax.ppermute(hidden_sum, EVERY, TO_OWNER)
 
-    gate_got, up_got = swapped_half(gate_late), swapped_half(up_late)
-    sent = forward_products(core, arrivals, gate_weight, gate_got, up_weight, up_got)
-
     terms = exchange(sent.reshape(CHIPS, -1, units), PLANE)
     copies, hidden_keep, hidden_send = activations(core, terms, grad_hidden)
     hidden = paired(at_core, hidden_keep, lax.ppermute(hidden_send, "core", SWAP))
-    hidden = gather_columns(hidden).reshape(CHIPS, -1, quarter)
+    hidden = gather_hidden(hidden).reshape(CHIPS, -1, quarter)
     pieces = exchange(copies, PLANE).reshape(-1, units)
-    pieces, hidden = lax.optimization_barrier((pieces, hidden))
+    parts = token_products(core, pieces, gate_weight, gate_got, up_weight, up_got)
+    parts = exchange(parts.reshape(ROWS, few, features), ROW)
+    gate_grad, up_grad, gate_send, up_send = weight_grads(core, arrivals, pieces, depth)
+    parts, hidden, gate_send = lax.optimization_barrier((parts, hidden, gate_send))
     hidden_panel = exchange(hidden, PLANE).reshape(-1, quarter)
 
-    token_part = token_products(core, pieces, gate_weight, gate_got, up_weight, up_got)
-    parts = output_product(core, hidden_panel, down_weight, token_part)
-    parts = exchange(parts.reshape(ROWS, few, width + features), ROW)
-
-    gate_grad, up_grad, gate_send, up_send = weight_grads(core, arrivals, pieces, depth)
-    grad_down_weight = columns_times(hidden_panel, cotangent).astype(BF16)
-    parts, gate_send, grad_down_weight = lax.optimization_barrier(
-        (parts, gate_send, grad_down_weight)
-    )
-    output = total(parts[:, :, :width]).astype(BF16)
-    terms = parts[:, :, width:].reshape(CHIPS, CORES, few, features).astype(F32)
+    terms = parts.reshape(CHIPS, CORES, few, features).astype(F32)
     terms = jnp.sum(terms, axis=1).astype(BF16).reshape(Z, 2, few, features)
     terms = terms.transpose(0, 2, 1, 3).reshape(Z, few, width)
-    terms = exchange(terms, "z")
+    own, got = near_exchange(terms)
+
+    output = times(hidden_panel, down_weight).astype(BF16).reshape(ROWS, few, width)
+    output = exchange(output, ROW)
+    grad_tokens = far_exchange(own, got)
 
     gate_back = lax.ppermute(gate_send, "core", SWAP)
     up_back = lax.ppermute(up_send, "core", SWAP)
     gate_grad, up_grad = fill(core, gate_grad, up_grad, gate_back, up_back)
-    terms, gate_grad, up_grad = lax.optimization_barrier((terms, gate_grad, up_grad))
-    grad_tokens = total(terms).astype(BF16)
+    grad_down_weight = columns_times(hidden_panel, cotangent).astype(BF16)
+    output, grad_tokens, gate_grad, up_grad, grad_down_weight = lax.optimization_barrier(
+        (output, grad_tokens, gate_grad, up_grad, grad_down_weight)
+    )
+    output = total(output).astype(BF16)
     return output, grad_tokens, gate_grad, up_grad, grad_down_weight
 
 

time: 181 us -> 177 us (0.978)
  starting transfers between devices: 70.4 us -> 85.4 us
  waiting for transfers between devices: 71 us -> 56 us
  local copies, waits for them, and re-layouts: 12.1 us -> 8.26 us
  other arithmetic: 6.87 us -> 4.35 us
    ppermute x6 -> x3, waiting for transfers between devices: 23.3 us -> 2.68 us  [gather_columns(): got = lax.ppermute(share, 'z', pairs(distance))]
    ppermute x3 -> x12, starting transfers between devices: 2.18 us -> 12.9 us  [the longest x6 7.33 us: near_exchange(): return (near[0], [lax.ppermute(near[d], 'z', pairs(d)) for d in (1, 2, 3)])]
    unnamed x22 -> x16, local copies, waits for them, and re-layouts: 6.5 us -> 1.9 us
    all_to_all x7, waiting for transfers between devices: 23.9 us -> 27 us  [exchange(): return lax.all_to_all(blocks, axis, split_axis=0, concat_axis=0, tiled=True)]
    ppermute x3 -> x12, waiting for transfers between devices: 20 us -> 22.7 us  [the longest x6 8.52 us: near_exchange(): return (near[0], [lax.ppermute(near[d], 'z', pairs(d)) for d in (1, 2, 3)])]
    all_to_all x7, starting transfers between devices: 49.6 us -> 51.7 us  [exchange(): return lax.all_to_all(blocks, axis, split_axis=0, concat_axis=0, tiled=True)]
    pallas_call x6 -> x5, Pallas kernels: 14.6 us -> 16.1 us  [call(): pl.pallas_call(body, grid_spec=pltpu.PrefetchScalarGridSpec(num_scalar_pr...]
    ppermute x6 -> x3, starting transfers between devices: 10.2 us -> 9.92 us  [gather_columns(): got = lax.ppermute(share, 'z', pairs(distance))]
  transfers between devices with their start and end apart: 23 -> 29, of which waited for: 16 -> 15; matrix products, arithmetic and copies ran while one was open for 9% -> 9% of each run, Pallas kernels for 5% -> 8%
where the time goes in v3:
time: 177 us; the launch traced here: 176 us
  starting transfers between devices  85.4 us (48%)
  waiting for transfers between devices  56 us (32%)
  Pallas kernels  16.1 us (9%)
  local copies, waits for them, and re-layouts  8.26 us (5%)
  matrix products  5.32 us (3%)
  other arithmetic  4.35 us (2%)
    all_to_all x7, starting transfers between devices, exchange(): return lax.all_to_all(blocks, axis, split_axis=0, concat_axis=0, tiled=True)  51.7 us
    all_to_all x7, waiting for transfers between devices, exchange(): return lax.all_to_all(blocks, axis, split_axis=0, concat_axis=0, tiled=True)  27 us
    pallas_call x5, Pallas kernels, call(): pl.pallas_call(body, grid_spec=pltpu.PrefetchScalarGridSpec(num_scalar_pr...  16.1 us
    ppermute x3, starting transfers between devices, gather_columns(): got = lax.ppermute(share, 'z', pairs(distance))  9.92 us
    ppermute x6, waiting for transfers between devices, near_exchange(): return (near[0], [lax.ppermute(near[d], 'z', pairs(d)) for d in (1, 2, 3)])  8.52 us
    ppermute x6, starting transfers between devices, near_exchange(): return (near[0], [lax.ppermute(near[d], 'z', pairs(d)) for d in (1, 2, 3)])  7.33 us
    ppermute x1, waiting for transfers between devices, gather_hidden(): got = lax.ppermute(block, 'z', pairs(4))  7.3 us
    ppermute x2, waiting for transfers between devices, far_exchange(): far = lax.ppermute(send, 'z', pairs(4))  6.86 us
  transfers between devices with their start and end apart: 29, of which 15 were waited for; matrix products, arithmetic and copies ran while one was open for 9% of the time, Pallas kernels for 8%

profile of v3, /device:TPU:1, one launch (start us, length us, event | category | flops | bytes accessed | tf_op | source)
XLA Modules:
  0.0 176.4 jit_solution(9188599791609366064)
XLA Ops:
  0.6 7.8 %collective-permute-start = (bf16[1,1,1,8,1024]{4,3,2,1,0:T(8,128)(2,1)}, bf16[1,1,1,8,1024]{4,3,2,1,0:T(8,128)(2,1)S(1)}, u32[]{:S(2)}, u32[]{:S(2)}) collective-permute-start(bf16[1,1,1,8,1024]{4,3,2,1,0:T(8,128)(2,1)} %bitcast.102), channel_id=1, source_target_pairs={{0,4},{1,5},{2,6},{3,7},{4,0},{5,1},{6,2},{7,3},{8,12},{9,13},{10,... | collective-permute-start | bytes 49160 | tf_op jit(solution)/shard_map/ppermute | solution.py:51
  10.0 8.0 %all-to-all-start = ((bf16[32,8,1024]{2,1,0:T(8,128)(2,1)}), bf16[32,8,1024]{2,1,0:T(8,128)(2,1)S(1)}, u32[]{:S(2)}, u32[]{:S(2)}) async-start(bf16[32,8,1024]{2,1,0:T(8,128)(2,1)} %broadcast_in_dim.19), calls=%async_computation | async-start | bytes 1048576 | tf_op jit(solution)/shard_map/all_to_all | solution.py:32
  20.3 2.2 %constant_dynamic-slice_fusion.2 = bf16[256,1792]{1,0:T(8,128)(2,1)} fusion(bf16[256,3584]{1,0:T(8,128)(2,1)} %gate_mine.3, s32[]{:T(128)S(6)} %select_n.253), kind=kLoop, calls=%fused_computation.46 | loop fusion | bytes 1835012 | tf_op jit(solution)/shard_map/dynamic_slice | solution.py:327
  24.9 2.7 %collective-permute-done.2 = bf16[2,2,1,8,1024]{4,3,2,1,0:T(8,128)(2,1)S(1)} collective-permute-done((bf16[2,2,1,8,1024]{4,3,2,1,0:T(8,128)(2,1)S(1)}, bf16[2,2,1,8,1024]{4,3,2,1,0:T(8,128)(2,1)S(1)}, u32[]{:S(2)}, u32[]{:S(2)}) %collective-permute-start.2) | collective-permute-done | bytes 65568 | tf_op jit(solution)/shard_map/ppermute | solution.py:51
  27.6 2.1 %all-to-all-done = bf16[32,8,1024]{2,1,0:T(8,128)(2,1)S(1)} async-done(((bf16[32,8,1024]{2,1,0:T(8,128)(2,1)}), bf16[32,8,1024]{2,1,0:T(8,128)(2,1)S(1)}, u32[]{:S(2)}, u32[]{:S(2)}) %all-to-all-start) | async-done | bytes 524320 | tf_op jit(solution)/shard_map/all_to_all | solution.py:32
  30.4 6.4 %all-to-all-start.1 = ((bf16[32,8,512]{2,1,0:T(8,128)(2,1)}), bf16[32,8,512]{2,1,0:T(8,128)(2,1)S(1)}, u32[]{:S(2)}, u32[]{:S(2)}) async-start(bf16[32,8,512]{2,1,0:T(8,128)(2,1)} %bitcast.91), calls=%async_computation.1 | async-start | bytes 524288 | tf_op jit(solution)/shard_map/all_to_all | solution.py:32
  39.7 3.7 %collective-permute-done.4 = bf16[2,32,896]{2,1,0:T(8,128)(2,1)S(1)} collective-permute-done((bf16[2,32,896]{2,1,0:T(8,128)(2,1)S(1)}, bf16[2,32,896]{2,1,0:T(8,128)(2,1)S(1)}, u32[]{:S(2)}, u32[]{:S(2)}) %collective-permute-start.4) | collective-permute-done | bytes 114720 | tf_op jit(solution)/shard_map/ppermute | solution.py:83
  43.4 2.3 %all-to-all-done.1 = bf16[32,8,512]{2,1,0:T(8,128)(2,1)S(1)} async-done(((bf16[32,8,512]{2,1,0:T(8,128)(2,1)}), bf16[32,8,512]{2,1,0:T(8,128)(2,1)S(1)}, u32[]{:S(2)}, u32[]{:S(2)}) %all-to-all-start.1) | async-done | bytes 262176 | tf_op jit(solution)/shard_map/all_to_all | solution.py:32
  45.8 3.7 %shard_map.92 = bf16[256,3584]{1,0:T(8,128)(2,1)} custom-call(s32[1]{0:T(128)} %bitcast.core, bf16[256,512]{1,0:T(8,128)(2,1)S(1)} %bitcast.82, bf16[256,3584]{1,0:T(8,128)(2,1)} %gate_mine.3, bf16[256,1792]{1,0:T(8,128)(2,1)S(1)} %collective-permute-done.5.gate_other, bf16[256,3584]{1,0:T(8,128)(2,1)} %up_mine.3, ...), custom_call_target="tpu_custom_call" | custom-call | flops 939524096 | bytes 5767168 | tf_op jit(solution)/shard_map/pallas_call | solution.py:118
  49.5 4.4 %all-to-all-start.2 = ((bf16[16,16,3584]{2,1,0:T(8,128)(2,1)}), bf16[16,16,3584]{2,1,0:T(8,128)(2,1)}, u32[]{:S(2)}, u32[]{:S(2)}) async-start(bf16[16,16,3584]{2,1,0:T(8,128)(2,1)} %bitcast.86), calls=%async_computation.2 | async-start | bytes 3670016 | tf_op jit(solution)/shard_map/all_to_all | solution.py:32
  53.9 1.7 collective-permute-start.7
  55.6 3.9 %collective-permute-done.7 = bf16[2,32,896]{2,1,0:T(8,128)(2,1)S(1)} collective-permute-done((bf16[2,32,896]{2,1,0:T(8,128)(2,1)S(1)}, bf16[2,32,896]{2,1,0:T(8,128)(2,1)S(1)}, u32[]{:S(2)}, u32[]{:S(2)}) %collective-permute-start.7) | collective-permute-done | bytes 114720 | tf_op jit(solution)/shard_map/ppermute | solution.py:83
  61.0 6.9 %collective-permute-done.8 = bf16[32,896]{1,0:T(8,128)(2,1)S(1)} collective-permute-done((bf16[32,896]{1,0:T(8,128)(2,1)S(1)}, bf16[32,896]{1,0:T(8,128)(2,1)S(1)}, u32[]{:S(2)}, u32[]{:S(2)}) %collective-permute-start.8) | collective-permute-done | bytes 57376 | tf_op jit(solution)/shard_map/ppermute | solution.py:94
  67.9 3.9 %collective-permute-start.9 = (bf16[16,896]{1,0:T(8,128)(2,1)S(1)}, bf16[16,896]{1,0:T(8,128)(2,1)S(1)}, u32[]{:S(2)}, u32[]{:S(2)}) collective-permute-start(bf16[16,896]{1,0:T(8,128)(2,1)S(1)} %get-tuple-element.68), channel_id=1, source_target_pairs={{0,8},{8,0},{1,9},{9,1},{2,10},{10,2},{3,11},{11,3},{4,12},{12,4},... | collective-permute-start | bytes 86024 | tf_op jit(solution)/shard_map/ppermute | solution.py:352
  72.7 3.7 %collective-permute-start.10 = (bf16[2,16,896]{2,1,0:T(8,128)(2,1)S(1)}, bf16[2,16,896]{2,1,0:T(8,128)(2,1)S(1)}, u32[]{:S(2)}, u32[]{:S(2)}) collective-permute-start(bf16[2,16,896]{2,1,0:T(8,128)(2,1)S(1)} %maximum_select_fusion.3), channel_id=1, source_target_pairs={{0,0},{1,32},{2,64},{3,96},{4,128},{5,160},{6,192},{7,224},{8,16},... | collective-permute-start | bytes 172040 | tf_op jit(solution)/shard_map/ppermute | solution.py:353
  76.4 1.8 %collective-permute-done.10.grad_hidden = bf16[2,16,896]{2,1,0:T(8,128)(2,1)S(1)} collective-permute-done((bf16[2,16,896]{2,1,0:T(8,128)(2,1)S(1)}, bf16[2,16,896]{2,1,0:T(8,128)(2,1)S(1)}, u32[]{:S(2)}, u32[]{:S(2)}) %collective-permute-start.10) | collective-permute-done | bytes 57376 | tf_op jit(solution)/shard_map/ppermute | solution.py:353
  78.3 2.6 %shard_map.93 = (bf16[16,16,3584]{2,1,0:T(8,128)(2,1)}, bf16[16,896]{1,0:T(8,128)(2,1)S(1)}, bf16[16,896]{1,0:T(8,128)(2,1)S(1)}) custom-call(s32[1]{0:T(128)} %bitcast.core, bf16[16,16,3584]{2,1,0:T(8,128)(2,1)} %all-to-all-done.2.terms, bf16[2,16,896]{2,1,0:T(8,128)(2,1)S(1)} %collective-permute-done.10.grad_hidden), custom_call_target="tpu_custom_call" | custom-call | flops 1720320 | bytes 1892352 | tf_op jit(solution)/shard_map/pallas_call | solution.py:118
  80.9 15.1 %all-to-all-start.3 = ((bf16[16,16,3584]{2,1,0:T(8,128)(2,1)}), bf16[16,16,3584]{2,1,0:T(8,128)(2,1)}, u32[]{:S(2)}, u32[]{:S(2)}) async-start(bf16[16,16,3584]{2,1,0:T(8,128)(2,1)} %get-tuple-element.40), calls=%async_computation.3 | async-start | bytes 3670016 | tf_op jit(solution)/shard_map/all_to_all | solution.py:32
  98.2 7.3 %collective-permute-done.12 = bf16[2,16,896]{2,1,0:T(8,128)(2,1)S(1)} collective-permute-done((bf16[2,16,896]{2,1,0:T(8,128)(2,1)S(1)}, bf16[2,16,896]{2,1,0:T(8,128)(2,1)S(1)}, u32[]{:S(2)}, u32[]{:S(2)}) %collective-permute-start.12) | collective-permute-done | bytes 57376 | tf_op jit(solution)/shard_map/ppermute | solution.py:69
  106.1 3.0 %collective-permute-start.15 = (bf16[2,2,16,896]{3,2,1,0:T(8,128)(2,1)S(1)}, bf16[2,2,16,896]{3,2,1,0:T(8,128)(2,1)}, u32[]{:S(2)}, u32[]{:S(2)}) collective-permute-start(bf16[2,2,16,896]{3,2,1,0:T(8,128)(2,1)S(1)} %maximum_select_fusion.1), channel_id=1, source_target_pairs={{0,3},{1,2},{2,1},{3,0},{4,7},{5,6},{6,5},{7,4},{8,11},{9,10},{10,... | collective-permute-start | bytes 344072 | tf_op jit(solution)/shard_map/ppermute | solution.py:72
  109.2 12.9 %all-to-all-done.3 = bf16[16,16,3584]{2,1,0:T(8,128)(2,1)} async-done(((bf16[16,16,3584]{2,1,0:T(8,128)(2,1)}), bf16[16,16,3584]{2,1,0:T(8,128)(2,1)}, u32[]{:S(2)}, u32[]{:S(2)}) %all-to-all-start.3) | async-done | bytes 1835040 | tf_op jit(solution)/shard_map/all_to_all | solution.py:32
  122.1 3.9 %shard_map.94 = bf16[256,512]{1,0:T(8,128)(2,1)} custom-call(s32[1]{0:T(128)} %bitcast.core, bf16[256,3584]{1,0:T(8,128)(2,1)} %bitcast.22.piece, bf16[256,3584]{1,0:T(8,128)(2,1)} %gate_mine.3, bf16[256,1792]{1,0:T(8,128)(2,1)S(1)} %collective-permute-done.5.gate_other, bf16[256,3584]{1,0:T(8,128)(2,1)} %up_mine.3, ...), custom_call_target="tpu_custom_call" | custom-call | flops 939524096 | bytes 7340032 | tf_op jit(solution)/shard_map/pallas_call | solution.py:118
  125.9 6.1 %all-to-all-start.4 = ((bf16[32,8,512]{2,1,0:T(8,128)(2,1)}), bf16[32,8,512]{2,1,0:T(8,128)(2,1)S(1)}, u32[]{:S(2)}, u32[]{:S(2)}) async-start(bf16[32,8,512]{2,1,0:T(8,128)(2,1)} %bitcast.23), calls=%async_computation.4 | async-start | bytes 524288 | tf_op jit(solution)/shard_map/all_to_all | solution.py:32
  134.0 3.6 %shard_map.95 = (bf16[256,3584]{1,0:T(8,128)(2,1)}, bf16[256,3584]{1,0:T(8,128)(2,1)}, bf16[256,1792]{1,0:T(8,128)(2,1)S(1)}, bf16[256,1792]{1,0:T(8,128)(2,1)S(1)}) custom-call(s32[1]{0:T(128)} %bitcast.core, bf16[256,512]{1,0:T(8,128)(2,1)S(1)} %bitcast.83, bf16[256,3584]{1,0:T(8,128)(2,1)} %bitcast.22.piece), custom_call_target="tpu_custom_call" | custom-call | flops 939524096 | bytes 2097152 | tf_op jit(solution)/shard_map/pallas_call | solution.py:118
  139.4 1.7 all-to-all-done.4
  141.1 5.1 %all-to-all-start.5 = ((bf16[16,16,896]{2,1,0:T(8,128)(2,1)}), bf16[16,16,896]{2,1,0:T(8,128)(2,1)S(1)}, u32[]{:S(2)}, u32[]{:S(2)}) async-start(bf16[16,16,896]{2,1,0:T(8,128)(2,1)} %bitcast.33), calls=%async_computation.5 | async-start | bytes 917504 | tf_op jit(solution)/shard_map/all_to_all | solution.py:32
  147.7 2.2 %collective-permute-start.18 = (bf16[2,8,1024]{2,1,0:T(8,128)(2,1)S(1)}, bf16[2,8,1024]{2,1,0:T(8,128)(2,1)S(1)}, u32[]{:S(2)}, u32[]{:S(2)}) collective-permute-start(bf16[2,8,1024]{2,1,0:T(8,128)(2,1)S(1)} %get-tuple-element.65), channel_id=1, source_target_pairs={{0,3},{1,2},{2,1},{3,0},{4,7},{5,6},{6,5},{7,4},{8,11},{9,10},{10,... | collective-permute-start | bytes 98312 | tf_op jit(solution)/shard_map/ppermute | solution.py:83
  153.7 2.5 %all-to-all-done.5 = bf16[16,16,896]{2,1,0:T(8,128)(2,1)S(1)} async-done(((bf16[16,16,896]{2,1,0:T(8,128)(2,1)}), bf16[16,16,896]{2,1,0:T(8,128)(2,1)S(1)}, u32[]{:S(2)}, u32[]{:S(2)}) %all-to-all-start.5) | async-done | bytes 458784 | tf_op jit(solution)/shard_map/all_to_all | solution.py:32
  157.7 6.5 %all-to-all-start.6 = ((bf16[32,8,1024]{2,1,0:T(8,128)(2,1)}), bf16[32,8,1024]{2,1,0:T(8,128)(2,1)S(1)}, u32[]{:S(2)}, u32[]{:S(2)}) async-start(bf16[32,8,1024]{2,1,0:T(8,128)(2,1)} %fusion), calls=%async_computation.6 | async-start | bytes 1048576 | tf_op jit(solution)/shard_map/all_to_all | solution.py:32
  164.8 3.1 %convolution_convert_fusion = bf16[896,1024]{1,0:T(8,128)(2,1)} fusion(bf16[256,896]{1,0:T(8,128)(2,1)} %bitcast.90, bf16[256,1024]{1,0:T(8,128)(2,1)} %bitcast.88), kind=kOutput, calls=%fused_computation | convolution fusion | flops 470679552 | bytes 2818048 | tf_op jit(solution)/shard_map/dot_general | solution.py:24
  167.9 2.3 %shard_map.96 = (bf16[256,3584]{1,0:T(8,128)(2,1)}, bf16[256,3584]{1,0:T(8,128)(2,1)}) custom-call(s32[1]{0:T(128)} %bitcast.core, bf16[256,3584]{1,0:T(8,128)(2,1)} %get-tuple-element.46._, bf16[256,3584]{1,0:T(8,128)(2,1)} %get-tuple-element.47.__, ...), custom_call_target="tpu_custom_call", output_to_operand_aliasing={{0}: (1, {}), {1}: (2, {})} | custom-call | bytes 5505024 | tf_op jit(solution)/shard_map/pallas_call | solution.py:118
  170.2 5.5 %all-to-all-done.6 = bf16[32,8,1024]{2,1,0:T(8,128)(2,1)S(1)} async-done(((bf16[32,8,1024]{2,1,0:T(8,128)(2,1)}), bf16[32,8,1024]{2,1,0:T(8,128)(2,1)S(1)}, u32[]{:S(2)}, u32[]{:S(2)}) %all-to-all-start.6) | async-done | bytes 524320 | tf_op jit(solution)/shard_map/all_to_all | solution.py:32
  (76 shorter events, 26.6 us)
Async XLA Ops:
  0.6 36.2 %copy-start = (bf16[896,1024]{1,0:T(8,128)(2,1)S(1)}, bf16[896,1024]{1,0:T(8,128)(2,1)}, u32[]{:S(2)}) copy-start(bf16[896,1024]{1,0:T(8,128)(2,1)} %param.8) | copy-start | bytes 5505028
  0.6 17.5 %collective-permute-start = (bf16[1,1,1,8,1024]{4,3,2,1,0:T(8,128)(2,1)}, bf16[1,1,1,8,1024]{4,3,2,1,0:T(8,128)(2,1)S(1)}, u32[]{:S(2)}, u32[]{:S(2)}) collective-permute-start(bf16[1,1,1,8,1024]{4,3,2,1,0:T(8,128)(2,1)} %bitcast.102), channel_id=1, source_target_pairs={{0,4},{1,5},{2,6},{3,7},{4,0},{5,1},{6,2},{7,3},{8,12},{9,13},{10,... | collective-permute-start | bytes 49160 | tf_op jit(solution)/shard_map/ppermute | solution.py:51
  10.0 19.6 %all-to-all-start = ((bf16[32,8,1024]{2,1,0:T(8,128)(2,1)}), bf16[32,8,1024]{2,1,0:T(8,128)(2,1)S(1)}, u32[]{:S(2)}, u32[]{:S(2)}) async-start(bf16[32,8,1024]{2,1,0:T(8,128)(2,1)} %broadcast_in_dim.19), calls=%async_computation | async-start | bytes 1048576 | tf_op jit(solution)/shard_map/all_to_all | solution.py:32
  19.0 4.9 %copy-start.7 = (bf16[8,1024]{1,0:T(8,128)(2,1)S(1)}, bf16[8,1024]{1,0:T(8,128)(2,1)}, u32[]{:S(2)}) copy-start(bf16[8,1024]{1,0:T(8,128)(2,1)} %param.5) | copy-start | bytes 49156
  19.1 5.0 %collective-permute-start.1 = (bf16[2,1,1,8,1024]{4,3,2,1,0:T(8,128)(2,1)S(1)}, bf16[2,1,1,8,1024]{4,3,2,1,0:T(8,128)(2,1)S(1)}, u32[]{:S(2)}, u32[]{:S(2)}) collective-permute-start(bf16[2,1,1,8,1024]{4,3,2,1,0:T(8,128)(2,1)S(1)} %maximum_select_fusion.7), channel_id=1, source_target_pairs={{0,2},{1,3},{2,0},{3,1},{4,6},{5,7},{6,4},{7,5},{8,10},{9,11},{10,... | collective-permute-start | bytes 98312 | tf_op jit(solution)/shard_map/ppermute | solution.py:51
  22.5 23.3 %collective-permute-start.5 = (bf16[256,1792]{1,0:T(8,128)(2,1)}, bf16[256,1792]{1,0:T(8,128)(2,1)S(1)}, u32[]{:S(2)}, u32[]{:S(2)}) collective-permute-start(bf16[256,1792]{1,0:T(8,128)(2,1)} %constant_dynamic-slice_fusion.2), channel_id=1, source_target_pairs={{0,8},{8,0},{1,9},{9,1},{2,10},{10,2},{3,11},{11,3},{4,12},{12,4},... | collective-permute-start | bytes 2752520 | tf_op jit(solution)/shard_map/ppermute | solution.py:328
  24.0 21.8 %collective-permute-start.6 = (bf16[256,1792]{1,0:T(8,128)(2,1)}, bf16[256,1792]{1,0:T(8,128)(2,1)}, u32[]{:S(2)}, u32[]{:S(2)}) collective-permute-start(bf16[256,1792]{1,0:T(8,128)(2,1)} %constant_dynamic-slice_fusion.1), channel_id=1, source_target_pairs={{0,8},{8,0},{1,9},{9,1},{2,10},{10,2},{3,11},{11,3},{4,12},{12,4},... | collective-permute-start | bytes 2752520 | tf_op jit(solution)/shard_map/ppermute | solution.py:328
  24.0 3.5 %collective-permute-start.2 = (bf16[2,2,1,8,1024]{4,3,2,1,0:T(8,128)(2,1)S(1)}, bf16[2,2,1,8,1024]{4,3,2,1,0:T(8,128)(2,1)S(1)}, u32[]{:S(2)}, u32[]{:S(2)}) collective-permute-start(bf16[2,2,1,8,1024]{4,3,2,1,0:T(8,128)(2,1)S(1)} %maximum_select_fusion.2), channel_id=1, source_target_pairs={{0,1},{1,0},{2,3},{3,2},{4,5},{5,4},{6,7},{7,6},{8,9},{9,8},{10,11... | collective-permute-start | bytes 196616 | tf_op jit(solution)/shard_map/ppermute | solution.py:51
  29.6 8.0 %copy-start.4 = (bf16[32,8,1024]{2,1,0:T(8,128)(2,1)}, bf16[32,8,1024]{2,1,0:T(8,128)(2,1)S(1)}, u32[]{:S(2)}) copy-start(bf16[32,8,1024]{2,1,0:T(8,128)(2,1)S(1)} %all-to-all-done) | copy-start | bytes 1572868
  30.4 15.4 %all-to-all-start.1 = ((bf16[32,8,512]{2,1,0:T(8,128)(2,1)}), bf16[32,8,512]{2,1,0:T(8,128)(2,1)S(1)}, u32[]{:S(2)}, u32[]{:S(2)}) async-start(bf16[32,8,512]{2,1,0:T(8,128)(2,1)} %bitcast.91), calls=%async_computation.1 | async-start | bytes 524288 | tf_op jit(solution)/shard_map/all_to_all | solution.py:32
  37.7 5.7 %collective-permute-start.4 = (bf16[2,32,896]{2,1,0:T(8,128)(2,1)S(1)}, bf16[2,32,896]{2,1,0:T(8,128)(2,1)S(1)}, u32[]{:S(2)}, u32[]{:S(2)}) collective-permute-start(bf16[2,32,896]{2,1,0:T(8,128)(2,1)S(1)} %get-tuple-element.62), channel_id=1, source_target_pairs={{0,1},{1,0},{2,3},{3,2},{4,5},{5,4},{6,7},{7,6},{8,9},{9,8},{10,11... | collective-permute-start | bytes 344072 | tf_op jit(solution)/shard_map/ppermute | solution.py:83
  38.5 11.0 %collective-permute-start.3 = (bf16[2,32,896]{2,1,0:T(8,128)(2,1)S(1)}, bf16[2,32,896]{2,1,0:T(8,128)(2,1)S(1)}, u32[]{:S(2)}, u32[]{:S(2)}) collective-permute-start(bf16[2,32,896]{2,1,0:T(8,128)(2,1)S(1)} %get-tuple-element.63), channel_id=1, source_target_pairs={{0,2},{1,3},{2,0},{3,1},{4,6},{5,7},{6,4},{7,5},{8,10},{9,11},{10,... | collective-permute-start | bytes 344072 | tf_op jit(solution)/shard_map/ppermute | solution.py:83
  49.5 28.8 %all-to-all-start.2 = ((bf16[16,16,3584]{2,1,0:T(8,128)(2,1)}), bf16[16,16,3584]{2,1,0:T(8,128)(2,1)}, u32[]{:S(2)}, u32[]{:S(2)}) async-start(bf16[16,16,3584]{2,1,0:T(8,128)(2,1)} %bitcast.86), calls=%async_computation.2 | async-start | bytes 3670016 | tf_op jit(solution)/shard_map/all_to_all | solution.py:32
  53.9 5.6 %collective-permute-start.7 = (bf16[2,32,896]{2,1,0:T(8,128)(2,1)S(1)}, bf16[2,32,896]{2,1,0:T(8,128)(2,1)S(1)}, u32[]{:S(2)}, u32[]{:S(2)}) collective-permute-start(bf16[2,32,896]{2,1,0:T(8,128)(2,1)S(1)} %get-tuple-element.61), channel_id=1, source_target_pairs={{0,3},{1,2},{2,1},{3,0},{4,7},{5,6},{6,5},{7,4},{8,11},{9,10},{10,... | collective-permute-start | bytes 344072 | tf_op jit(solution)/shard_map/ppermute | solution.py:83
  60.5 7.4 %collective-permute-start.8 = (bf16[32,896]{1,0:T(8,128)(2,1)S(1)}, bf16[32,896]{1,0:T(8,128)(2,1)S(1)}, u32[]{:S(2)}, u32[]{:S(2)}) collective-permute-start(bf16[32,896]{1,0:T(8,128)(2,1)S(1)} %dynamic-slice_bitcast_fusion.3), channel_id=1, source_target_pairs={{0,4},{1,5},{2,6},{3,7},{4,0},{5,1},{6,2},{7,3},{8,12},{9,13},{10,... | collective-permute-start | bytes 172040 | tf_op jit(solution)/shard_map/ppermute | solution.py:94
  67.9 4.8 %collective-permute-start.9 = (bf16[16,896]{1,0:T(8,128)(2,1)S(1)}, bf16[16,896]{1,0:T(8,128)(2,1)S(1)}, u32[]{:S(2)}, u32[]{:S(2)}) collective-permute-start(bf16[16,896]{1,0:T(8,128)(2,1)S(1)} %get-tuple-element.68), channel_id=1, source_target_pairs={{0,8},{8,0},{1,9},{9,1},{2,10},{10,2},{3,11},{11,3},{4,12},{12,4},... | collective-permute-start | bytes 86024 | tf_op jit(solution)/shard_map/ppermute | solution.py:352
  72.7 5.5 %collective-permute-start.10 = (bf16[2,16,896]{2,1,0:T(8,128)(2,1)S(1)}, bf16[2,16,896]{2,1,0:T(8,128)(2,1)S(1)}, u32[]{:S(2)}, u32[]{:S(2)}) collective-permute-start(bf16[2,16,896]{2,1,0:T(8,128)(2,1)S(1)} %maximum_select_fusion.3), channel_id=1, source_target_pairs={{0,0},{1,32},{2,64},{3,96},{4,128},{5,160},{6,192},{7,224},{8,16},... | collective-permute-start | bytes 172040 | tf_op jit(solution)/shard_map/ppermute | solution.py:353
  80.9 41.2 %all-to-all-start.3 = ((bf16[16,16,3584]{2,1,0:T(8,128)(2,1)}), bf16[16,16,3584]{2,1,0:T(8,128)(2,1)}, u32[]{:S(2)}, u32[]{:S(2)}) async-start(bf16[16,16,3584]{2,1,0:T(8,128)(2,1)} %get-tuple-element.40), calls=%async_computation.3 | async-start | bytes 3670016 | tf_op jit(solution)/shard_map/all_to_all | solution.py:32
  96.0 2.1 %collective-permute-start.11 = (bf16[16,896]{1,0:T(8,128)(2,1)S(1)}, bf16[16,896]{1,0:T(8,128)(2,1)S(1)}, u32[]{:S(2)}, u32[]{:S(2)}) collective-permute-start(bf16[16,896]{1,0:T(8,128)(2,1)S(1)} %get-tuple-element.42), channel_id=1, source_target_pairs={{0,8},{8,0},{1,9},{9,1},{2,10},{10,2},{3,11},{11,3},{4,12},{12,4},... | collective-permute-start | bytes 86024 | tf_op jit(solution)/shard_map/ppermute | solution.py:357
  98.1 7.4 %collective-permute-start.12 = (bf16[2,16,896]{2,1,0:T(8,128)(2,1)S(1)}, bf16[2,16,896]{2,1,0:T(8,128)(2,1)S(1)}, u32[]{:S(2)}, u32[]{:S(2)}) collective-permute-start(bf16[2,16,896]{2,1,0:T(8,128)(2,1)S(1)} %maximum_select_fusion.5), channel_id=1, source_target_pairs={{0,4},{1,5},{2,6},{3,7},{4,0},{5,1},{6,2},{7,3},{8,12},{9,13},{10,... | collective-permute-start | bytes 172040 | tf_op jit(solution)/shard_map/ppermute | solution.py:69
  105.5 26.5 %collective-permute-start.13 = (bf16[2,2,16,896]{3,2,1,0:T(8,128)(2,1)S(1)}, bf16[2,2,16,896]{3,2,1,0:T(8,128)(2,1)S(1)}, u32[]{:S(2)}, u32[]{:S(2)}) collective-permute-start(bf16[2,2,16,896]{3,2,1,0:T(8,128)(2,1)S(1)} %maximum_select_fusion.1), channel_id=1, source_target_pairs={{0,1},{1,0},{2,3},{3,2},{4,5},{5,4},{6,7},{7,6},{8,9},{9,8},{10,11... | collective-permute-start | bytes 344072 | tf_op jit(solution)/shard_map/ppermute | solution.py:72
  105.6 26.4 %collective-permute-start.14 = (bf16[2,2,16,896]{3,2,1,0:T(8,128)(2,1)S(1)}, bf16[2,2,16,896]{3,2,1,0:T(8,128)(2,1)S(1)}, u32[]{:S(2)}, u32[]{:S(2)}) collective-permute-start(bf16[2,2,16,896]{3,2,1,0:T(8,128)(2,1)S(1)} %maximum_select_fusion.1), channel_id=1, source_target_pairs={{0,2},{1,3},{2,0},{3,1},{4,6},{5,7},{6,4},{7,5},{8,10},{9,11},{10,... | collective-permute-start | bytes 344072 | tf_op jit(solution)/shard_map/ppermute | solution.py:72
  106.1 26.0 %collective-permute-start.15 = (bf16[2,2,16,896]{3,2,1,0:T(8,128)(2,1)S(1)}, bf16[2,2,16,896]{3,2,1,0:T(8,128)(2,1)}, u32[]{:S(2)}, u32[]{:S(2)}) collective-permute-start(bf16[2,2,16,896]{3,2,1,0:T(8,128)(2,1)S(1)} %maximum_select_fusion.1), channel_id=1, source_target_pairs={{0,3},{1,2},{2,1},{3,0},{4,7},{5,6},{6,5},{7,4},{8,11},{9,10},{10,... | collective-permute-start | bytes 344072 | tf_op jit(solution)/shard_map/ppermute | solution.py:72
  125.9 15.1 %all-to-all-start.4 = ((bf16[32,8,512]{2,1,0:T(8,128)(2,1)}), bf16[32,8,512]{2,1,0:T(8,128)(2,1)S(1)}, u32[]{:S(2)}, u32[]{:S(2)}) async-start(bf16[32,8,512]{2,1,0:T(8,128)(2,1)} %bitcast.23), calls=%async_computation.4 | async-start | bytes 524288 | tf_op jit(solution)/shard_map/all_to_all | solution.py:32
  141.1 15.1 %all-to-all-start.5 = ((bf16[16,16,896]{2,1,0:T(8,128)(2,1)}), bf16[16,16,896]{2,1,0:T(8,128)(2,1)S(1)}, u32[]{:S(2)}, u32[]{:S(2)}) async-start(bf16[16,16,896]{2,1,0:T(8,128)(2,1)} %bitcast.33), calls=%async_computation.5 | async-start | bytes 917504 | tf_op jit(solution)/shard_map/all_to_all | solution.py:32
  146.3 5.1 %collective-permute-start.16 = (bf16[2,8,1024]{2,1,0:T(8,128)(2,1)S(1)}, bf16[2,8,1024]{2,1,0:T(8,128)(2,1)S(1)}, u32[]{:S(2)}, u32[]{:S(2)}) collective-permute-start(bf16[2,8,1024]{2,1,0:T(8,128)(2,1)S(1)} %get-tuple-element.64), channel_id=1, source_target_pairs={{0,1},{1,0},{2,3},{3,2},{4,5},{5,4},{6,7},{7,6},{8,9},{9,8},{10,11... | collective-permute-start | bytes 98312 | tf_op jit(solution)/shard_map/ppermute | solution.py:83
  146.4 5.0 %collective-permute-start.17 = (bf16[2,8,1024]{2,1,0:T(8,128)(2,1)S(1)}, bf16[2,8,1024]{2,1,0:T(8,128)(2,1)S(1)}, u32[]{:S(2)}, u32[]{:S(2)}) collective-permute-start(bf16[2,8,1024]{2,1,0:T(8,128)(2,1)S(1)} %get-tuple-element.66), channel_id=1, source_target_pairs={{0,2},{1,3},{2,0},{3,1},{4,6},{5,7},{6,4},{7,5},{8,10},{9,11},{10,... | collective-permute-start | bytes 98312 | tf_op jit(solution)/shard_map/ppermute | solution.py:83
  147.7 4.6 %collective-permute-start.18 = (bf16[2,8,1024]{2,1,0:T(8,128)(2,1)S(1)}, bf16[2,8,1024]{2,1,0:T(8,128)(2,1)S(1)}, u32[]{:S(2)}, u32[]{:S(2)}) collective-permute-start(bf16[2,8,1024]{2,1,0:T(8,128)(2,1)S(1)} %get-tuple-element.65), channel_id=1, source_target_pairs={{0,3},{1,2},{2,1},{3,0},{4,7},{5,6},{6,5},{7,4},{8,11},{9,10},{10,... | collective-permute-start | bytes 98312 | tf_op jit(solution)/shard_map/ppermute | solution.py:83
  149.9 17.9 %collective-permute-start.21 = (bf16[256,1792]{1,0:T(8,128)(2,1)}, bf16[256,1792]{1,0:T(8,128)(2,1)S(1)}, u32[]{:S(2)}, u32[]{:S(2)}) collective-permute-start(bf16[256,1792]{1,0:T(8,128)(2,1)} %copy-done.2), channel_id=1, source_target_pairs={{0,8},{8,0},{1,9},{9,1},{2,10},{10,2},{3,11},{11,3},{4,12},{12,4},... | collective-permute-start | bytes 2752520 | tf_op jit(solution)/shard_map/ppermute | solution.py:376
  151.4 16.5 %collective-permute-start.20 = (bf16[256,1792]{1,0:T(8,128)(2,1)}, bf16[256,1792]{1,0:T(8,128)(2,1)}, u32[]{:S(2)}, u32[]{:S(2)}) collective-permute-start(bf16[256,1792]{1,0:T(8,128)(2,1)} %copy-done.1), channel_id=1, source_target_pairs={{0,8},{8,0},{1,9},{9,1},{2,10},{10,2},{3,11},{11,3},{4,12},{12,4},... | collective-permute-start | bytes 2752520 | tf_op jit(solution)/shard_map/ppermute | solution.py:375
  152.3 11.8 %collective-permute-start.19 = (bf16[8,1024]{1,0:T(8,128)(2,1)S(1)}, bf16[8,1024]{1,0:T(8,128)(2,1)S(1)}, u32[]{:S(2)}, u32[]{:S(2)}) collective-permute-start(bf16[8,1024]{1,0:T(8,128)(2,1)S(1)} %dynamic-slice_bitcast_fusion.8), channel_id=1, source_target_pairs={{0,4},{1,5},{2,6},{3,7},{4,0},{5,1},{6,2},{7,3},{8,12},{9,13},{10,... | collective-permute-start | bytes 49160 | tf_op jit(solution)/shard_map/ppermute | solution.py:94
  157.7 18.0 %all-to-all-start.6 = ((bf16[32,8,1024]{2,1,0:T(8,128)(2,1)}), bf16[32,8,1024]{2,1,0:T(8,128)(2,1)S(1)}, u32[]{:S(2)}, u32[]{:S(2)}) async-start(bf16[32,8,1024]{2,1,0:T(8,128)(2,1)} %fusion), calls=%async_computation.6 | async-start | bytes 1048576 | tf_op jit(solution)/shard_map/all_to_all | solution.py:32
  (5 other events, 10.3 us)

commit v4 on v3

--- a/solution.py
+++ b/solution.py
@@ -174,17 +174,19 @@
     )
 
 
-def activations(core, terms, grad_hidden):
+def activations(core, terms):
     chips, tall, wide = terms.shape
     quarter = wide // 4
 
-    def body(core, terms, grad_hidden, copies, keep, send):
+    def body(core, terms, factors, keep, send):
         both = terms[0].astype(F32)
         for chip in range(1, chips):
             both = both + terms[chip].astype(F32)
         gate, up = both[:, :quarter], both[:, quarter:]
         sigmoid_gate = 1.0 / (1.0 + jnp.exp(-gate))
         silu_gate = gate * sigmoid_gate
+        factors[:, :quarter] = up * sigmoid_gate * (1.0 + gate * (1.0 - sigmoid_gate))
+        factors[:, quarter:] = silu_gate
         hidden = (silu_gate * up).astype(BF16)
 
         @pl.when(pl.program_id(0) == core[0])
@@ -195,26 +197,45 @@
         def _():
             send[...] = hidden
 
+    half = pl.BlockSpec((chips, tall, 2 * quarter), lambda step, core: (0, 0, step))
+    flat = pl.BlockSpec((tall, quarter), lambda step, core: (0, 0))
+    return call(
+        body,
+        core,
+        (terms,),
+        [half],
+        [jax.ShapeDtypeStruct((tall, wide), F32)]
+        + [jax.ShapeDtypeStruct((tall, quarter), BF16)] * 2,
+        [pl.BlockSpec((tall, 2 * quarter), in_turn), flat, flat],
+        2,
+        cost=30 * tall * wide,
+    )
+
+
+def unit_grads(core, factors, grad_hidden, chips):
+    tall, wide = factors.shape
+    quarter = wide // 4
+
+    def body(core, factors, grad_hidden, copies):
         cotangent = grad_hidden[0].astype(F32)
-        grad_gate = cotangent * up * sigmoid_gate * (1.0 + gate * (1.0 - sigmoid_gate))
-        grad_gate = grad_gate.astype(BF16)
-        grad_up = (cotangent * silu_gate).astype(BF16)
+        grad_gate = (cotangent * factors[:, :quarter]).astype(BF16)
+        grad_up = (cotangent * factors[:, quarter:]).astype(BF16)
         for chip in range(chips):
             copies[chip, :, :quarter] = grad_gate
             copies[chip, :, quarter:] = grad_up
 
-    half = pl.BlockSpec((chips, tall, 2 * quarter), lambda step, core: (0, 0, step))
-    flat = pl.BlockSpec((tall, quarter), lambda step, core: (0, 0))
-    return call(
-        body,
-        core,
-        (terms, grad_hidden),
-        [half, pl.BlockSpec((1, tall, quarter), lambda step, core: (step, 0, 0))],
-        [pltpu.HBM(terms.shape, BF16)]
-        + [jax.ShapeDtypeStruct((tall, quarter), BF16)] * 2,
-        [half, flat, flat],
-        2,
-        cost=30 * tall * wide,
+    return call(
+        body,
+        core,
+        (factors, grad_hidden),
+        [
+            pl.BlockSpec((tall, 2 * quarter), in_turn),
+            pl.BlockSpec((1, tall, quarter), lambda step, core: (step, 0, 0)),
+        ],
+        pltpu.HBM((chips, tall, wide), BF16),
+        pl.BlockSpec((chips, tall, 2 * quarter), lambda step, core: (0, 0, step)),
+        2,
+        cost=2 * tall * wide,
     )
 
 
@@ -353,7 +374,8 @@
     grad_hidden = lax.ppermute(hidden_sum, EVERY, TO_OWNER)
 
     terms = exchange(sent.reshape(CHIPS, -1, units), PLANE)
-    copies, hidden_keep, hidden_send = activations(core, terms, grad_hidden)
+    factors, hidden_keep, hidden_send = activations(core, terms)
+    copies = unit_grads(core, factors, grad_hidden, CHIPS)
     hidden = paired(at_core, hidden_keep, lax.ppermute(hidden_send, "core", SWAP))
     hidden = gather_hidden(hidden).reshape(CHIPS, -1, quarter)
     pieces = exchange(copies, PLANE).reshape(-1, units)

time: 177 us -> 176 us (level)
    ppermute x1, waiting for transfers between devices: 1.85 us -> 0.01 us  [local(): grad_hidden = lax.ppermute(hidden_sum, EVERY, TO_OWNER)]
    pallas_call x5 -> x6, Pallas kernels: 16.1 us -> 16.5 us  [call(): pl.pallas_call(body, grid_spec=pltpu.PrefetchScalarGridSpec(num_scalar_pr...]
  transfers between devices with their start and end apart: 29 -> 29, of which waited for: 15 -> 15; matrix products, arithmetic and copies ran while one was open for 9% -> 9% of each run, Pallas kernels for 8% -> 9%
where the time goes in v4:
time: 176 us; the launch traced here: 175 us
  starting transfers between devices  83.8 us (48%)
  waiting for transfers between devices  55.7 us (32%)
  Pallas kernels  16.5 us (9%)
  local copies, waits for them, and re-layouts  8.26 us (5%)
  matrix products  5.32 us (3%)
  other arithmetic  4.35 us (2%)
    all_to_all x7, starting transfers between devices, exchange(): return lax.all_to_all(blocks, axis, split_axis=0, concat_axis=0, tiled=True)  50.9 us
    all_to_all x7, waiting for transfers between devices, exchange(): return lax.all_to_all(blocks, axis, split_axis=0, concat_axis=0, tiled=True)  28.7 us
    pallas_call x6, Pallas kernels, call(): pl.pallas_call(body, grid_spec=pltpu.PrefetchScalarGridSpec(num_scalar_pr...  16.5 us
    ppermute x3, starting transfers between devices, gather_columns(): got = lax.ppermute(share, 'z', pairs(distance))  9.92 us
    ppermute x6, waiting for transfers between devices, near_exchange(): return (near[0], [lax.ppermute(near[d], 'z', pairs(d)) for d in (1, 2, 3)])  8.52 us
    ppermute x6, starting transfers between devices, near_exchange(): return (near[0], [lax.ppermute(near[d], 'z', pairs(d)) for d in (1, 2, 3)])  7.33 us
    ppermute x1, waiting for transfers between devices, gather_hidden(): got = lax.ppermute(block, 'z', pairs(4))  7.3 us
    ppermute x2, waiting for transfers between devices, far_exchange(): far = lax.ppermute(send, 'z', pairs(4))  6.86 us
  transfers between devices with their start and end apart: 29, of which 15 were waited for; matrix products, arithmetic and copies ran while one was open for 9% of the time, Pallas kernels for 9%

profile of v4, /device:TPU:1, one launch (start us, length us, event | category | flops | bytes accessed | tf_op | source)
XLA Modules:
  0.0 174.9 jit_solution(17905116028018893617)
XLA Ops:
  0.6 7.8 %collective-permute-start = (bf16[1,1,1,8,1024]{4,3,2,1,0:T(8,128)(2,1)}, bf16[1,1,1,8,1024]{4,3,2,1,0:T(8,128)(2,1)S(1)}, u32[]{:S(2)}, u32[]{:S(2)}) collective-permute-start(bf16[1,1,1,8,1024]{4,3,2,1,0:T(8,128)(2,1)} %bitcast.102), channel_id=1, source_target_pairs={{0,4},{1,5},{2,6},{3,7},{4,0},{5,1},{6,2},{7,3},{8,12},{9,13},{10,... | collective-permute-start | bytes 49160 | tf_op jit(solution)/shard_map/ppermute | solution.py:51
  8.5 1.6 broadcast_in_dim.19
  10.0 8.0 %all-to-all-start = ((bf16[32,8,1024]{2,1,0:T(8,128)(2,1)}), bf16[32,8,1024]{2,1,0:T(8,128)(2,1)S(1)}, u32[]{:S(2)}, u32[]{:S(2)}) async-start(bf16[32,8,1024]{2,1,0:T(8,128)(2,1)} %broadcast_in_dim.19), calls=%async_computation | async-start | bytes 1048576 | tf_op jit(solution)/shard_map/all_to_all | solution.py:32
  20.3 2.2 %constant_dynamic-slice_fusion.2 = bf16[256,1792]{1,0:T(8,128)(2,1)} fusion(bf16[256,3584]{1,0:T(8,128)(2,1)} %gate_mine.3, s32[]{:T(128)S(6)} %select_n.253), kind=kLoop, calls=%fused_computation.46 | loop fusion | bytes 1835012 | tf_op jit(solution)/shard_map/dynamic_slice | solution.py:348
  24.9 2.7 %collective-permute-done.2 = bf16[2,2,1,8,1024]{4,3,2,1,0:T(8,128)(2,1)S(1)} collective-permute-done((bf16[2,2,1,8,1024]{4,3,2,1,0:T(8,128)(2,1)S(1)}, bf16[2,2,1,8,1024]{4,3,2,1,0:T(8,128)(2,1)S(1)}, u32[]{:S(2)}, u32[]{:S(2)}) %collective-permute-start.2) | collective-permute-done | bytes 65568 | tf_op jit(solution)/shard_map/ppermute | solution.py:51
  27.6 2.1 %all-to-all-done = bf16[32,8,1024]{2,1,0:T(8,128)(2,1)S(1)} async-done(((bf16[32,8,1024]{2,1,0:T(8,128)(2,1)}), bf16[32,8,1024]{2,1,0:T(8,128)(2,1)S(1)}, u32[]{:S(2)}, u32[]{:S(2)}) %all-to-all-start) | async-done | bytes 524320 | tf_op jit(solution)/shard_map/all_to_all | solution.py:32
  30.4 6.4 %all-to-all-start.1 = ((bf16[32,8,512]{2,1,0:T(8,128)(2,1)}), bf16[32,8,512]{2,1,0:T(8,128)(2,1)S(1)}, u32[]{:S(2)}, u32[]{:S(2)}) async-start(bf16[32,8,512]{2,1,0:T(8,128)(2,1)} %bitcast.91), calls=%async_computation.1 | async-start | bytes 524288 | tf_op jit(solution)/shard_map/all_to_all | solution.py:32
  39.7 3.7 %collective-permute-done.4 = bf16[2,32,896]{2,1,0:T(8,128)(2,1)S(1)} collective-permute-done((bf16[2,32,896]{2,1,0:T(8,128)(2,1)S(1)}, bf16[2,32,896]{2,1,0:T(8,128)(2,1)S(1)}, u32[]{:S(2)}, u32[]{:S(2)}) %collective-permute-start.4) | collective-permute-done | bytes 114720 | tf_op jit(solution)/shard_map/ppermute | solution.py:83
  43.4 2.3 %all-to-all-done.1 = bf16[32,8,512]{2,1,0:T(8,128)(2,1)S(1)} async-done(((bf16[32,8,512]{2,1,0:T(8,128)(2,1)}), bf16[32,8,512]{2,1,0:T(8,128)(2,1)S(1)}, u32[]{:S(2)}, u32[]{:S(2)}) %all-to-all-start.1) | async-done | bytes 262176 | tf_op jit(solution)/shard_map/all_to_all | solution.py:32
  45.8 3.7 %shard_map.92 = bf16[256,3584]{1,0:T(8,128)(2,1)} custom-call(s32[1]{0:T(128)} %bitcast.core, bf16[256,512]{1,0:T(8,128)(2,1)S(1)} %bitcast.82, bf16[256,3584]{1,0:T(8,128)(2,1)} %gate_mine.3, bf16[256,1792]{1,0:T(8,128)(2,1)S(1)} %collective-permute-done.5.gate_other, bf16[256,3584]{1,0:T(8,128)(2,1)} %up_mine.3, ...), custom_call_target="tpu_custom_call" | custom-call | flops 939524096 | bytes 5767168 | tf_op jit(solution)/shard_map/pallas_call | solution.py:118
  49.5 4.4 %all-to-all-start.2 = ((bf16[16,16,3584]{2,1,0:T(8,128)(2,1)}), bf16[16,16,3584]{2,1,0:T(8,128)(2,1)}, u32[]{:S(2)}, u32[]{:S(2)}) async-start(bf16[16,16,3584]{2,1,0:T(8,128)(2,1)} %bitcast.86), calls=%async_computation.2 | async-start | bytes 3670016 | tf_op jit(solution)/shard_map/all_to_all | solution.py:32
  53.9 1.7 collective-permute-start.7
  55.6 3.9 %collective-permute-done.7 = bf16[2,32,896]{2,1,0:T(8,128)(2,1)S(1)} collective-permute-done((bf16[2,32,896]{2,1,0:T(8,128)(2,1)S(1)}, bf16[2,32,896]{2,1,0:T(8,128)(2,1)S(1)}, u32[]{:S(2)}, u32[]{:S(2)}) %collective-permute-start.7) | collective-permute-done | bytes 114720 | tf_op jit(solution)/shard_map/ppermute | solution.py:83
  61.0 6.9 %collective-permute-done.8 = bf16[32,896]{1,0:T(8,128)(2,1)S(1)} collective-permute-done((bf16[32,896]{1,0:T(8,128)(2,1)S(1)}, bf16[32,896]{1,0:T(8,128)(2,1)S(1)}, u32[]{:S(2)}, u32[]{:S(2)}) %collective-permute-start.8) | collective-permute-done | bytes 57376 | tf_op jit(solution)/shard_map/ppermute | solution.py:94
  67.9 3.9 %collective-permute-start.9 = (bf16[16,896]{1,0:T(8,128)(2,1)S(1)}, bf16[16,896]{1,0:T(8,128)(2,1)S(1)}, u32[]{:S(2)}, u32[]{:S(2)}) collective-permute-start(bf16[16,896]{1,0:T(8,128)(2,1)S(1)} %get-tuple-element.68), channel_id=1, source_target_pairs={{0,8},{8,0},{1,9},{9,1},{2,10},{10,2},{3,11},{11,3},{4,12},{12,4},... | collective-permute-start | bytes 86024 | tf_op jit(solution)/shard_map/ppermute | solution.py:373
  72.7 3.7 %collective-permute-start.10 = (bf16[2,16,896]{2,1,0:T(8,128)(2,1)S(1)}, bf16[2,16,896]{2,1,0:T(8,128)(2,1)S(1)}, u32[]{:S(2)}, u32[]{:S(2)}) collective-permute-start(bf16[2,16,896]{2,1,0:T(8,128)(2,1)S(1)} %maximum_select_fusion.3), channel_id=1, source_target_pairs={{0,0},{1,32},{2,64},{3,96},{4,128},{5,160},{6,192},{7,224},{8,16},... | collective-permute-start | bytes 172040 | tf_op jit(solution)/shard_map/ppermute | solution.py:374
  77.2 1.6 shard_map.93
  80.3 14.4 %all-to-all-start.3 = ((bf16[16,16,3584]{2,1,0:T(8,128)(2,1)}), bf16[16,16,3584]{2,1,0:T(8,128)(2,1)}, u32[]{:S(2)}, u32[]{:S(2)}) async-start(bf16[16,16,3584]{2,1,0:T(8,128)(2,1)} %shard_map.94), calls=%async_computation.3 | async-start | bytes 3670016 | tf_op jit(solution)/shard_map/all_to_all | solution.py:32
  96.9 7.3 %collective-permute-done.12 = bf16[2,16,896]{2,1,0:T(8,128)(2,1)S(1)} collective-permute-done((bf16[2,16,896]{2,1,0:T(8,128)(2,1)S(1)}, bf16[2,16,896]{2,1,0:T(8,128)(2,1)S(1)}, u32[]{:S(2)}, u32[]{:S(2)}) %collective-permute-start.12) | collective-permute-done | bytes 57376 | tf_op jit(solution)/shard_map/ppermute | solution.py:69
  105.1 2.8 %collective-permute-start.15 = (bf16[2,2,16,896]{3,2,1,0:T(8,128)(2,1)S(1)}, bf16[2,2,16,896]{3,2,1,0:T(8,128)(2,1)}, u32[]{:S(2)}, u32[]{:S(2)}) collective-permute-start(bf16[2,2,16,896]{3,2,1,0:T(8,128)(2,1)S(1)} %maximum_select_fusion.1), channel_id=1, source_target_pairs={{0,3},{1,2},{2,1},{3,0},{4,7},{5,6},{6,5},{7,4},{8,11},{9,10},{10,... | collective-permute-start | bytes 344072 | tf_op jit(solution)/shard_map/ppermute | solution.py:72
  107.9 12.9 %all-to-all-done.3 = bf16[16,16,3584]{2,1,0:T(8,128)(2,1)} async-done(((bf16[16,16,3584]{2,1,0:T(8,128)(2,1)}), bf16[16,16,3584]{2,1,0:T(8,128)(2,1)}, u32[]{:S(2)}, u32[]{:S(2)}) %all-to-all-start.3) | async-done | bytes 1835040 | tf_op jit(solution)/shard_map/all_to_all | solution.py:32
  120.8 3.9 %shard_map.95 = bf16[256,512]{1,0:T(8,128)(2,1)} custom-call(s32[1]{0:T(128)} %bitcast.core, bf16[256,3584]{1,0:T(8,128)(2,1)} %bitcast.22.piece, bf16[256,3584]{1,0:T(8,128)(2,1)} %gate_mine.3, bf16[256,1792]{1,0:T(8,128)(2,1)S(1)} %collective-permute-done.5.gate_other, bf16[256,3584]{1,0:T(8,128)(2,1)} %up_mine.3, ...), custom_call_target="tpu_custom_call" | custom-call | flops 939524096 | bytes 7340032 | tf_op jit(solution)/shard_map/pallas_call | solution.py:118
  124.7 6.1 %all-to-all-start.4 = ((bf16[32,8,512]{2,1,0:T(8,128)(2,1)}), bf16[32,8,512]{2,1,0:T(8,128)(2,1)S(1)}, u32[]{:S(2)}, u32[]{:S(2)}) async-start(bf16[32,8,512]{2,1,0:T(8,128)(2,1)} %bitcast.23), calls=%async_computation.4 | async-start | bytes 524288 | tf_op jit(solution)/shard_map/all_to_all | solution.py:32
  132.7 3.6 %shard_map.96 = (bf16[256,3584]{1,0:T(8,128)(2,1)}, bf16[256,3584]{1,0:T(8,128)(2,1)}, bf16[256,1792]{1,0:T(8,128)(2,1)S(1)}, bf16[256,1792]{1,0:T(8,128)(2,1)S(1)}) custom-call(s32[1]{0:T(128)} %bitcast.core, bf16[256,512]{1,0:T(8,128)(2,1)S(1)} %bitcast.83, bf16[256,3584]{1,0:T(8,128)(2,1)} %bitcast.22.piece), custom_call_target="tpu_custom_call" | custom-call | flops 939524096 | bytes 2097152 | tf_op jit(solution)/shard_map/pallas_call | solution.py:118
  138.1 1.7 all-to-all-done.4
  139.8 5.1 %all-to-all-start.5 = ((bf16[16,16,896]{2,1,0:T(8,128)(2,1)}), bf16[16,16,896]{2,1,0:T(8,128)(2,1)S(1)}, u32[]{:S(2)}, u32[]{:S(2)}) async-start(bf16[16,16,896]{2,1,0:T(8,128)(2,1)} %bitcast.33), calls=%async_computation.5 | async-start | bytes 917504 | tf_op jit(solution)/shard_map/all_to_all | solution.py:32
  146.4 2.2 %collective-permute-start.18 = (bf16[2,8,1024]{2,1,0:T(8,128)(2,1)S(1)}, bf16[2,8,1024]{2,1,0:T(8,128)(2,1)S(1)}, u32[]{:S(2)}, u32[]{:S(2)}) collective-permute-start(bf16[2,8,1024]{2,1,0:T(8,128)(2,1)S(1)} %get-tuple-element.65), channel_id=1, source_target_pairs={{0,3},{1,2},{2,1},{3,0},{4,7},{5,6},{6,5},{7,4},{8,11},{9,10},{10,... | collective-permute-start | bytes 98312 | tf_op jit(solution)/shard_map/ppermute | solution.py:83
  151.6 3.3 %all-to-all-done.5 = bf16[16,16,896]{2,1,0:T(8,128)(2,1)S(1)} async-done(((bf16[16,16,896]{2,1,0:T(8,128)(2,1)}), bf16[16,16,896]{2,1,0:T(8,128)(2,1)S(1)}, u32[]{:S(2)}, u32[]{:S(2)}) %all-to-all-start.5) | async-done | bytes 458784 | tf_op jit(solution)/shard_map/all_to_all | solution.py:32
  156.4 6.3 %all-to-all-start.6 = ((bf16[32,8,1024]{2,1,0:T(8,128)(2,1)}), bf16[32,8,1024]{2,1,0:T(8,128)(2,1)S(1)}, u32[]{:S(2)}, u32[]{:S(2)}) async-start(bf16[32,8,1024]{2,1,0:T(8,128)(2,1)} %fusion), calls=%async_computation.6 | async-start | bytes 1048576 | tf_op jit(solution)/shard_map/all_to_all | solution.py:32
  163.3 3.1 %convolution_convert_fusion = bf16[896,1024]{1,0:T(8,128)(2,1)} fusion(bf16[256,896]{1,0:T(8,128)(2,1)} %bitcast.90, bf16[256,1024]{1,0:T(8,128)(2,1)} %bitcast.88), kind=kOutput, calls=%fused_computation | convolution fusion | flops 470679552 | bytes 2818048 | tf_op jit(solution)/shard_map/dot_general | solution.py:24
  166.4 2.3 %shard_map.97 = (bf16[256,3584]{1,0:T(8,128)(2,1)}, bf16[256,3584]{1,0:T(8,128)(2,1)}) custom-call(s32[1]{0:T(128)} %bitcast.core, bf16[256,3584]{1,0:T(8,128)(2,1)} %get-tuple-element.46._, bf16[256,3584]{1,0:T(8,128)(2,1)} %get-tuple-element.47.__, ...), custom_call_target="tpu_custom_call", output_to_operand_aliasing={{0}: (1, {}), {1}: (2, {})} | custom-call | bytes 5505024 | tf_op jit(solution)/shard_map/pallas_call | solution.py:118
  168.7 5.5 %all-to-all-done.6 = bf16[32,8,1024]{2,1,0:T(8,128)(2,1)S(1)} async-done(((bf16[32,8,1024]{2,1,0:T(8,128)(2,1)}), bf16[32,8,1024]{2,1,0:T(8,128)(2,1)S(1)}, u32[]{:S(2)}, u32[]{:S(2)}) %all-to-all-start.6) | async-done | bytes 524320 | tf_op jit(solution)/shard_map/all_to_all | solution.py:32
  (77 shorter events, 26.6 us)
Async XLA Ops:
  0.6 36.2 %copy-start = (bf16[896,1024]{1,0:T(8,128)(2,1)S(1)}, bf16[896,1024]{1,0:T(8,128)(2,1)}, u32[]{:S(2)}) copy-start(bf16[896,1024]{1,0:T(8,128)(2,1)} %param.8) | copy-start | bytes 5505028
  0.6 17.5 %collective-permute-start = (bf16[1,1,1,8,1024]{4,3,2,1,0:T(8,128)(2,1)}, bf16[1,1,1,8,1024]{4,3,2,1,0:T(8,128)(2,1)S(1)}, u32[]{:S(2)}, u32[]{:S(2)}) collective-permute-start(bf16[1,1,1,8,1024]{4,3,2,1,0:T(8,128)(2,1)} %bitcast.102), channel_id=1, source_target_pairs={{0,4},{1,5},{2,6},{3,7},{4,0},{5,1},{6,2},{7,3},{8,12},{9,13},{10,... | collective-permute-start | bytes 49160 | tf_op jit(solution)/shard_map/ppermute | solution.py:51
  10.0 19.6 %all-to-all-start = ((bf16[32,8,1024]{2,1,0:T(8,128)(2,1)}), bf16[32,8,1024]{2,1,0:T(8,128)(2,1)S(1)}, u32[]{:S(2)}, u32[]{:S(2)}) async-start(bf16[32,8,1024]{2,1,0:T(8,128)(2,1)} %broadcast_in_dim.19), calls=%async_computation | async-start | bytes 1048576 | tf_op jit(solution)/shard_map/all_to_all | solution.py:32
  19.0 4.9 %copy-start.7 = (bf16[8,1024]{1,0:T(8,128)(2,1)S(1)}, bf16[8,1024]{1,0:T(8,128)(2,1)}, u32[]{:S(2)}) copy-start(bf16[8,1024]{1,0:T(8,128)(2,1)} %param.5) | copy-start | bytes 49156
  19.1 5.0 %collective-permute-start.1 = (bf16[2,1,1,8,1024]{4,3,2,1,0:T(8,128)(2,1)S(1)}, bf16[2,1,1,8,1024]{4,3,2,1,0:T(8,128)(2,1)S(1)}, u32[]{:S(2)}, u32[]{:S(2)}) collective-permute-start(bf16[2,1,1,8,1024]{4,3,2,1,0:T(8,128)(2,1)S(1)} %maximum_select_fusion.7), channel_id=1, source_target_pairs={{0,2},{1,3},{2,0},{3,1},{4,6},{5,7},{6,4},{7,5},{8,10},{9,11},{10,... | collective-permute-start | bytes 98312 | tf_op jit(solution)/shard_map/ppermute | solution.py:51
  22.5 23.3 %collective-permute-start.5 = (bf16[256,1792]{1,0:T(8,128)(2,1)}, bf16[256,1792]{1,0:T(8,128)(2,1)S(1)}, u32[]{:S(2)}, u32[]{:S(2)}) collective-permute-start(bf16[256,1792]{1,0:T(8,128)(2,1)} %constant_dynamic-slice_fusion.2), channel_id=1, source_target_pairs={{0,8},{8,0},{1,9},{9,1},{2,10},{10,2},{3,11},{11,3},{4,12},{12,4},... | collective-permute-start | bytes 2752520 | tf_op jit(solution)/shard_map/ppermute | solution.py:349
  24.0 21.8 %collective-permute-start.6 = (bf16[256,1792]{1,0:T(8,128)(2,1)}, bf16[256,1792]{1,0:T(8,128)(2,1)}, u32[]{:S(2)}, u32[]{:S(2)}) collective-permute-start(bf16[256,1792]{1,0:T(8,128)(2,1)} %constant_dynamic-slice_fusion.1), channel_id=1, source_target_pairs={{0,8},{8,0},{1,9},{9,1},{2,10},{10,2},{3,11},{11,3},{4,12},{12,4},... | collective-permute-start | bytes 2752520 | tf_op jit(solution)/shard_map/ppermute | solution.py:349
  24.0 3.5 %collective-permute-start.2 = (bf16[2,2,1,8,1024]{4,3,2,1,0:T(8,128)(2,1)S(1)}, bf16[2,2,1,8,1024]{4,3,2,1,0:T(8,128)(2,1)S(1)}, u32[]{:S(2)}, u32[]{:S(2)}) collective-permute-start(bf16[2,2,1,8,1024]{4,3,2,1,0:T(8,128)(2,1)S(1)} %maximum_select_fusion.2), channel_id=1, source_target_pairs={{0,1},{1,0},{2,3},{3,2},{4,5},{5,4},{6,7},{7,6},{8,9},{9,8},{10,11... | collective-permute-start | bytes 196616 | tf_op jit(solution)/shard_map/ppermute | solution.py:51
  29.6 8.0 %copy-start.4 = (bf16[32,8,1024]{2,1,0:T(8,128)(2,1)}, bf16[32,8,1024]{2,1,0:T(8,128)(2,1)S(1)}, u32[]{:S(2)}) copy-start(bf16[32,8,1024]{2,1,0:T(8,128)(2,1)S(1)} %all-to-all-done) | copy-start | bytes 1572868
  30.4 15.4 %all-to-all-start.1 = ((bf16[32,8,512]{2,1,0:T(8,128)(2,1)}), bf16[32,8,512]{2,1,0:T(8,128)(2,1)S(1)}, u32[]{:S(2)}, u32[]{:S(2)}) async-start(bf16[32,8,512]{2,1,0:T(8,128)(2,1)} %bitcast.91), calls=%async_computation.1 | async-start | bytes 524288 | tf_op jit(solution)/shard_map/all_to_all | solution.py:32
  37.7 5.7 %collective-permute-start.4 = (bf16[2,32,896]{2,1,0:T(8,128)(2,1)S(1)}, bf16[2,32,896]{2,1,0:T(8,128)(2,1)S(1)}, u32[]{:S(2)}, u32[]{:S(2)}) collective-permute-start(bf16[2,32,896]{2,1,0:T(8,128)(2,1)S(1)} %get-tuple-element.62), channel_id=1, source_target_pairs={{0,1},{1,0},{2,3},{3,2},{4,5},{5,4},{6,7},{7,6},{8,9},{9,8},{10,11... | collective-permute-start | bytes 344072 | tf_op jit(solution)/shard_map/ppermute | solution.py:83
  38.5 11.0 %collective-permute-start.3 = (bf16[2,32,896]{2,1,0:T(8,128)(2,1)S(1)}, bf16[2,32,896]{2,1,0:T(8,128)(2,1)S(1)}, u32[]{:S(2)}, u32[]{:S(2)}) collective-permute-start(bf16[2,32,896]{2,1,0:T(8,128)(2,1)S(1)} %get-tuple-element.63), channel_id=1, source_target_pairs={{0,2},{1,3},{2,0},{3,1},{4,6},{5,7},{6,4},{7,5},{8,10},{9,11},{10,... | collective-permute-start | bytes 344072 | tf_op jit(solution)/shard_map/ppermute | solution.py:83
  49.5 27.8 %all-to-all-start.2 = ((bf16[16,16,3584]{2,1,0:T(8,128)(2,1)}), bf16[16,16,3584]{2,1,0:T(8,128)(2,1)}, u32[]{:S(2)}, u32[]{:S(2)}) async-start(bf16[16,16,3584]{2,1,0:T(8,128)(2,1)} %bitcast.86), calls=%async_computation.2 | async-start | bytes 3670016 | tf_op jit(solution)/shard_map/all_to_all | solution.py:32
  53.9 5.6 %collective-permute-start.7 = (bf16[2,32,896]{2,1,0:T(8,128)(2,1)S(1)}, bf16[2,32,896]{2,1,0:T(8,128)(2,1)S(1)}, u32[]{:S(2)}, u32[]{:S(2)}) collective-permute-start(bf16[2,32,896]{2,1,0:T(8,128)(2,1)S(1)} %get-tuple-element.61), channel_id=1, source_target_pairs={{0,3},{1,2},{2,1},{3,0},{4,7},{5,6},{6,5},{7,4},{8,11},{9,10},{10,... | collective-permute-start | bytes 344072 | tf_op jit(solution)/shard_map/ppermute | solution.py:83
  60.5 7.4 %collective-permute-start.8 = (bf16[32,896]{1,0:T(8,128)(2,1)S(1)}, bf16[32,896]{1,0:T(8,128)(2,1)S(1)}, u32[]{:S(2)}, u32[]{:S(2)}) collective-permute-start(bf16[32,896]{1,0:T(8,128)(2,1)S(1)} %dynamic-slice_bitcast_fusion.3), channel_id=1, source_target_pairs={{0,4},{1,5},{2,6},{3,7},{4,0},{5,1},{6,2},{7,3},{8,12},{9,13},{10,... | collective-permute-start | bytes 172040 | tf_op jit(solution)/shard_map/ppermute | solution.py:94
  67.9 4.8 %collective-permute-start.9 = (bf16[16,896]{1,0:T(8,128)(2,1)S(1)}, bf16[16,896]{1,0:T(8,128)(2,1)S(1)}, u32[]{:S(2)}, u32[]{:S(2)}) collective-permute-start(bf16[16,896]{1,0:T(8,128)(2,1)S(1)} %get-tuple-element.68), channel_id=1, source_target_pairs={{0,8},{8,0},{1,9},{9,1},{2,10},{10,2},{3,11},{11,3},{4,12},{12,4},... | collective-permute-start | bytes 86024 | tf_op jit(solution)/shard_map/ppermute | solution.py:373
  72.7 6.2 %collective-permute-start.10 = (bf16[2,16,896]{2,1,0:T(8,128)(2,1)S(1)}, bf16[2,16,896]{2,1,0:T(8,128)(2,1)S(1)}, u32[]{:S(2)}, u32[]{:S(2)}) collective-permute-start(bf16[2,16,896]{2,1,0:T(8,128)(2,1)S(1)} %maximum_select_fusion.3), channel_id=1, source_target_pairs={{0,0},{1,32},{2,64},{3,96},{4,128},{5,160},{6,192},{7,224},{8,16},... | collective-permute-start | bytes 172040 | tf_op jit(solution)/shard_map/ppermute | solution.py:374
  80.3 40.5 %all-to-all-start.3 = ((bf16[16,16,3584]{2,1,0:T(8,128)(2,1)}), bf16[16,16,3584]{2,1,0:T(8,128)(2,1)}, u32[]{:S(2)}, u32[]{:S(2)}) async-start(bf16[16,16,3584]{2,1,0:T(8,128)(2,1)} %shard_map.94), calls=%async_computation.3 | async-start | bytes 3670016 | tf_op jit(solution)/shard_map/all_to_all | solution.py:32
  94.7 2.1 %collective-permute-start.11 = (bf16[16,896]{1,0:T(8,128)(2,1)S(1)}, bf16[16,896]{1,0:T(8,128)(2,1)S(1)}, u32[]{:S(2)}, u32[]{:S(2)}) collective-permute-start(bf16[16,896]{1,0:T(8,128)(2,1)S(1)} %get-tuple-element.42), channel_id=1, source_target_pairs={{0,8},{8,0},{1,9},{9,1},{2,10},{10,2},{3,11},{11,3},{4,12},{12,4},... | collective-permute-start | bytes 86024 | tf_op jit(solution)/shard_map/ppermute | solution.py:379
  96.8 7.4 %collective-permute-start.12 = (bf16[2,16,896]{2,1,0:T(8,128)(2,1)S(1)}, bf16[2,16,896]{2,1,0:T(8,128)(2,1)S(1)}, u32[]{:S(2)}, u32[]{:S(2)}) collective-permute-start(bf16[2,16,896]{2,1,0:T(8,128)(2,1)S(1)} %maximum_select_fusion.5), channel_id=1, source_target_pairs={{0,4},{1,5},{2,6},{3,7},{4,0},{5,1},{6,2},{7,3},{8,12},{9,13},{10,... | collective-permute-start | bytes 172040 | tf_op jit(solution)/shard_map/ppermute | solution.py:69
  104.3 26.5 %collective-permute-start.13 = (bf16[2,2,16,896]{3,2,1,0:T(8,128)(2,1)S(1)}, bf16[2,2,16,896]{3,2,1,0:T(8,128)(2,1)S(1)}, u32[]{:S(2)}, u32[]{:S(2)}) collective-permute-start(bf16[2,2,16,896]{3,2,1,0:T(8,128)(2,1)S(1)} %maximum_select_fusion.1), channel_id=1, source_target_pairs={{0,1},{1,0},{2,3},{3,2},{4,5},{5,4},{6,7},{7,6},{8,9},{9,8},{10,11... | collective-permute-start | bytes 344072 | tf_op jit(solution)/shard_map/ppermute | solution.py:72
  104.4 26.5 %collective-permute-start.14 = (bf16[2,2,16,896]{3,2,1,0:T(8,128)(2,1)S(1)}, bf16[2,2,16,896]{3,2,1,0:T(8,128)(2,1)S(1)}, u32[]{:S(2)}, u32[]{:S(2)}) collective-permute-start(bf16[2,2,16,896]{3,2,1,0:T(8,128)(2,1)S(1)} %maximum_select_fusion.1), channel_id=1, source_target_pairs={{0,2},{1,3},{2,0},{3,1},{4,6},{5,7},{6,4},{7,5},{8,10},{9,11},{10,... | collective-permute-start | bytes 344072 | tf_op jit(solution)/shard_map/ppermute | solution.py:72
  105.1 25.8 %collective-permute-start.15 = (bf16[2,2,16,896]{3,2,1,0:T(8,128)(2,1)S(1)}, bf16[2,2,16,896]{3,2,1,0:T(8,128)(2,1)}, u32[]{:S(2)}, u32[]{:S(2)}) collective-permute-start(bf16[2,2,16,896]{3,2,1,0:T(8,128)(2,1)S(1)} %maximum_select_fusion.1), channel_id=1, source_target_pairs={{0,3},{1,2},{2,1},{3,0},{4,7},{5,6},{6,5},{7,4},{8,11},{9,10},{10,... | collective-permute-start | bytes 344072 | tf_op jit(solution)/shard_map/ppermute | solution.py:72
  124.7 15.2 %all-to-all-start.4 = ((bf16[32,8,512]{2,1,0:T(8,128)(2,1)}), bf16[32,8,512]{2,1,0:T(8,128)(2,1)S(1)}, u32[]{:S(2)}, u32[]{:S(2)}) async-start(bf16[32,8,512]{2,1,0:T(8,128)(2,1)} %bitcast.23), calls=%async_computation.4 | async-start | bytes 524288 | tf_op jit(solution)/shard_map/all_to_all | solution.py:32
  139.8 15.1 %all-to-all-start.5 = ((bf16[16,16,896]{2,1,0:T(8,128)(2,1)}), bf16[16,16,896]{2,1,0:T(8,128)(2,1)S(1)}, u32[]{:S(2)}, u32[]{:S(2)}) async-start(bf16[16,16,896]{2,1,0:T(8,128)(2,1)} %bitcast.33), calls=%async_computation.5 | async-start | bytes 917504 | tf_op jit(solution)/shard_map/all_to_all | solution.py:32
  145.0 5.1 %collective-permute-start.16 = (bf16[2,8,1024]{2,1,0:T(8,128)(2,1)S(1)}, bf16[2,8,1024]{2,1,0:T(8,128)(2,1)S(1)}, u32[]{:S(2)}, u32[]{:S(2)}) collective-permute-start(bf16[2,8,1024]{2,1,0:T(8,128)(2,1)S(1)} %get-tuple-element.64), channel_id=1, source_target_pairs={{0,1},{1,0},{2,3},{3,2},{4,5},{5,4},{6,7},{7,6},{8,9},{9,8},{10,11... | collective-permute-start | bytes 98312 | tf_op jit(solution)/shard_map/ppermute | solution.py:83
  145.1 5.0 %collective-permute-start.17 = (bf16[2,8,1024]{2,1,0:T(8,128)(2,1)S(1)}, bf16[2,8,1024]{2,1,0:T(8,128)(2,1)S(1)}, u32[]{:S(2)}, u32[]{:S(2)}) collective-permute-start(bf16[2,8,1024]{2,1,0:T(8,128)(2,1)S(1)} %get-tuple-element.66), channel_id=1, source_target_pairs={{0,2},{1,3},{2,0},{3,1},{4,6},{5,7},{6,4},{7,5},{8,10},{9,11},{10,... | collective-permute-start | bytes 98312 | tf_op jit(solution)/shard_map/ppermute | solution.py:83
  146.4 4.6 %collective-permute-start.18 = (bf16[2,8,1024]{2,1,0:T(8,128)(2,1)S(1)}, bf16[2,8,1024]{2,1,0:T(8,128)(2,1)S(1)}, u32[]{:S(2)}, u32[]{:S(2)}) collective-permute-start(bf16[2,8,1024]{2,1,0:T(8,128)(2,1)S(1)} %get-tuple-element.65), channel_id=1, source_target_pairs={{0,3},{1,2},{2,1},{3,0},{4,7},{5,6},{6,5},{7,4},{8,11},{9,10},{10,... | collective-permute-start | bytes 98312 | tf_op jit(solution)/shard_map/ppermute | solution.py:83
  148.6 17.8 %collective-permute-start.21 = (bf16[256,1792]{1,0:T(8,128)(2,1)}, bf16[256,1792]{1,0:T(8,128)(2,1)S(1)}, u32[]{:S(2)}, u32[]{:S(2)}) collective-permute-start(bf16[256,1792]{1,0:T(8,128)(2,1)} %copy-done.2), channel_id=1, source_target_pairs={{0,8},{8,0},{1,9},{9,1},{2,10},{10,2},{3,11},{11,3},{4,12},{12,4},... | collective-permute-start | bytes 2752520 | tf_op jit(solution)/shard_map/ppermute | solution.py:398
  150.1 16.3 %collective-permute-start.20 = (bf16[256,1792]{1,0:T(8,128)(2,1)}, bf16[256,1792]{1,0:T(8,128)(2,1)}, u32[]{:S(2)}, u32[]{:S(2)}) collective-permute-start(bf16[256,1792]{1,0:T(8,128)(2,1)} %copy-done.1), channel_id=1, source_target_pairs={{0,8},{8,0},{1,9},{9,1},{2,10},{10,2},{3,11},{11,3},{4,12},{12,4},... | collective-permute-start | bytes 2752520 | tf_op jit(solution)/shard_map/ppermute | solution.py:397
  151.0 11.7 %collective-permute-start.19 = (bf16[8,1024]{1,0:T(8,128)(2,1)S(1)}, bf16[8,1024]{1,0:T(8,128)(2,1)S(1)}, u32[]{:S(2)}, u32[]{:S(2)}) collective-permute-start(bf16[8,1024]{1,0:T(8,128)(2,1)S(1)} %dynamic-slice_bitcast_fusion.8), channel_id=1, source_target_pairs={{0,4},{1,5},{2,6},{3,7},{4,0},{5,1},{6,2},{7,3},{8,12},{9,13},{10,... | collective-permute-start | bytes 49160 | tf_op jit(solution)/shard_map/ppermute | solution.py:94
  156.4 17.9 %all-to-all-start.6 = ((bf16[32,8,1024]{2,1,0:T(8,128)(2,1)}), bf16[32,8,1024]{2,1,0:T(8,128)(2,1)S(1)}, u32[]{:S(2)}, u32[]{:S(2)}) async-start(bf16[32,8,1024]{2,1,0:T(8,128)(2,1)} %fusion), calls=%async_computation.6 | async-start | bytes 1048576 | tf_op jit(solution)/shard_map/all_to_all | solution.py:32
  (5 other events, 10.3 us)

commit v5 on v4

--- a/solution.py
+++ b/solution.py
@@ -391,6 +391,7 @@
     own, got = near_exchange(terms)
 
     output = times(hidden_panel, down_weight).astype(BF16).reshape(ROWS, few, width)
+    own, output = lax.optimization_barrier((own, output))
     output = exchange(output, ROW)
     grad_tokens = far_exchange(own, got)
 

time: 176 us -> 175 us (level)
  starting transfers between devices: 83.8 us -> 81.8 us
  transfers between devices with their start and end apart: 29 -> 29, of which waited for: 15 -> 14; matrix products, arithmetic and copies ran while one was open for 9% -> 9% of each run, Pallas kernels for 9% -> 9%
where the time goes in v5:
time: 175 us; the launch traced here: 174 us
  starting transfers between devices  81.8 us (47%)
  waiting for transfers between devices  56.4 us (32%)
  Pallas kernels  16.5 us (9%)
  local copies, waits for them, and re-layouts  8.27 us (5%)
  matrix products  5.32 us (3%)
  other arithmetic  5.11 us (3%)
    all_to_all x7, starting transfers between devices, exchange(): return lax.all_to_all(blocks, axis, split_axis=0, concat_axis=0, tiled=True)  50.1 us
    all_to_all x7, waiting for transfers between devices, exchange(): return lax.all_to_all(blocks, axis, split_axis=0, concat_axis=0, tiled=True)  30.2 us
    pallas_call x6, Pallas kernels, call(): pl.pallas_call(body, grid_spec=pltpu.PrefetchScalarGridSpec(num_scalar_pr...  16.5 us
    ppermute x3, starting transfers between devices, gather_columns(): got = lax.ppermute(share, 'z', pairs(distance))  9.92 us
    ppermute x6, waiting for transfers between devices, near_exchange(): return (near[0], [lax.ppermute(near[d], 'z', pairs(d)) for d in (1, 2, 3)])  7.66 us
    ppermute x6, starting transfers between devices, near_exchange(): return (near[0], [lax.ppermute(near[d], 'z', pairs(d)) for d in (1, 2, 3)])  7.33 us
    ppermute x1, waiting for transfers between devices, gather_hidden(): got = lax.ppermute(block, 'z', pairs(4))  7.3 us
    ppermute x2, waiting for transfers between devices, far_exchange(): far = lax.ppermute(send, 'z', pairs(4))  6.86 us
  transfers between devices with their start and end apart: 29, of which 14 were waited for; matrix products, arithmetic and copies ran while one was open for 9% of the time, Pallas kernels for 9%

profile of v5, /device:TPU:1, one launch (start us, length us, event | category | flops | bytes accessed | tf_op | source)
XLA Modules:
  0.0 174.4 jit_solution(11192874135962432732)
XLA Ops:
  0.6 7.8 %collective-permute-start = (bf16[1,1,1,8,1024]{4,3,2,1,0:T(8,128)(2,1)}, bf16[1,1,1,8,1024]{4,3,2,1,0:T(8,128)(2,1)S(1)}, u32[]{:S(2)}, u32[]{:S(2)}) collective-permute-start(bf16[1,1,1,8,1024]{4,3,2,1,0:T(8,128)(2,1)} %bitcast.100), channel_id=1, source_target_pairs={{0,4},{1,5},{2,6},{3,7},{4,0},{5,1},{6,2},{7,3},{8,12},{9,13},{10,... | collective-permute-start | bytes 49160 | tf_op jit(solution)/shard_map/ppermute | solution.py:51
  8.5 1.6 broadcast_in_dim.19
  10.0 8.0 %all-to-all-start = ((bf16[32,8,1024]{2,1,0:T(8,128)(2,1)}), bf16[32,8,1024]{2,1,0:T(8,128)(2,1)S(1)}, u32[]{:S(2)}, u32[]{:S(2)}) async-start(bf16[32,8,1024]{2,1,0:T(8,128)(2,1)} %broadcast_in_dim.19), calls=%async_computation | async-start | bytes 1048576 | tf_op jit(solution)/shard_map/all_to_all | solution.py:32
  20.3 2.2 %constant_dynamic-slice_fusion.2 = bf16[256,1792]{1,0:T(8,128)(2,1)} fusion(bf16[256,3584]{1,0:T(8,128)(2,1)} %gate_mine.3, s32[]{:T(128)S(6)} %select_n.253), kind=kLoop, calls=%fused_computation.44 | loop fusion | bytes 1835012 | tf_op jit(solution)/shard_map/dynamic_slice | solution.py:348
  24.9 2.7 %collective-permute-done.2 = bf16[2,2,1,8,1024]{4,3,2,1,0:T(8,128)(2,1)S(1)} collective-permute-done((bf16[2,2,1,8,1024]{4,3,2,1,0:T(8,128)(2,1)S(1)}, bf16[2,2,1,8,1024]{4,3,2,1,0:T(8,128)(2,1)S(1)}, u32[]{:S(2)}, u32[]{:S(2)}) %collective-permute-start.2) | collective-permute-done | bytes 65568 | tf_op jit(solution)/shard_map/ppermute | solution.py:51
  27.6 2.1 %all-to-all-done = bf16[32,8,1024]{2,1,0:T(8,128)(2,1)S(1)} async-done(((bf16[32,8,1024]{2,1,0:T(8,128)(2,1)}), bf16[32,8,1024]{2,1,0:T(8,128)(2,1)S(1)}, u32[]{:S(2)}, u32[]{:S(2)}) %all-to-all-start) | async-done | bytes 524320 | tf_op jit(solution)/shard_map/all_to_all | solution.py:32
  30.4 6.4 %all-to-all-start.1 = ((bf16[32,8,512]{2,1,0:T(8,128)(2,1)}), bf16[32,8,512]{2,1,0:T(8,128)(2,1)S(1)}, u32[]{:S(2)}, u32[]{:S(2)}) async-start(bf16[32,8,512]{2,1,0:T(8,128)(2,1)} %bitcast.90), calls=%async_computation.1 | async-start | bytes 524288 | tf_op jit(solution)/shard_map/all_to_all | solution.py:32
  39.7 3.7 %collective-permute-done.4 = bf16[2,32,896]{2,1,0:T(8,128)(2,1)S(1)} collective-permute-done((bf16[2,32,896]{2,1,0:T(8,128)(2,1)S(1)}, bf16[2,32,896]{2,1,0:T(8,128)(2,1)S(1)}, u32[]{:S(2)}, u32[]{:S(2)}) %collective-permute-start.4) | collective-permute-done | bytes 114720 | tf_op jit(solution)/shard_map/ppermute | solution.py:83
  43.4 2.3 %all-to-all-done.1 = bf16[32,8,512]{2,1,0:T(8,128)(2,1)S(1)} async-done(((bf16[32,8,512]{2,1,0:T(8,128)(2,1)}), bf16[32,8,512]{2,1,0:T(8,128)(2,1)S(1)}, u32[]{:S(2)}, u32[]{:S(2)}) %all-to-all-start.1) | async-done | bytes 262176 | tf_op jit(solution)/shard_map/all_to_all | solution.py:32
  45.8 3.7 %shard_map.92 = bf16[256,3584]{1,0:T(8,128)(2,1)} custom-call(s32[1]{0:T(128)} %bitcast.core, bf16[256,512]{1,0:T(8,128)(2,1)S(1)} %bitcast.81, bf16[256,3584]{1,0:T(8,128)(2,1)} %gate_mine.3, bf16[256,1792]{1,0:T(8,128)(2,1)S(1)} %collective-permute-done.5.gate_other, bf16[256,3584]{1,0:T(8,128)(2,1)} %up_mine.3, ...), custom_call_target="tpu_custom_call" | custom-call | flops 939524096 | bytes 5767168 | tf_op jit(solution)/shard_map/pallas_call | solution.py:118
  49.5 4.4 %all-to-all-start.2 = ((bf16[16,16,3584]{2,1,0:T(8,128)(2,1)}), bf16[16,16,3584]{2,1,0:T(8,128)(2,1)}, u32[]{:S(2)}, u32[]{:S(2)}) async-start(bf16[16,16,3584]{2,1,0:T(8,128)(2,1)} %bitcast.85), calls=%async_computation.2 | async-start | bytes 3670016 | tf_op jit(solution)/shard_map/all_to_all | solution.py:32
  53.9 1.7 collective-permute-start.7
  55.6 3.9 %collective-permute-done.7 = bf16[2,32,896]{2,1,0:T(8,128)(2,1)S(1)} collective-permute-done((bf16[2,32,896]{2,1,0:T(8,128)(2,1)S(1)}, bf16[2,32,896]{2,1,0:T(8,128)(2,1)S(1)}, u32[]{:S(2)}, u32[]{:S(2)}) %collective-permute-start.7) | collective-permute-done | bytes 114720 | tf_op jit(solution)/shard_map/ppermute | solution.py:83
  61.0 6.9 %collective-permute-done.8 = bf16[32,896]{1,0:T(8,128)(2,1)S(1)} collective-permute-done((bf16[32,896]{1,0:T(8,128)(2,1)S(1)}, bf16[32,896]{1,0:T(8,128)(2,1)S(1)}, u32[]{:S(2)}, u32[]{:S(2)}) %collective-permute-start.8) | collective-permute-done | bytes 57376 | tf_op jit(solution)/shard_map/ppermute | solution.py:94
  67.9 3.9 %collective-permute-start.9 = (bf16[16,896]{1,0:T(8,128)(2,1)S(1)}, bf16[16,896]{1,0:T(8,128)(2,1)S(1)}, u32[]{:S(2)}, u32[]{:S(2)}) collective-permute-start(bf16[16,896]{1,0:T(8,128)(2,1)S(1)} %get-tuple-element.73), channel_id=1, source_target_pairs={{0,8},{8,0},{1,9},{9,1},{2,10},{10,2},{3,11},{11,3},{4,12},{12,4},... | collective-permute-start | bytes 86024 | tf_op jit(solution)/shard_map/ppermute | solution.py:373
  72.7 3.7 %collective-permute-start.10 = (bf16[2,16,896]{2,1,0:T(8,128)(2,1)S(1)}, bf16[2,16,896]{2,1,0:T(8,128)(2,1)S(1)}, u32[]{:S(2)}, u32[]{:S(2)}) collective-permute-start(bf16[2,16,896]{2,1,0:T(8,128)(2,1)S(1)} %maximum_select_fusion.3), channel_id=1, source_target_pairs={{0,0},{1,32},{2,64},{3,96},{4,128},{5,160},{6,192},{7,224},{8,16},... | collective-permute-start | bytes 172040 | tf_op jit(solution)/shard_map/ppermute | solution.py:374
  77.2 1.6 shard_map.93
  80.3 14.4 %all-to-all-start.3 = ((bf16[16,16,3584]{2,1,0:T(8,128)(2,1)}), bf16[16,16,3584]{2,1,0:T(8,128)(2,1)}, u32[]{:S(2)}, u32[]{:S(2)}) async-start(bf16[16,16,3584]{2,1,0:T(8,128)(2,1)} %shard_map.94), calls=%async_computation.3 | async-start | bytes 3670016 | tf_op jit(solution)/shard_map/all_to_all | solution.py:32
  96.9 7.3 %collective-permute-done.12 = bf16[2,16,896]{2,1,0:T(8,128)(2,1)S(1)} collective-permute-done((bf16[2,16,896]{2,1,0:T(8,128)(2,1)S(1)}, bf16[2,16,896]{2,1,0:T(8,128)(2,1)S(1)}, u32[]{:S(2)}, u32[]{:S(2)}) %collective-permute-start.12) | collective-permute-done | bytes 57376 | tf_op jit(solution)/shard_map/ppermute | solution.py:69
  105.6 2.8 %collective-permute-start.15 = (bf16[2,2,16,896]{3,2,1,0:T(8,128)(2,1)}, bf16[2,2,16,896]{3,2,1,0:T(8,128)(2,1)}, u32[]{:S(2)}, u32[]{:S(2)}) collective-permute-start(bf16[2,2,16,896]{3,2,1,0:T(8,128)(2,1)} %maximum_select_fusion.1), channel_id=1, source_target_pairs={{0,3},{1,2},{2,1},{3,0},{4,7},{5,6},{6,5},{7,4},{8,11},{9,10},{10,... | collective-permute-start | bytes 344072 | tf_op jit(solution)/shard_map/ppermute | solution.py:72
  108.5 12.3 %all-to-all-done.3 = bf16[16,16,3584]{2,1,0:T(8,128)(2,1)} async-done(((bf16[16,16,3584]{2,1,0:T(8,128)(2,1)}), bf16[16,16,3584]{2,1,0:T(8,128)(2,1)}, u32[]{:S(2)}, u32[]{:S(2)}) %all-to-all-start.3) | async-done | bytes 1835040 | tf_op jit(solution)/shard_map/all_to_all | solution.py:32
  120.8 3.9 %shard_map.95 = bf16[256,512]{1,0:T(8,128)(2,1)} custom-call(s32[1]{0:T(128)} %bitcast.core, bf16[256,3584]{1,0:T(8,128)(2,1)} %bitcast.22.piece, bf16[256,3584]{1,0:T(8,128)(2,1)} %gate_mine.3, bf16[256,1792]{1,0:T(8,128)(2,1)S(1)} %collective-permute-done.5.gate_other, bf16[256,3584]{1,0:T(8,128)(2,1)} %up_mine.3, ...), custom_call_target="tpu_custom_call" | custom-call | flops 939524096 | bytes 7340032 | tf_op jit(solution)/shard_map/pallas_call | solution.py:118
  124.7 6.1 %all-to-all-start.4 = ((bf16[32,8,512]{2,1,0:T(8,128)(2,1)}), bf16[32,8,512]{2,1,0:T(8,128)(2,1)S(1)}, u32[]{:S(2)}, u32[]{:S(2)}) async-start(bf16[32,8,512]{2,1,0:T(8,128)(2,1)} %bitcast.23), calls=%async_computation.4 | async-start | bytes 524288 | tf_op jit(solution)/shard_map/all_to_all | solution.py:32
  132.8 3.6 %shard_map.96 = (bf16[256,3584]{1,0:T(8,128)(2,1)}, bf16[256,3584]{1,0:T(8,128)(2,1)}, bf16[256,1792]{1,0:T(8,128)(2,1)S(1)}, bf16[256,1792]{1,0:T(8,128)(2,1)S(1)}) custom-call(s32[1]{0:T(128)} %bitcast.core, bf16[256,512]{1,0:T(8,128)(2,1)S(1)} %bitcast.82, bf16[256,3584]{1,0:T(8,128)(2,1)} %bitcast.22.piece), custom_call_target="tpu_custom_call" | custom-call | flops 939524096 | bytes 2097152 | tf_op jit(solution)/shard_map/pallas_call | solution.py:118
  138.2 1.6 all-to-all-done.4
  139.8 5.2 %all-to-all-start.5 = ((bf16[16,16,896]{2,1,0:T(8,128)(2,1)}), bf16[16,16,896]{2,1,0:T(8,128)(2,1)S(1)}, u32[]{:S(2)}, u32[]{:S(2)}) async-start(bf16[16,16,896]{2,1,0:T(8,128)(2,1)} %bitcast.33), calls=%async_computation.5 | async-start | bytes 917504 | tf_op jit(solution)/shard_map/all_to_all | solution.py:32
  147.4 2.2 %collective-permute-start.18 = (bf16[2,8,1024]{2,1,0:T(8,128)(2,1)S(1)}, bf16[2,8,1024]{2,1,0:T(8,128)(2,1)S(1)}, u32[]{:S(2)}, u32[]{:S(2)}) collective-permute-start(bf16[2,8,1024]{2,1,0:T(8,128)(2,1)S(1)} %get-tuple-element.69), channel_id=1, source_target_pairs={{0,3},{1,2},{2,1},{3,0},{4,7},{5,6},{6,5},{7,4},{8,11},{9,10},{10,... | collective-permute-start | bytes 98312 | tf_op jit(solution)/shard_map/ppermute | solution.py:83
  149.6 5.4 %all-to-all-done.5 = bf16[16,16,896]{2,1,0:T(8,128)(2,1)S(1)} async-done(((bf16[16,16,896]{2,1,0:T(8,128)(2,1)}), bf16[16,16,896]{2,1,0:T(8,128)(2,1)S(1)}, u32[]{:S(2)}, u32[]{:S(2)}) %all-to-all-start.5) | async-done | bytes 458784 | tf_op jit(solution)/shard_map/all_to_all | solution.py:32
  156.7 5.4 %all-to-all-start.6 = ((bf16[32,8,1024]{2,1,0:T(8,128)(2,1)}), bf16[32,8,1024]{2,1,0:T(8,128)(2,1)S(1)}, u32[]{:S(2)}, u32[]{:S(2)}) async-start(bf16[32,8,1024]{2,1,0:T(8,128)(2,1)} %fusion), calls=%async_computation.6 | async-start | bytes 1048576 | tf_op jit(solution)/shard_map/all_to_all | solution.py:32
  162.0 3.1 %convolution_convert_fusion = bf16[896,1024]{1,0:T(8,128)(2,1)} fusion(bf16[256,896]{1,0:T(8,128)(2,1)} %bitcast.89, bf16[256,1024]{1,0:T(8,128)(2,1)} %bitcast.87), kind=kOutput, calls=%fused_computation | convolution fusion | flops 470679552 | bytes 2818048 | tf_op jit(solution)/shard_map/dot_general | solution.py:24
  165.7 2.3 %shard_map.97 = (bf16[256,3584]{1,0:T(8,128)(2,1)}, bf16[256,3584]{1,0:T(8,128)(2,1)}) custom-call(s32[1]{0:T(128)} %bitcast.core, bf16[256,3584]{1,0:T(8,128)(2,1)} %get-tuple-element.50._, bf16[256,3584]{1,0:T(8,128)(2,1)} %get-tuple-element.51.__, ...), custom_call_target="tpu_custom_call", output_to_operand_aliasing={{0}: (1, {}), {1}: (2, {})} | custom-call | bytes 5505024 | tf_op jit(solution)/shard_map/pallas_call | solution.py:118
  168.1 5.6 %all-to-all-done.6 = bf16[32,8,1024]{2,1,0:T(8,128)(2,1)S(1)} async-done(((bf16[32,8,1024]{2,1,0:T(8,128)(2,1)}), bf16[32,8,1024]{2,1,0:T(8,128)(2,1)S(1)}, u32[]{:S(2)}, u32[]{:S(2)}) %all-to-all-start.6) | async-done | bytes 524320 | tf_op jit(solution)/shard_map/all_to_all | solution.py:32
  (77 shorter events, 25.4 us)
Async XLA Ops:
  0.6 36.2 %copy-start = (bf16[896,1024]{1,0:T(8,128)(2,1)S(1)}, bf16[896,1024]{1,0:T(8,128)(2,1)}, u32[]{:S(2)}) copy-start(bf16[896,1024]{1,0:T(8,128)(2,1)} %param.8) | copy-start | bytes 5505028
  0.6 17.5 %collective-permute-start = (bf16[1,1,1,8,1024]{4,3,2,1,0:T(8,128)(2,1)}, bf16[1,1,1,8,1024]{4,3,2,1,0:T(8,128)(2,1)S(1)}, u32[]{:S(2)}, u32[]{:S(2)}) collective-permute-start(bf16[1,1,1,8,1024]{4,3,2,1,0:T(8,128)(2,1)} %bitcast.100), channel_id=1, source_target_pairs={{0,4},{1,5},{2,6},{3,7},{4,0},{5,1},{6,2},{7,3},{8,12},{9,13},{10,... | collective-permute-start | bytes 49160 | tf_op jit(solution)/shard_map/ppermute | solution.py:51
  10.0 19.6 %all-to-all-start = ((bf16[32,8,1024]{2,1,0:T(8,128)(2,1)}), bf16[32,8,1024]{2,1,0:T(8,128)(2,1)S(1)}, u32[]{:S(2)}, u32[]{:S(2)}) async-start(bf16[32,8,1024]{2,1,0:T(8,128)(2,1)} %broadcast_in_dim.19), calls=%async_computation | async-start | bytes 1048576 | tf_op jit(solution)/shard_map/all_to_all | solution.py:32
  19.0 4.9 %copy-start.7 = (bf16[8,1024]{1,0:T(8,128)(2,1)S(1)}, bf16[8,1024]{1,0:T(8,128)(2,1)}, u32[]{:S(2)}) copy-start(bf16[8,1024]{1,0:T(8,128)(2,1)} %param.5) | copy-start | bytes 49156
  19.1 5.0 %collective-permute-start.1 = (bf16[2,1,1,8,1024]{4,3,2,1,0:T(8,128)(2,1)S(1)}, bf16[2,1,1,8,1024]{4,3,2,1,0:T(8,128)(2,1)S(1)}, u32[]{:S(2)}, u32[]{:S(2)}) collective-permute-start(bf16[2,1,1,8,1024]{4,3,2,1,0:T(8,128)(2,1)S(1)} %maximum_select_fusion.7), channel_id=1, source_target_pairs={{0,2},{1,3},{2,0},{3,1},{4,6},{5,7},{6,4},{7,5},{8,10},{9,11},{10,... | collective-permute-start | bytes 98312 | tf_op jit(solution)/shard_map/ppermute | solution.py:51
  22.5 23.3 %collective-permute-start.5 = (bf16[256,1792]{1,0:T(8,128)(2,1)}, bf16[256,1792]{1,0:T(8,128)(2,1)S(1)}, u32[]{:S(2)}, u32[]{:S(2)}) collective-permute-start(bf16[256,1792]{1,0:T(8,128)(2,1)} %constant_dynamic-slice_fusion.2), channel_id=1, source_target_pairs={{0,8},{8,0},{1,9},{9,1},{2,10},{10,2},{3,11},{11,3},{4,12},{12,4},... | collective-permute-start | bytes 2752520 | tf_op jit(solution)/shard_map/ppermute | solution.py:349
  24.0 21.8 %collective-permute-start.6 = (bf16[256,1792]{1,0:T(8,128)(2,1)}, bf16[256,1792]{1,0:T(8,128)(2,1)}, u32[]{:S(2)}, u32[]{:S(2)}) collective-permute-start(bf16[256,1792]{1,0:T(8,128)(2,1)} %constant_dynamic-slice_fusion.1), channel_id=1, source_target_pairs={{0,8},{8,0},{1,9},{9,1},{2,10},{10,2},{3,11},{11,3},{4,12},{12,4},... | collective-permute-start | bytes 2752520 | tf_op jit(solution)/shard_map/ppermute | solution.py:349
  24.0 3.5 %collective-permute-start.2 = (bf16[2,2,1,8,1024]{4,3,2,1,0:T(8,128)(2,1)S(1)}, bf16[2,2,1,8,1024]{4,3,2,1,0:T(8,128)(2,1)S(1)}, u32[]{:S(2)}, u32[]{:S(2)}) collective-permute-start(bf16[2,2,1,8,1024]{4,3,2,1,0:T(8,128)(2,1)S(1)} %maximum_select_fusion.2), channel_id=1, source_target_pairs={{0,1},{1,0},{2,3},{3,2},{4,5},{5,4},{6,7},{7,6},{8,9},{9,8},{10,11... | collective-permute-start | bytes 196616 | tf_op jit(solution)/shard_map/ppermute | solution.py:51
  29.6 8.0 %copy-start.4 = (bf16[32,8,1024]{2,1,0:T(8,128)(2,1)}, bf16[32,8,1024]{2,1,0:T(8,128)(2,1)S(1)}, u32[]{:S(2)}) copy-start(bf16[32,8,1024]{2,1,0:T(8,128)(2,1)S(1)} %all-to-all-done) | copy-start | bytes 1572868
  30.4 15.4 %all-to-all-start.1 = ((bf16[32,8,512]{2,1,0:T(8,128)(2,1)}), bf16[32,8,512]{2,1,0:T(8,128)(2,1)S(1)}, u32[]{:S(2)}, u32[]{:S(2)}) async-start(bf16[32,8,512]{2,1,0:T(8,128)(2,1)} %bitcast.90), calls=%async_computation.1 | async-start | bytes 524288 | tf_op jit(solution)/shard_map/all_to_all | solution.py:32
  37.7 5.7 %collective-permute-start.4 = (bf16[2,32,896]{2,1,0:T(8,128)(2,1)S(1)}, bf16[2,32,896]{2,1,0:T(8,128)(2,1)S(1)}, u32[]{:S(2)}, u32[]{:S(2)}) collective-permute-start(bf16[2,32,896]{2,1,0:T(8,128)(2,1)S(1)} %get-tuple-element.66), channel_id=1, source_target_pairs={{0,1},{1,0},{2,3},{3,2},{4,5},{5,4},{6,7},{7,6},{8,9},{9,8},{10,11... | collective-permute-start | bytes 344072 | tf_op jit(solution)/shard_map/ppermute | solution.py:83
  38.5 11.0 %collective-permute-start.3 = (bf16[2,32,896]{2,1,0:T(8,128)(2,1)S(1)}, bf16[2,32,896]{2,1,0:T(8,128)(2,1)S(1)}, u32[]{:S(2)}, u32[]{:S(2)}) collective-permute-start(bf16[2,32,896]{2,1,0:T(8,128)(2,1)S(1)} %get-tuple-element.67), channel_id=1, source_target_pairs={{0,2},{1,3},{2,0},{3,1},{4,6},{5,7},{6,4},{7,5},{8,10},{9,11},{10,... | collective-permute-start | bytes 344072 | tf_op jit(solution)/shard_map/ppermute | solution.py:83
  49.5 27.8 %all-to-all-start.2 = ((bf16[16,16,3584]{2,1,0:T(8,128)(2,1)}), bf16[16,16,3584]{2,1,0:T(8,128)(2,1)}, u32[]{:S(2)}, u32[]{:S(2)}) async-start(bf16[16,16,3584]{2,1,0:T(8,128)(2,1)} %bitcast.85), calls=%async_computation.2 | async-start | bytes 3670016 | tf_op jit(solution)/shard_map/all_to_all | solution.py:32
  53.9 5.6 %collective-permute-start.7 = (bf16[2,32,896]{2,1,0:T(8,128)(2,1)S(1)}, bf16[2,32,896]{2,1,0:T(8,128)(2,1)S(1)}, u32[]{:S(2)}, u32[]{:S(2)}) collective-permute-start(bf16[2,32,896]{2,1,0:T(8,128)(2,1)S(1)} %get-tuple-element.65), channel_id=1, source_target_pairs={{0,3},{1,2},{2,1},{3,0},{4,7},{5,6},{6,5},{7,4},{8,11},{9,10},{10,... | collective-permute-start | bytes 344072 | tf_op jit(solution)/shard_map/ppermute | solution.py:83
  60.5 7.4 %collective-permute-start.8 = (bf16[32,896]{1,0:T(8,128)(2,1)S(1)}, bf16[32,896]{1,0:T(8,128)(2,1)S(1)}, u32[]{:S(2)}, u32[]{:S(2)}) collective-permute-start(bf16[32,896]{1,0:T(8,128)(2,1)S(1)} %dynamic-slice_bitcast_fusion.3), channel_id=1, source_target_pairs={{0,4},{1,5},{2,6},{3,7},{4,0},{5,1},{6,2},{7,3},{8,12},{9,13},{10,... | collective-permute-start | bytes 172040 | tf_op jit(solution)/shard_map/ppermute | solution.py:94
  67.9 4.8 %collective-permute-start.9 = (bf16[16,896]{1,0:T(8,128)(2,1)S(1)}, bf16[16,896]{1,0:T(8,128)(2,1)S(1)}, u32[]{:S(2)}, u32[]{:S(2)}) collective-permute-start(bf16[16,896]{1,0:T(8,128)(2,1)S(1)} %get-tuple-element.73), channel_id=1, source_target_pairs={{0,8},{8,0},{1,9},{9,1},{2,10},{10,2},{3,11},{11,3},{4,12},{12,4},... | collective-permute-start | bytes 86024 | tf_op jit(solution)/shard_map/ppermute | solution.py:373
  72.7 6.2 %collective-permute-start.10 = (bf16[2,16,896]{2,1,0:T(8,128)(2,1)S(1)}, bf16[2,16,896]{2,1,0:T(8,128)(2,1)S(1)}, u32[]{:S(2)}, u32[]{:S(2)}) collective-permute-start(bf16[2,16,896]{2,1,0:T(8,128)(2,1)S(1)} %maximum_select_fusion.3), channel_id=1, source_target_pairs={{0,0},{1,32},{2,64},{3,96},{4,128},{5,160},{6,192},{7,224},{8,16},... | collective-permute-start | bytes 172040 | tf_op jit(solution)/shard_map/ppermute | solution.py:374
  80.3 40.5 %all-to-all-start.3 = ((bf16[16,16,3584]{2,1,0:T(8,128)(2,1)}), bf16[16,16,3584]{2,1,0:T(8,128)(2,1)}, u32[]{:S(2)}, u32[]{:S(2)}) async-start(bf16[16,16,3584]{2,1,0:T(8,128)(2,1)} %shard_map.94), calls=%async_computation.3 | async-start | bytes 3670016 | tf_op jit(solution)/shard_map/all_to_all | solution.py:32
  94.7 2.1 %collective-permute-start.11 = (bf16[16,896]{1,0:T(8,128)(2,1)S(1)}, bf16[16,896]{1,0:T(8,128)(2,1)S(1)}, u32[]{:S(2)}, u32[]{:S(2)}) collective-permute-start(bf16[16,896]{1,0:T(8,128)(2,1)S(1)} %get-tuple-element.44), channel_id=1, source_target_pairs={{0,8},{8,0},{1,9},{9,1},{2,10},{10,2},{3,11},{11,3},{4,12},{12,4},... | collective-permute-start | bytes 86024 | tf_op jit(solution)/shard_map/ppermute | solution.py:379
  96.8 7.4 %collective-permute-start.12 = (bf16[2,16,896]{2,1,0:T(8,128)(2,1)S(1)}, bf16[2,16,896]{2,1,0:T(8,128)(2,1)S(1)}, u32[]{:S(2)}, u32[]{:S(2)}) collective-permute-start(bf16[2,16,896]{2,1,0:T(8,128)(2,1)S(1)} %maximum_select_fusion.5), channel_id=1, source_target_pairs={{0,4},{1,5},{2,6},{3,7},{4,0},{5,1},{6,2},{7,3},{8,12},{9,13},{10,... | collective-permute-start | bytes 172040 | tf_op jit(solution)/shard_map/ppermute | solution.py:69
  104.9 25.9 %collective-permute-start.13 = (bf16[2,2,16,896]{3,2,1,0:T(8,128)(2,1)}, bf16[2,2,16,896]{3,2,1,0:T(8,128)(2,1)}, u32[]{:S(2)}, u32[]{:S(2)}) collective-permute-start(bf16[2,2,16,896]{3,2,1,0:T(8,128)(2,1)} %maximum_select_fusion.1), channel_id=1, source_target_pairs={{0,1},{1,0},{2,3},{3,2},{4,5},{5,4},{6,7},{7,6},{8,9},{9,8},{10,11... | collective-permute-start | bytes 344072 | tf_op jit(solution)/shard_map/ppermute | solution.py:72
  104.9 25.9 %collective-permute-start.14 = (bf16[2,2,16,896]{3,2,1,0:T(8,128)(2,1)}, bf16[2,2,16,896]{3,2,1,0:T(8,128)(2,1)}, u32[]{:S(2)}, u32[]{:S(2)}) collective-permute-start(bf16[2,2,16,896]{3,2,1,0:T(8,128)(2,1)} %maximum_select_fusion.1), channel_id=1, source_target_pairs={{0,2},{1,3},{2,0},{3,1},{4,6},{5,7},{6,4},{7,5},{8,10},{9,11},{10,... | collective-permute-start | bytes 344072 | tf_op jit(solution)/shard_map/ppermute | solution.py:72
  105.6 25.2 %collective-permute-start.15 = (bf16[2,2,16,896]{3,2,1,0:T(8,128)(2,1)}, bf16[2,2,16,896]{3,2,1,0:T(8,128)(2,1)}, u32[]{:S(2)}, u32[]{:S(2)}) collective-permute-start(bf16[2,2,16,896]{3,2,1,0:T(8,128)(2,1)} %maximum_select_fusion.1), channel_id=1, source_target_pairs={{0,3},{1,2},{2,1},{3,0},{4,7},{5,6},{6,5},{7,4},{8,11},{9,10},{10,... | collective-permute-start | bytes 344072 | tf_op jit(solution)/shard_map/ppermute | solution.py:72
  124.7 15.2 %all-to-all-start.4 = ((bf16[32,8,512]{2,1,0:T(8,128)(2,1)}), bf16[32,8,512]{2,1,0:T(8,128)(2,1)S(1)}, u32[]{:S(2)}, u32[]{:S(2)}) async-start(bf16[32,8,512]{2,1,0:T(8,128)(2,1)} %bitcast.23), calls=%async_computation.4 | async-start | bytes 524288 | tf_op jit(solution)/shard_map/all_to_all | solution.py:32
  139.8 15.2 %all-to-all-start.5 = ((bf16[16,16,896]{2,1,0:T(8,128)(2,1)}), bf16[16,16,896]{2,1,0:T(8,128)(2,1)S(1)}, u32[]{:S(2)}, u32[]{:S(2)}) async-start(bf16[16,16,896]{2,1,0:T(8,128)(2,1)} %bitcast.33), calls=%async_computation.5 | async-start | bytes 917504 | tf_op jit(solution)/shard_map/all_to_all | solution.py:32
  145.1 20.7 %collective-permute-start.21 = (bf16[256,1792]{1,0:T(8,128)(2,1)}, bf16[256,1792]{1,0:T(8,128)(2,1)S(1)}, u32[]{:S(2)}, u32[]{:S(2)}) collective-permute-start(bf16[256,1792]{1,0:T(8,128)(2,1)} %copy-done.2), channel_id=1, source_target_pairs={{0,8},{8,0},{1,9},{9,1},{2,10},{10,2},{3,11},{11,3},{4,12},{12,4},... | collective-permute-start | bytes 2752520 | tf_op jit(solution)/shard_map/ppermute | solution.py:399
  145.8 19.9 %collective-permute-start.20 = (bf16[256,1792]{1,0:T(8,128)(2,1)}, bf16[256,1792]{1,0:T(8,128)(2,1)}, u32[]{:S(2)}, u32[]{:S(2)}) collective-permute-start(bf16[256,1792]{1,0:T(8,128)(2,1)} %copy-done.1), channel_id=1, source_target_pairs={{0,8},{8,0},{1,9},{9,1},{2,10},{10,2},{3,11},{11,3},{4,12},{12,4},... | collective-permute-start | bytes 2752520 | tf_op jit(solution)/shard_map/ppermute | solution.py:398
  146.0 10.5 %collective-permute-start.16 = (bf16[2,8,1024]{2,1,0:T(8,128)(2,1)S(1)}, bf16[2,8,1024]{2,1,0:T(8,128)(2,1)S(1)}, u32[]{:S(2)}, u32[]{:S(2)}) collective-permute-start(bf16[2,8,1024]{2,1,0:T(8,128)(2,1)S(1)} %get-tuple-element.68), channel_id=1, source_target_pairs={{0,1},{1,0},{2,3},{3,2},{4,5},{5,4},{6,7},{7,6},{8,9},{9,8},{10,11... | collective-permute-start | bytes 98312 | tf_op jit(solution)/shard_map/ppermute | solution.py:83
  146.1 10.4 %collective-permute-start.17 = (bf16[2,8,1024]{2,1,0:T(8,128)(2,1)S(1)}, bf16[2,8,1024]{2,1,0:T(8,128)(2,1)S(1)}, u32[]{:S(2)}, u32[]{:S(2)}) collective-permute-start(bf16[2,8,1024]{2,1,0:T(8,128)(2,1)S(1)} %get-tuple-element.70), channel_id=1, source_target_pairs={{0,2},{1,3},{2,0},{3,1},{4,6},{5,7},{6,4},{7,5},{8,10},{9,11},{10,... | collective-permute-start | bytes 98312 | tf_op jit(solution)/shard_map/ppermute | solution.py:83
  147.4 9.1 %collective-permute-start.18 = (bf16[2,8,1024]{2,1,0:T(8,128)(2,1)S(1)}, bf16[2,8,1024]{2,1,0:T(8,128)(2,1)S(1)}, u32[]{:S(2)}, u32[]{:S(2)}) collective-permute-start(bf16[2,8,1024]{2,1,0:T(8,128)(2,1)S(1)} %get-tuple-element.69), channel_id=1, source_target_pairs={{0,3},{1,2},{2,1},{3,0},{4,7},{5,6},{6,5},{7,4},{8,11},{9,10},{10,... | collective-permute-start | bytes 98312 | tf_op jit(solution)/shard_map/ppermute | solution.py:83
  156.6 8.6 %collective-permute-start.19 = (bf16[8,1024]{1,0:T(8,128)(2,1)S(1)}, bf16[8,1024]{1,0:T(8,128)(2,1)S(1)}, u32[]{:S(2)}, u32[]{:S(2)}) collective-permute-start(bf16[8,1024]{1,0:T(8,128)(2,1)S(1)} %dynamic-slice_bitcast_fusion.9), channel_id=1, source_target_pairs={{0,4},{1,5},{2,6},{3,7},{4,0},{5,1},{6,2},{7,3},{8,12},{9,13},{10,... | collective-permute-start | bytes 49160 | tf_op jit(solution)/shard_map/ppermute | solution.py:94
  156.7 17.0 %all-to-all-start.6 = ((bf16[32,8,1024]{2,1,0:T(8,128)(2,1)}), bf16[32,8,1024]{2,1,0:T(8,128)(2,1)S(1)}, u32[]{:S(2)}, u32[]{:S(2)}) async-start(bf16[32,8,1024]{2,1,0:T(8,128)(2,1)} %fusion), calls=%async_computation.6 | async-start | bytes 1048576 | tf_op jit(solution)/shard_map/all_to_all | solution.py:32
  (5 other events, 10.4 us)
